TPU v7x, 32 devices: a whole 2x2x4 slice. The times are simulated.
32 devices in a mesh: stack: 2 (over y), acq: 4 (over z), lines: 4 (over x, core).
Axes of the slice: x: 2, y: 2, z: 4, core: 2. Of those that a mesh axis runs over, the one named last changes fastest.
Arguments:
- returned_radar_signal_data: bfloat16 [8, 2, 512, 4096], P(('stack', 'acq'), None, 'lines'), parts along dimension 0, may hold values from -6 to 6
- slant_replica_filter_response: float32 [8, 2, 4096], P(('stack', 'acq')), parts along dimension 0, may hold values from -6 to 6
- along_track_sharpening_slope: float32 [8, 4096], P(('stack', 'acq'), 'lines'), parts along dimension 0, may hold values from 0.25 to 1
- motion_shift_centroid_hz: float32 [8, 4096], P(('stack', 'acq'), 'lines'), parts along dimension 0, may hold values from -0.2 to 0.2
- valid_along_track_rows: int32 [8], P(('stack', 'acq')), parts along dimension 0, may hold values from 256 to 512, as said below
- reference_index: int32 [2], P('stack'), parts along dimension 0, may hold values from 0 to 3
- patch_offsets: int32 [8, 2, 4, 32], P(('stack', 'acq'), None, None, 'lines'), parts along dimension 0, may hold values from -64 to 64
Outputs:
- correlation: float32 [8, 2, 256, 2048], P(('stack', 'acq'), None, None, 'lines'), parts along dimension 0
There are 2 independent parts, one for each index of `stack`. A program takes and returns all parts, laid end to end along the dimension named above; each array names one. Nothing has to cross between parts.
Inputs may be any that keep to these rules, and one draw needn't show every extreme that they name: `valid_along_track_rows`: some acquisition has all 512 lines valid and some exactly half of them.
All inputs are finite; a program needn't handle non-finite values.
Results may differ from a plain program's by a relative error of at most 0.0053.
Values may be sent and summed in bfloat16 or wider, within the bound.
No kernel may reach another device: no remote copies, remote signals or barrier semaphores. Data moves between devices by JAX's collectives and lax.ppermute only.
A program may use at most 64 MiB of HBM per device.

v0:
```python
import functools
import math

import jax
import jax.numpy as jnp
import ml_dtypes
import numpy as np
from jax import lax
from jax.experimental import pallas as pl
from jax.experimental.pallas import tpu as pltpu
from jax.sharding import PartitionSpec as P

PATCH = 64
LANES = 128
HALF = PATCH // 2
EPS = 1e-06
F32 = jnp.float32
BF16 = jnp.bfloat16
VMEM_BYTES = 56 * 1024 * 1024

SIN_POLY = (3.141582022139052, -5.167142795074894, 2.541899011376644, -0.5546361478584824)
COS_POLY = (0.9999933027022169, -4.9339382503784215, 4.041285686469419, -1.2221312612719153)


def split_np(matrix):
    high = matrix.astype(ml_dtypes.bfloat16)
    low = (matrix - high.astype(np.float64)).astype(ml_dtypes.bfloat16)
    return high, low


def angle_np(rows, cols, period):
    return 2.0 * np.pi * ((np.asarray(rows)[:, None] * np.asarray(cols)[None, :]) % period) / period


def right_matrix(theta, sign, scale=1.0):
    cos, sin = np.cos(theta) * scale, sign * np.sin(theta) * scale
    return split_np(np.block([[cos, sin], [-sin, cos]]))


def left_matrix(theta, sign, scale=1.0):
    cos, sin = np.cos(theta) * scale, sign * np.sin(theta) * scale
    return split_np(np.block([[cos, -sin], [sin, cos]]))


def split(value):
    high = value.astype(BF16)
    low = (value - high.astype(F32)).astype(BF16)
    return high, low


def dot(lhs, rhs):
    return jnp.dot(lhs, rhs, preferred_element_type=F32)


def fft_list(re, im, sign):
    size = len(re)
    if size == 1:
        return re, im
    if size == 2:
        return [re[0] + re[1], re[0] - re[1]], [im[0] + im[1], im[0] - im[1]]
    even_re, even_im = fft_list(re[0::2], im[0::2], sign)
    odd_re, odd_im = fft_list(re[1::2], im[1::2], sign)
    half = size // 2
    out_re, out_im = [None] * size, [None] * size
    root = math.sqrt(0.5)
    for k in range(half):
        a, b = odd_re[k], odd_im[k]
        if k == 0:
            t_re, t_im = a, b
        elif 4 * k == size:
            t_re, t_im = (b, -a) if sign < 0 else (-b, a)
        elif 8 * k == size:
            t_re, t_im = ((a + b) * root, (b - a) * root) if sign < 0 else ((a - b) * root, (a + b) * root)
        elif 8 * k == 3 * size:
            t_re, t_im = ((b - a) * root, (a + b) * -root) if sign < 0 else ((a + b) * -root, (a - b) * root)
        else:
            cos = math.cos(2.0 * math.pi * k / size)
            sin = sign * math.sin(2.0 * math.pi * k / size)
            t_re, t_im = a * cos - b * sin, a * sin + b * cos
        if 4 * k == size:
            if sign < 0:
                out_re[k], out_re[k + half] = even_re[k] + b, even_re[k] - b
                out_im[k], out_im[k + half] = even_im[k] - a, even_im[k] + a
            else:
                out_re[k], out_re[k + half] = even_re[k] - b, even_re[k] + b
                out_im[k], out_im[k + half] = even_im[k] + a, even_im[k] - a
            continue
        out_re[k], out_re[k + half] = even_re[k] + t_re, even_re[k] - t_re
        out_im[k], out_im[k + half] = even_im[k] + t_im, even_im[k] - t_im
    return out_re, out_im


def three_pass(lhs, high, low):
    lhs_high, lhs_low = lhs
    return dot(lhs_high, high) + dot(lhs_low, high) + dot(lhs_high, low)


def range_kernel(info, x_ref, filt_ref, twf_ref, twi_ref, mfh, mfl, mih, mil, *rest, devices, sub):
    outs, (in_scr, out_scr) = rest[: 2 * devices], rest[2 * devices :]
    inner_refs, outer_refs = outs[:devices], outs[devices:]
    rows, length = x_ref.shape[1], x_ref.shape[2]
    count = length // LANES
    per = count // devices
    me, valid = info[0], info[1]
    first = (me * pl.num_programs(0) + pl.program_id(0)) * rows
    lane = lax.broadcasted_iota(jnp.int32, (sub, LANES), 1)
    for block in range(rows // sub):
        span = slice(block * sub, (block + 1) * sub)
        line = first + block * sub + lax.broadcasted_iota(jnp.int32, (sub, LANES), 0)
        keep = line < valid
        re, im = [], []
        for a in range(count):
            at = slice(a * LANES, (a + 1) * LANES)
            re.append(jnp.where(keep, x_ref[0, span, at].astype(F32), 0.0))
            im.append(jnp.where(keep, x_ref[1, span, at].astype(F32), 0.0))
        re, im = fft_list(re, im, -1)
        high, low = [], []
        for c in range(count):
            cos, sin = twf_ref[0, c : c + 1, :], twf_ref[1, c : c + 1, :]
            h_re, l_re = split(re[c] * cos - im[c] * sin)
            h_im, l_im = split(re[c] * sin + im[c] * cos)
            high.append(jnp.concatenate([h_re, h_im], axis=1))
            low.append(jnp.concatenate([l_re, l_im], axis=1))
        spectrum = three_pass((jnp.concatenate(high, 0), jnp.concatenate(low, 0)), mfh[...], mfl[...])
        high, low = [], []
        for c in range(count):
            at = slice(c * sub, (c + 1) * sub)
            a, b = spectrum[at, :LANES], spectrum[at, LANES:]
            cos, sin = filt_ref[0, c : c + 1, :], filt_ref[1, c : c + 1, :]
            h_re, l_re = split(a * cos - b * sin)
            h_im, l_im = split(a * sin + b * cos)
            high.append(jnp.concatenate([h_re, h_im], axis=1))
            low.append(jnp.concatenate([l_re, l_im], axis=1))
        pulse = three_pass((jnp.concatenate(high, 0), jnp.concatenate(low, 0)), mih[...], mil[...])
        re, im = [], []
        for c in range(count):
            at = slice(c * sub, (c + 1) * sub)
            a, b = pulse[at, :LANES], pulse[at, LANES:]
            cos, sin = twi_ref[0, c : c + 1, :], twi_ref[1, c : c + 1, :]
            re.append(a * cos - b * sin)
            im.append(a * sin + b * cos)
        parts = fft_list(re, im, 1)
        zero = jnp.zeros((sub, LANES), F32)
        for part in range(2):
            y = list(parts[part])
            group = [jnp.where(lane < 96, y[a - 1] if a else zero, y[a] if a < count else zero) for a in range(count + 1)]
            group.append(zero)
            for u in range(count // 2):
                in_scr[u, part, span, :] = jnp.where(
                    lane < 64, y[2 * u], pltpu.roll(y[2 * u + 1], 64, 1)
                ).astype(BF16)
            for u in range(count // 2 + 1):
                out_scr[u, part, span, :] = jnp.where(
                    lane < 64, pltpu.roll(group[2 * u], 64, 1), group[2 * u + 1]
                ).astype(BF16)
    for k in range(devices):
        base = (me ^ k) * (per // 2)
        for t in range(per // 2):
            inner_refs[k][:, :, t * LANES : (t + 1) * LANES] = in_scr[base + t]
        for t in range(per // 2 + 1):
            outer_refs[k][:, :, t * LANES : (t + 1) * LANES] = out_scr[base + t]


def compress(echo, filt, me, valid, devices):
    _, rows, length = echo.shape
    count = length // LANES
    per = count // devices
    step = min(32, rows)
    sub = 16
    natural = np.arange(LANES)
    turned = (natural + HALF) % LANES
    twf = -angle_np(np.arange(count), natural, length)
    twi = angle_np(np.arange(count), turned, length)
    twf = jnp.asarray(np.stack([np.cos(twf), np.sin(twf)]), F32)
    twi = jnp.asarray(np.stack([np.cos(twi), np.sin(twi)]), F32)
    mats = right_matrix(angle_np(natural, natural, LANES), -1) + right_matrix(
        angle_np(natural, turned, LANES), 1, 1.0 / length
    )
    widths = [per // 2 * LANES] * devices + [(per // 2 + 1) * LANES] * devices
    whole2 = pl.BlockSpec((2 * LANES, 2 * LANES), lambda i, _: (0, 0))
    whole3 = pl.BlockSpec((2, count, LANES), lambda i, _: (0, 0, 0))
    outs = pl.pallas_call(
        functools.partial(range_kernel, devices=devices, sub=sub),
        grid_spec=pltpu.PrefetchScalarGridSpec(
            num_scalar_prefetch=1,
            grid=(rows // step,),
            in_specs=[pl.BlockSpec((2, step, length), lambda i, _: (0, i, 0)), whole3, whole3, whole3]
            + [whole2] * 4,
            out_specs=[pl.BlockSpec((2, step, w), lambda i, _: (0, i, 0)) for w in widths],
            scratch_shapes=[
                pltpu.VMEM((count // 2, 2, step, LANES), BF16),
                pltpu.VMEM((count // 2 + 1, 2, step, LANES), BF16),
            ],
        ),
        out_shape=[jax.ShapeDtypeStruct((2, rows, w), BF16) for w in widths],
        compiler_params=pltpu.CompilerParams(vmem_limit_bytes=VMEM_BYTES),
        name="range_compress",
    )(
        jnp.stack([me, valid]).astype(jnp.int32),
        echo,
        filt.reshape(2, LANES, count).transpose(0, 2, 1),
        twf,
        twi,
        *[jnp.asarray(m) for m in mats],
    )
    return outs[:devices], outs[devices:]


def turn(turns):
    x = turns - jnp.round(turns)
    z = x * x
    sin = x * (SIN_POLY[0] + z * (SIN_POLY[1] + z * (SIN_POLY[2] + z * SIN_POLY[3])))
    cos = COS_POLY[0] + z * (COS_POLY[1] + z * (COS_POLY[2] + z * COS_POLY[3]))
    return 1.0 - 2.0 * (sin * sin), 2.0 * (sin * cos)


def focus_tile(scr, col, width, slope, centre, af_ref, ai_ref):
    lines = scr.shape[1]
    radix = lines // LANES
    at = slice(col, col + width)
    re = [scr[0, s * LANES : (s + 1) * LANES, at].astype(F32) for s in range(radix)]
    im = [scr[1, s * LANES : (s + 1) * LANES, at].astype(F32) for s in range(radix)]
    re, im = fft_list(re, im, -1)
    d = lax.broadcasted_iota(jnp.int32, (LANES, width), 0)
    back_re, back_im = [], []
    rate = slope * (lines / 8.0)
    for c in range(radix):
        high, low = split(jnp.concatenate([re[c], im[c]], axis=0))
        rhs = jnp.concatenate([high, low, high], axis=0)
        freq = dot(af_ref[c], rhs)
        k = c + radix * d
        u = jnp.where(k >= lines // 2, k - lines, k).astype(F32) * (1.0 / lines)
        w = u - centre
        cos, sin = turn(rate * w * w)
        a, b = freq[:LANES], freq[LANES:]
        high, low = split(jnp.concatenate([a * cos - b * sin, a * sin + b * cos], axis=0))
        rhs = jnp.concatenate([high, low, high], axis=0)
        back = dot(ai_ref[c], rhs)
        back_re.append(back[:LANES])
        back_im.append(back[LANES:])
    return fft_list(back_re, back_im, 1)


def azimuth_matrices(lines):
    radix = lines // LANES
    t = np.arange(LANES)
    forward, inverse = [], []
    for c in range(radix):
        k = c + radix * t
        high, low = left_matrix(angle_np(k, t, lines), -1)
        forward.append(np.concatenate([high, high, low], axis=1))
        high, low = left_matrix(angle_np(t, k, lines), 1, 1.0 / lines)
        inverse.append(np.concatenate([high, high, low], axis=1))
    return jnp.asarray(np.stack(forward)), jnp.asarray(np.stack(inverse))


def gather_lines(info, blocks, scr):
    rows = blocks[0].shape[1]
    for k, block in enumerate(blocks):
        start = pl.multiple_of((info[0] ^ k) * rows, rows)
        scr[:, pl.ds(start, rows), :] = block[...]


def inner_kernel(info, *rest, devices, parts):
    blocks, rest = rest[:devices], rest[devices:]
    slope_ref, centre_ref, af_ref, ai_ref, out_ref = rest[:5]
    p_refs, (scr, p_scr) = rest[5 : 5 + parts], rest[5 + parts :]
    gather_lines(info, blocks, scr)
    width = out_ref.shape[2]
    lane = lax.broadcasted_iota(jnp.int32, (1, LANES), 1)

    def packed(ref):
        tiles = []
        for t in range(width // LANES):
            a = pltpu.roll(ref[:, 2 * t * LANES : (2 * t + 1) * LANES], 96, 1)
            b = pltpu.roll(ref[:, (2 * t + 1) * LANES : (2 * t + 2) * LANES], 32, 1)
            tiles.append(jnp.where(lane < 64, a, b))
        return jnp.concatenate(tiles, axis=1)

    re, im = focus_tile(scr, 0, width, packed(slope_ref), packed(centre_ref), af_ref, ai_ref)
    for part, value in enumerate((re, im)):
        for s in range(len(value)):
            image = value[s].astype(BF16)
            out_ref[part, s * LANES : (s + 1) * LANES, :] = image
            p_scr[part, s * PATCH : (s + 1) * PATCH, :] = image[HALF : HALF + PATCH]
    share = p_scr.shape[1] // parts
    for k in range(parts):
        start = pl.multiple_of((info[1] ^ k) * share, share)
        p_refs[k][...] = p_scr[:, pl.ds(start, share), :]


def focus_inner(blocks, slope, centre, matrices, me, me_acq, parts):
    devices = len(blocks)
    _, rows, cols = blocks[0].shape
    lines = rows * devices
    tile = 2 * LANES if cols % (2 * LANES) == 0 else LANES
    prows = lines // 2
    shape = (lines // LANES, 2 * LANES, 6 * LANES)
    return pl.pallas_call(
        functools.partial(inner_kernel, devices=devices, parts=parts),
        grid_spec=pltpu.PrefetchScalarGridSpec(
            num_scalar_prefetch=1,
            grid=(cols // tile,),
            in_specs=[pl.BlockSpec((2, rows, tile), lambda i, _: (0, 0, i))] * devices
            + [pl.BlockSpec((1, 2 * tile), lambda i, _: (0, i))] * 2
            + [pl.BlockSpec(shape, lambda i, _: (0, 0, 0))] * 2,
            out_specs=[pl.BlockSpec((2, lines, tile), lambda i, _: (0, 0, i))]
            + [pl.BlockSpec((2, prows // parts, tile), lambda i, _: (0, 0, i))] * parts,
            scratch_shapes=[pltpu.VMEM((2, lines, tile), BF16), pltpu.VMEM((2, prows, tile), BF16)],
        ),
        out_shape=[jax.ShapeDtypeStruct((2, lines, cols), BF16)]
        + [jax.ShapeDtypeStruct((2, prows // parts, cols), BF16)] * parts,
        compiler_params=pltpu.CompilerParams(vmem_limit_bytes=VMEM_BYTES),
        name="focus_inner",
    )(jnp.stack([me, me_acq]).astype(jnp.int32), *blocks, slope, centre, *matrices)


def patch_matrices():
    n = np.arange(PATCH)
    theta = angle_np(n, n, PATCH)

    def lanes(sign):
        cos = np.kron(np.eye(2), np.cos(theta))
        sin = sign * np.kron(np.eye(2), np.sin(theta))
        return np.stack(split_np(np.block([[cos, sin], [-sin, cos]])))

    high, low = split_np(np.concatenate([np.cos(theta), np.sin(theta)], axis=0))
    column = np.concatenate([high, high, low], axis=1)
    return jnp.asarray(lanes(-1)), jnp.asarray(lanes(1)), jnp.asarray(column)


def columns(value, column_ref, sign):
    high, low = split(value)
    both = dot(column_ref[...], jnp.concatenate([high, low, high], axis=0))
    c_re, c_im = both[:PATCH, :LANES], both[:PATCH, LANES:]
    s_re, s_im = both[PATCH:, :LANES], both[PATCH:, LANES:]
    if sign < 0:
        return c_re + s_im, c_im - s_re
    return c_re - s_im, c_im + s_re


def power(re, im):
    lane = lax.broadcasted_iota(jnp.int32, (1, LANES), 1)
    total = jnp.sum(re * re + im * im, axis=0, keepdims=True)
    left = jnp.sum(jnp.where(lane < PATCH, total, 0.0), axis=1, keepdims=True)
    right = jnp.sum(jnp.where(lane < PATCH, 0.0, total), axis=1, keepdims=True)
    return jnp.where(lane < PATCH, left, right) * (1.0 / (PATCH * PATCH))


def outer_kernel(info, offsets, *rest, devices):
    blocks, rest = rest[:devices], rest[devices:]
    inner_ref, slope_ref, centre_ref, af_ref, ai_ref, lane_ref, column_ref = rest[:7]
    spec_ref, gain_ref, scr, image, windows = rest[7:]
    gather_lines(info, blocks, scr)
    lines, width = scr.shape[1], scr.shape[2]
    lane = lax.broadcasted_iota(jnp.int32, (1, LANES), 1)
    pairs = width // LANES - 1

    def group(ref, a):
        before = ref[:, a * LANES : (a + 1) * LANES]
        after = ref[:, (a + 1) * LANES : (a + 2) * LANES]
        return jnp.where(lane < 96, pltpu.roll(before, 96, 1), pltpu.roll(after, 96, 1))

    def packed(ref, u):
        left = pltpu.roll(group(ref, 2 * u), 64, 1)
        if u == pairs:
            return jnp.where(lane < 64, left, 0.0)
        return jnp.where(lane < 64, left, group(ref, 2 * u + 1))

    edge = jnp.zeros((HALF, image.shape[2]), F32)
    for part in range(2):
        image[part, :HALF, :] = edge
        image[part, HALF + lines : 2 * HALF + lines, :] = edge
    for u in range(pairs + 1):
        re, im = focus_tile(scr, u * LANES, LANES, packed(slope_ref, u), packed(centre_ref, u), af_ref, ai_ref)
        for part, value in enumerate((re, im)):
            for s in range(len(value)):
                at = slice(HALF + s * LANES, HALF + (s + 1) * LANES)
                fresh = value[s].astype(BF16).astype(F32)
                if u == pairs:
                    image[part, at, 2 * u * LANES : (2 * u + 1) * LANES] = fresh
                    continue
                known = inner_ref[part, s * LANES : (s + 1) * LANES, u * LANES : (u + 1) * LANES].astype(F32)
                image[part, at, 2 * u * LANES : (2 * u + 1) * LANES] = jnp.where(
                    lane < 64, fresh, pltpu.roll(known, 64, 1)
                )
                image[part, at, (2 * u + 1) * LANES : (2 * u + 2) * LANES] = jnp.where(
                    lane < 64, pltpu.roll(fresh, 64, 1), known
                )
    row_blocks = lines // (2 * PATCH)
    wide = lax.broadcasted_iota(jnp.int32, (PATCH + 8, LANES), 1)
    for i in range(row_blocks):
        for u in range(pairs):
            found = [[], []]
            for side in range(2):
                j = 2 * u + side
                start = 2 * PATCH * i + PATCH + offsets[0, i, j]
                shift = PATCH + offsets[1, i, j]
                back = jnp.bitwise_and(2 * LANES - shift + side * PATCH, LANES - 1)
                base = pl.multiple_of(lax.shift_left(lax.shift_right_logical(start, 3), 3), 8)
                up = PATCH + 8 - jnp.bitwise_and(start, 7)
                for part in range(2):
                    left = image[part, pl.ds(base, PATCH + 8), j * LANES : (j + 1) * LANES]
                    right = image[part, pl.ds(base, PATCH + 8), (j + 1) * LANES : (j + 2) * LANES]
                    turned = pltpu.roll(jnp.where(wide >= shift, left, right), back, 1)
                    found[part].append(pltpu.roll(turned, up, 0)[:PATCH])
            re = jnp.where(lane < PATCH, found[0][0], found[0][1])
            im = jnp.where(lane < PATCH, found[1][0], found[1][1])
            at = i * pairs + u
            gain_ref[at] = jnp.broadcast_to(lax.rsqrt(power(re, im) + EPS), gain_ref.shape[1:])
            windows[at * PATCH : (at + 1) * PATCH, :] = jnp.concatenate([re, im], axis=1).astype(BF16)
    mixed = dot(windows[...], lane_ref[0]) + dot(windows[...], lane_ref[1])
    for at in range(row_blocks * pairs):
        re, im = columns(mixed[at * PATCH : (at + 1) * PATCH], column_ref, -1)
        spec_ref[0, at] = re
        spec_ref[1, at] = im


def focus_outer(blocks, inner, slope, centre, matrices, patch, me, offsets):
    devices = len(blocks)
    _, rows, cols = blocks[0].shape
    lines = rows * devices
    pairs = cols // LANES - 1
    groups = lines // (2 * PATCH) * pairs
    vmem = pl.BlockSpec(memory_space=pltpu.VMEM)
    smem = pl.BlockSpec(memory_space=pltpu.SMEM)
    return pl.pallas_call(
        functools.partial(outer_kernel, devices=devices),
        in_specs=[smem, smem] + [vmem] * (devices + 7),
        out_specs=[vmem, vmem],
        out_shape=[
            jax.ShapeDtypeStruct((2, groups, PATCH, LANES), F32),
            jax.ShapeDtypeStruct((groups, 8, LANES), F32),
        ],
        scratch_shapes=[
            pltpu.VMEM((2, lines, cols), BF16),
            pltpu.VMEM((2, lines + 2 * HALF + 8, (2 * pairs + 1) * LANES), F32),
            pltpu.VMEM((groups * PATCH, 2 * LANES), BF16),
        ],
        compiler_params=pltpu.CompilerParams(vmem_limit_bytes=VMEM_BYTES),
        name="focus_outer",
    )(me.reshape(1).astype(jnp.int32), offsets, *blocks, inner, slope, centre, *matrices, patch[0], patch[2])


def correlate_kernel(info, *rest, parts):
    shares, rest = rest[:parts], rest[parts:]
    spec_ref, gain_ref, forward_ref, inverse_ref, column_ref, out_ref, p_scr = rest
    share = shares[0].shape[1]
    for k in range(parts):
        start = pl.multiple_of((info[0] ^ k) * share, share)
        p_scr[:, pl.ds(start, share), :] = shares[k][...]
    prows, cols = p_scr.shape[1], p_scr.shape[2]
    pairs = cols // LANES
    groups = prows // PATCH * pairs
    first = []
    for at in range(groups):
        i, u = divmod(at, pairs)
        rows, lanes = slice(i * PATCH, (i + 1) * PATCH), slice(u * LANES, (u + 1) * LANES)
        first.append(jnp.concatenate([p_scr[0, rows, lanes], p_scr[1, rows, lanes]], axis=1))
    stack = jnp.concatenate(first, axis=0)
    mixed = dot(stack, forward_ref[0]) + dot(stack, forward_ref[1])
    middle, gains = [], []
    for at in range(groups):
        i, u = divmod(at, pairs)
        p = first[at].astype(F32)
        gain = lax.rsqrt(power(p[:, :LANES], p[:, LANES:]) + EPS) * gain_ref[at][:1]
        gains.append(gain * (1.0 / PATCH**3))
        p_re, p_im = columns(mixed[at * PATCH : (at + 1) * PATCH], column_ref, -1)
        s_re, s_im = spec_ref[0, at], spec_ref[1, at]
        cross = jnp.concatenate([p_re * s_re + p_im * s_im, p_im * s_re - p_re * s_im], axis=1)
        re, im = columns(cross, column_ref, 1)
        middle.append(jnp.concatenate([re, im], axis=1))
    surface = three_pass(split(jnp.concatenate(middle, axis=0)), inverse_ref[0], inverse_ref[1])
    for at in range(groups):
        i, u = divmod(at, pairs)
        block = surface[at * PATCH : (at + 1) * PATCH]
        rows, lanes = slice(i * PATCH, (i + 1) * PATCH), slice(u * LANES, (u + 1) * LANES)
        out_ref[0, 0, rows, lanes] = block[:, :LANES] * gains[at]
        out_ref[0, 1, rows, lanes] = block[:, LANES:] * gains[at]


def correlate(shares, spectrum, gain, patch, me_acq):
    parts = len(shares)
    _, share, cols = shares[0].shape
    vmem = pl.BlockSpec(memory_space=pltpu.VMEM)
    return pl.pallas_call(
        functools.partial(correlate_kernel, parts=parts),
        in_specs=[pl.BlockSpec(memory_space=pltpu.SMEM)] + [vmem] * (parts + 5),
        out_specs=vmem,
        out_shape=jax.ShapeDtypeStruct((1, 2, share * parts, cols), F32),
        scratch_shapes=[pltpu.VMEM((2, share * parts, cols), BF16)],
        compiler_params=pltpu.CompilerParams(vmem_limit_bytes=VMEM_BYTES),
        name="correlate",
    )(me_acq.reshape(1).astype(jnp.int32), *shares, spectrum, gain, *patch)


def trade(blocks, axis):
    devices = len(blocks)
    return [blocks[0]] + [
        lax.ppermute(blocks[k], axis, [(i, i ^ k) for i in range(devices)]) for k in range(1, devices)
    ]


def with_edges(array, axis):
    devices = lax.axis_size(axis)
    up = [(i, i + 1) for i in range(devices - 1)]
    down = [(i + 1, i) for i in range(devices - 1)]
    before = lax.ppermute(array[:, -LANES:], axis, up)
    after = lax.ppermute(array[:, :LANES], axis, down)
    return jnp.concatenate([before, array, after], axis=1)


def on_device(echo, filt, slope, centre, valid, reference, offsets):
    devices, parts = lax.axis_size("lines"), lax.axis_size("acq")
    me, me_acq = lax.axis_index("lines"), lax.axis_index("acq")
    lines = echo.shape[2] * devices
    matrices = azimuth_matrices(lines)
    patch = patch_matrices()
    inner, outer = compress(echo[0], filt[0], me, valid[0], devices)
    inner = trade(inner, "lines")
    outer = trade(outer, "lines")
    image, *shares = focus_inner(inner, slope, centre, matrices, me, me_acq, parts)
    shares = trade(shares, "acq")
    edged = with_edges(jnp.concatenate([slope, centre], axis=0), "lines")
    spectrum, gain = focus_outer(
        outer, image, edged[:1], edged[1:], matrices, patch, me, offsets[0]
    )
    source = me_acq ^ reference[0]
    mine = shares[0]
    for k in range(1, parts):
        mine = jnp.where(source == k, shares[k], mine)
    shares = trade([mine] * parts, "acq")
    return correlate(shares, spectrum, gain, patch, me_acq)


def solution(mesh):
    return jax.shard_map(
        on_device,
        mesh=mesh,
        in_specs=(
            P(("stack", "acq"), None, "lines", None),
            P(("stack", "acq"), None, None),
            P(("stack", "acq"), "lines"),
            P(("stack", "acq"), "lines"),
            P(("stack", "acq")),
            P("stack"),
            P(("stack", "acq"), None, None, "lines"),
        ),
        out_specs=P(("stack", "acq"), None, None, "lines"),
        check_vma=False,
    )
```

profile of v0, /device:TPU:0, one launch (start us, length us, event | category | flops | bytes accessed | tf_op | source)
XLA Modules:
  0.0 79.3 jit_solution(216770692207497692)
XLA Ops:
  0.7 0.9 %reshape_squeeze.3 = f32[2,128,32]{2,1,0:T(8,128)S(1)} reshape(f32[1,2,4096]{2,1,0:T(2,128)} %param.19) | data formatting | bytes 65536 | tf_op jit(solution)/shard_map/reshape;squeeze | solution.py:201
  1.6 0.7 copy.19
  2.2 0.6 pad_add_fusion.1.info
  2.9 11.5 %range_compress.1 = (bf16[2,128,512]{2,1,0:T(8,128)(2,1)}, bf16[2,128,512]{2,1,0:T(8,128)(2,1)}, bf16[2,128,512]{2,1,0:T(8,128)(2,1)}, bf16[2,128,512]{2,1,0:T(8...) custom-call(s32[2]{0:T(128)} %pad_add_fusion.1.info, ...), custom_call_target="tpu_custom_call" | custom-call | tf_op jit(solution)/shard_map/range_compress/pallas_call | solution.py:182
  14.4 0.5 collective-permute-start
  14.9 2.6 %collective-permute-start.1 = (bf16[2,128,512]{2,1,0:T(8,128)(2,1)}, bf16[2,128,512]{2,1,0:T(8,128)(2,1)S(1)}, u32[]{:S(2)}, u32[]{:S(2)}) collective-permute-start(bf16[2,128,512]{2,1,0:T(8,128)(2,1)} %get-tuple-element.22), channel_id=1, source_target_pairs={{0,2},{1,3},{2,0},{3,1},{4,6},{5,7},{6,4},{7,5},{8,10},{9,11},{10,... | collective-permute-start | bytes 786440 | tf_op jit(solution)/shard_map/ppermute | solution.py:500
  17.4 0.1 collective-permute-start.2
  17.5 0.0 copy-done.10
  17.5 0.0 copy-done.12
  17.5 2.0 %collective-permute-start.12 = (f32[2,128]{1,0:T(2,128)S(1)}, f32[2,128]{1,0:T(2,128)S(1)}, u32[]{:S(2)}, u32[]{:S(2)}) collective-permute-start(f32[2,128]{1,0:T(2,128)S(1)} %get-tuple-element.37), channel_id=1, source_target_pairs={{0,1},{1,2},{2,3},{4,5},{5,6},{6,7},{8,9},{9,10},{10,11},{12,13},{... | collective-permute-start | bytes 3080 | tf_op jit(solution)/shard_map/ppermute | solution.py:508
  19.6 1.3 %collective-permute-start.13 = (f32[2,128]{1,0:T(2,128)S(1)}, f32[2,128]{1,0:T(2,128)S(1)}, u32[]{:S(2)}, u32[]{:S(2)}) collective-permute-start(f32[2,128]{1,0:T(2,128)S(1)} %get-tuple-element.38), channel_id=1, source_target_pairs={{1,0},{2,1},{3,2},{5,4},{6,5},{7,6},{9,8},{10,9},{11,10},{13,12},{... | collective-permute-start | bytes 3080 | tf_op jit(solution)/shard_map/ppermute | solution.py:509
  21.5 0.7 pad_add_fusion.info
  22.2 0.0 collective-permute-done.rest_1_
  22.2 4.0 %collective-permute-start.10 = (bf16[2,128,640]{2,1,0:T(8,128)(2,1)}, bf16[2,128,640]{2,1,0:T(8,128)(2,1)S(1)}, u32[]{:S(2)}, u32[]{:S(2)}) collective-permute-start(bf16[2,128,640]{2,1,0:T(8,128)(2,1)} %get-tuple-element.30), channel_id=1, source_target_pairs={{0,2},{1,3},{2,0},{3,1},{4,6},{5,7},{6,4},{7,5},{8,10},{9,11},{10,... | collective-permute-start | bytes 983048 | tf_op jit(solution)/shard_map/ppermute | solution.py:500
  26.1 0.0 collective-permute-done.1.rest_2_
  26.2 0.0 collective-permute-start.11
  26.2 3.8 %collective-permute-done.2.rest_3_ = bf16[2,128,512]{2,1,0:T(8,128)(2,1)S(1)} collective-permute-done((bf16[2,128,512]{2,1,0:T(8,128)(2,1)}, bf16[2,128,512]{2,1,0:T(8,128)(2,1)S(1)}, u32[]{:S(2)}, u32[]{:S(2)}) %collective-permute-start.2) | collective-permute-done | bytes 262176 | tf_op jit(solution)/shard_map/ppermute | solution.py:500
  30.0 0.0 copy-done.4
  30.0 0.7 copy-done.6
  30.7 7.2 %focus_inner.1 = (bf16[2,512,512]{2,1,0:T(8,128)(2,1)}, bf16[2,64,512]{2,1,0:T(8,128)(2,1)}, bf16[2,64,512]{2,1,0:T(8,128)(2,1)}, bf16[2,64,512]{2,1,0:T(8,128)(2,1)}, bf16[2,64,512]{2,1,0:T(8,128)(2,1)}) custom-call(s32[2]{0:T(128)} %pad_add_fusion.info, bf16[2,128,512]{2,1,0:T(8,128)(2,1)} %get-tuple-element.20.rest_0_, bf16[2,128,512]{2,1,0:T(8,128)(2,1)} %copy-done.4, ...), custom_call_target="tpu_custom_call" | custom-call | tf_op jit(solution)/shard_map/focus_inner/pallas_call | solution.py:299
  37.9 3.7 %collective-permute-start.3 = (bf16[2,64,512]{2,1,0:T(8,128)(2,1)}, bf16[2,64,512]{2,1,0:T(8,128)(2,1)S(1)}, u32[]{:S(2)}, u32[]{:S(2)}) collective-permute-start(bf16[2,64,512]{2,1,0:T(8,128)(2,1)} %get-tuple-element.24), channel_id=1, source_target_pairs={{0,12},{4,8},{8,4},{12,0},{1,13},{5,9},{9,5},{13,1},{2,14},{6,10},... | collective-permute-start | bytes 393224 | tf_op jit(solution)/shard_map/ppermute | solution.py:500
  41.6 0.0 collective-permute-done.12
  41.6 0.0 collective-permute-start.4
  41.6 0.0 collective-permute-done.13
  41.6 0.8 collective-permute-start.5
  42.4 4.1 %collective-permute-done.3 = bf16[2,64,512]{2,1,0:T(8,128)(2,1)S(1)} collective-permute-done((bf16[2,64,512]{2,1,0:T(8,128)(2,1)}, bf16[2,64,512]{2,1,0:T(8,128)(2,1)S(1)}, u32[]{:S(2)}, u32[]{:S(2)}) %collective-permute-start.3) | collective-permute-done | bytes 131104 | tf_op jit(solution)/shard_map/ppermute | solution.py:500
  46.5 0.0 collective-permute-start.9
  46.5 7.3 %collective-permute-done.4 = bf16[2,64,512]{2,1,0:T(8,128)(2,1)S(1)} collective-permute-done((bf16[2,64,512]{2,1,0:T(8,128)(2,1)}, bf16[2,64,512]{2,1,0:T(8,128)(2,1)S(1)}, u32[]{:S(2)}, u32[]{:S(2)}) %collective-permute-start.4) | collective-permute-done | bytes 131104 | tf_op jit(solution)/shard_map/ppermute | solution.py:500
  53.7 0.0 collective-permute-done.5
  53.8 0.8 %collective-permute-start.6 = (bf16[2,64,512]{2,1,0:T(8,128)(2,1)S(1)}, bf16[2,64,512]{2,1,0:T(8,128)(2,1)S(1)}, u32[]{:S(2)}, u32[]{:S(2)}) collective-permute-start(bf16[2,64,512]{2,1,0:T(8,128)(2,1)S(1)} %select_select_fusion.rest_0_), channel_id=1, source_target_pairs={{0,4},{4,0},{8,12},{12,8},{1,5},{5,1},{9,13},{13,9},{2,6},{6,2},{1... | collective-permute-start | bytes 393224 | tf_op jit(solution)/shard_map/ppermute | solution.py:500
  54.6 3.2 %collective-permute-start.7 = (bf16[2,64,512]{2,1,0:T(8,128)(2,1)S(1)}, bf16[2,64,512]{2,1,0:T(8,128)(2,1)S(1)}, u32[]{:S(2)}, u32[]{:S(2)}) collective-permute-start(bf16[2,64,512]{2,1,0:T(8,128)(2,1)S(1)} %select_select_fusion.rest_0_), channel_id=1, source_target_pairs={{0,8},{4,12},{8,0},{12,4},{1,9},{5,13},{9,1},{13,5},{2,10},{6,14},... | collective-permute-start | bytes 393224 | tf_op jit(solution)/shard_map/ppermute | solution.py:500
  57.8 0.0 collective-permute-done.10.rest_2_
  57.8 0.4 collective-permute-start.8
  58.2 0.6 fusion
  58.8 0.0 collective-permute-done.11.rest_3_
  58.9 0.0 collective-permute-done.9.rest_1_
  58.9 0.7 copy-done.2
  59.6 0.1 copy-done.3
  59.7 13.2 %focus_outer.1 = (f32[2,16,64,128]{3,2,1,0:T(8,128)}, f32[16,8,128]{2,1,0:T(8,128)}) custom-call(s32[1]{0:T(128)} %bitcast.2.info, s32[2,4,8]{2,1,0:T(4,128)} %bitcast.9, bf16[2,128,640]{2,1,0:T(8,128)(2,1)} %get-tuple-element.28.rest_0_, bf16[2,128,640]{2,1,0:T(8,128)(2,1)} %copy-done.3, bf16[2,128,640]{2,1,0:T(8,128)(2,1)} %copy-done.1, ...), custom_call_target="tpu_custom_call" | custom-call | tf_op jit(solution)/shard_map/focus_outer/pallas_call | solution.py:427
  72.9 0.0 copy-done
  72.9 0.0 collective-permute-done.6.rest_1_
  72.9 0.0 collective-permute-done.7.rest_2_
  72.9 0.0 collective-permute-done.8.rest_3_
  72.9 0.0 copy-start.9
  73.0 0.6 copy-done.7
  73.5 0.1 copy-done.8
  73.6 0.0 copy-done.9
  73.6 5.6 %correlate.1 = f32[1,2,256,512]{3,2,1,0:T(8,128)} custom-call(s32[1]{0:T(128)} %bitcast.info, bf16[2,64,512]{2,1,0:T(8,128)(2,1)} %copy-done, bf16[2,64,512]{2,1,0:T(8,128)(2,1)} %copy-done.7, bf16[2,64,512]{2,1,0:T(8,128)(2,1)} %copy-done.8, bf16[2,64,512]{2,1,0:T(8,128)(2,1)} %copy-done.9, f32[2,16,64,128]{3,2,1,0:T(8,128)} %get-tuple-element.33.rest_4_, ...), custom_call_target="tpu_custom_call" | custom-call | tf_op jit(solution)/shard_map/correlate/pallas_call | solution.py:486
  (22 shorter events, 0.1 us)
Async XLA Ops:
  0.0 17.5 %copy-start.10 = (f32[1,1024]{1,0:T(1,128)S(1)}, f32[1,1024]{1,0:T(1,128)}, u32[]{:S(2)}) copy-start(f32[1,1024]{1,0:T(1,128)} %rest_4_.1) | copy-start | bytes 12292
  0.0 17.5 %copy-start.12 = (f32[1,1024]{1,0:T(1,128)S(1)}, f32[1,1024]{1,0:T(1,128)}, u32[]{:S(2)}) copy-start(f32[1,1024]{1,0:T(1,128)} %rest_5_.1) | copy-start | bytes 12292
  14.4 7.8 %collective-permute-start = (bf16[2,128,512]{2,1,0:T(8,128)(2,1)}, bf16[2,128,512]{2,1,0:T(8,128)(2,1)S(1)}, u32[]{:S(2)}, u32[]{:S(2)}) collective-permute-start(bf16[2,128,512]{2,1,0:T(8,128)(2,1)} %get-tuple-element.21), channel_id=1, source_target_pairs={{0,1},{1,0},{2,3},{3,2},{4,5},{5,4},{6,7},{7,6},{8,9},{9,8},{10,11... | collective-permute-start | bytes 786440 | tf_op jit(solution)/shard_map/ppermute | solution.py:500
  14.9 11.3 %collective-permute-start.1 = (bf16[2,128,512]{2,1,0:T(8,128)(2,1)}, bf16[2,128,512]{2,1,0:T(8,128)(2,1)S(1)}, u32[]{:S(2)}, u32[]{:S(2)}) collective-permute-start(bf16[2,128,512]{2,1,0:T(8,128)(2,1)} %get-tuple-element.22), channel_id=1, source_target_pairs={{0,2},{1,3},{2,0},{3,1},{4,6},{5,7},{6,4},{7,5},{8,10},{9,11},{10,... | collective-permute-start | bytes 786440 | tf_op jit(solution)/shard_map/ppermute | solution.py:500
  17.4 12.6 %collective-permute-start.2 = (bf16[2,128,512]{2,1,0:T(8,128)(2,1)}, bf16[2,128,512]{2,1,0:T(8,128)(2,1)S(1)}, u32[]{:S(2)}, u32[]{:S(2)}) collective-permute-start(bf16[2,128,512]{2,1,0:T(8,128)(2,1)} %get-tuple-element.23), channel_id=1, source_target_pairs={{0,3},{1,2},{2,1},{3,0},{4,7},{5,6},{6,5},{7,4},{8,11},{9,10},{10,... | collective-permute-start | bytes 786440 | tf_op jit(solution)/shard_map/ppermute | solution.py:500
  17.5 24.1 %collective-permute-start.12 = (f32[2,128]{1,0:T(2,128)S(1)}, f32[2,128]{1,0:T(2,128)S(1)}, u32[]{:S(2)}, u32[]{:S(2)}) collective-permute-start(f32[2,128]{1,0:T(2,128)S(1)} %get-tuple-element.37), channel_id=1, source_target_pairs={{0,1},{1,2},{2,3},{4,5},{5,6},{6,7},{8,9},{9,10},{10,11},{12,13},{... | collective-permute-start | bytes 3080 | tf_op jit(solution)/shard_map/ppermute | solution.py:508
  19.6 22.0 %collective-permute-start.13 = (f32[2,128]{1,0:T(2,128)S(1)}, f32[2,128]{1,0:T(2,128)S(1)}, u32[]{:S(2)}, u32[]{:S(2)}) collective-permute-start(f32[2,128]{1,0:T(2,128)S(1)} %get-tuple-element.38), channel_id=1, source_target_pairs={{1,0},{2,1},{3,2},{5,4},{6,5},{7,6},{9,8},{10,9},{11,10},{13,12},{... | collective-permute-start | bytes 3080 | tf_op jit(solution)/shard_map/ppermute | solution.py:509
  22.2 7.8 %copy-start.4 = (bf16[2,128,512]{2,1,0:T(8,128)(2,1)}, bf16[2,128,512]{2,1,0:T(8,128)(2,1)S(1)}, u32[]{:S(2)}) copy-start(bf16[2,128,512]{2,1,0:T(8,128)(2,1)S(1)} %collective-permute-done.rest_1_) | copy-start | bytes 786436
  22.2 35.6 %collective-permute-start.10 = (bf16[2,128,640]{2,1,0:T(8,128)(2,1)}, bf16[2,128,640]{2,1,0:T(8,128)(2,1)S(1)}, u32[]{:S(2)}, u32[]{:S(2)}) collective-permute-start(bf16[2,128,640]{2,1,0:T(8,128)(2,1)} %get-tuple-element.30), channel_id=1, source_target_pairs={{0,2},{1,3},{2,0},{3,1},{4,6},{5,7},{6,4},{7,5},{8,10},{9,11},{10,... | collective-permute-start | bytes 983048 | tf_op jit(solution)/shard_map/ppermute | solution.py:500
  26.2 3.8 %copy-start.5 = (bf16[2,128,512]{2,1,0:T(8,128)(2,1)}, bf16[2,128,512]{2,1,0:T(8,128)(2,1)S(1)}, u32[]{:S(2)}) copy-start(bf16[2,128,512]{2,1,0:T(8,128)(2,1)S(1)} %collective-permute-done.1.rest_2_) | copy-start | bytes 786436
  26.2 32.7 %collective-permute-start.11 = (bf16[2,128,640]{2,1,0:T(8,128)(2,1)}, bf16[2,128,640]{2,1,0:T(8,128)(2,1)S(1)}, u32[]{:S(2)}, u32[]{:S(2)}) collective-permute-start(bf16[2,128,640]{2,1,0:T(8,128)(2,1)} %get-tuple-element.31), channel_id=1, source_target_pairs={{0,3},{1,2},{2,1},{3,0},{4,7},{5,6},{6,5},{7,4},{8,11},{9,10},{10,... | collective-permute-start | bytes 983048 | tf_op jit(solution)/shard_map/ppermute | solution.py:500
  30.0 0.7 copy-start.6
  30.7 11.6 %copy-start.11 = (f32[1,1024]{1,0:T(1,128)S(1)}, f32[1,1024]{1,0:T(1,128)}, u32[]{:S(2)}) copy-start(f32[1,1024]{1,0:T(1,128)} %rest_4_.1) | copy-start | bytes 12292
  30.7 11.6 %copy-start.13 = (f32[1,1024]{1,0:T(1,128)S(1)}, f32[1,1024]{1,0:T(1,128)}, u32[]{:S(2)}) copy-start(f32[1,1024]{1,0:T(1,128)} %rest_5_.1) | copy-start | bytes 12292
  30.7 15.7 %copy-start.14 = (bf16[2,128,640]{2,1,0:T(8,128)(2,1)S(1)}, bf16[2,128,640]{2,1,0:T(8,128)(2,1)}, u32[]{:S(2)}) copy-start(bf16[2,128,640]{2,1,0:T(8,128)(2,1)} %get-tuple-element.29) | copy-start | bytes 983044
  37.9 8.5 %collective-permute-start.3 = (bf16[2,64,512]{2,1,0:T(8,128)(2,1)}, bf16[2,64,512]{2,1,0:T(8,128)(2,1)S(1)}, u32[]{:S(2)}, u32[]{:S(2)}) collective-permute-start(bf16[2,64,512]{2,1,0:T(8,128)(2,1)} %get-tuple-element.24), channel_id=1, source_target_pairs={{0,12},{4,8},{8,4},{12,0},{1,13},{5,9},{9,5},{13,1},{2,14},{6,10},... | collective-permute-start | bytes 393224 | tf_op jit(solution)/shard_map/ppermute | solution.py:500
  41.6 12.2 %collective-permute-start.4 = (bf16[2,64,512]{2,1,0:T(8,128)(2,1)}, bf16[2,64,512]{2,1,0:T(8,128)(2,1)S(1)}, u32[]{:S(2)}, u32[]{:S(2)}) collective-permute-start(bf16[2,64,512]{2,1,0:T(8,128)(2,1)} %get-tuple-element.25), channel_id=1, source_target_pairs={{0,8},{4,12},{8,0},{12,4},{1,9},{5,13},{9,1},{13,5},{2,10},{6,14},... | collective-permute-start | bytes 393224 | tf_op jit(solution)/shard_map/ppermute | solution.py:500
  41.6 12.1 %collective-permute-start.5 = (bf16[2,64,512]{2,1,0:T(8,128)(2,1)}, bf16[2,64,512]{2,1,0:T(8,128)(2,1)S(1)}, u32[]{:S(2)}, u32[]{:S(2)}) collective-permute-start(bf16[2,64,512]{2,1,0:T(8,128)(2,1)} %get-tuple-element.26), channel_id=1, source_target_pairs={{0,4},{4,0},{8,12},{12,8},{1,5},{5,1},{9,13},{13,9},{2,6},{6,2},{1... | collective-permute-start | bytes 393224 | tf_op jit(solution)/shard_map/ppermute | solution.py:500
  46.5 12.4 %collective-permute-start.9 = (bf16[2,128,640]{2,1,0:T(8,128)(2,1)S(1)}, bf16[2,128,640]{2,1,0:T(8,128)(2,1)S(1)}, u32[]{:S(2)}, u32[]{:S(2)}) collective-permute-start(bf16[2,128,640]{2,1,0:T(8,128)(2,1)S(1)} %copy-done.14), channel_id=1, source_target_pairs={{0,1},{1,0},{2,3},{3,2},{4,5},{5,4},{6,7},{7,6},{8,9},{9,8},{10,11... | collective-permute-start | bytes 983048 | tf_op jit(solution)/shard_map/ppermute | solution.py:500
  53.8 19.1 %copy-start = (bf16[2,64,512]{2,1,0:T(8,128)(2,1)}, bf16[2,64,512]{2,1,0:T(8,128)(2,1)S(1)}, u32[]{:S(2)}) copy-start(bf16[2,64,512]{2,1,0:T(8,128)(2,1)S(1)} %select_select_fusion.rest_0_) | copy-start | bytes 393220
  53.8 19.1 %collective-permute-start.6 = (bf16[2,64,512]{2,1,0:T(8,128)(2,1)S(1)}, bf16[2,64,512]{2,1,0:T(8,128)(2,1)S(1)}, u32[]{:S(2)}, u32[]{:S(2)}) collective-permute-start(bf16[2,64,512]{2,1,0:T(8,128)(2,1)S(1)} %select_select_fusion.rest_0_), channel_id=1, source_target_pairs={{0,4},{4,0},{8,12},{12,8},{1,5},{5,1},{9,13},{13,9},{2,6},{6,2},{1... | collective-permute-start | bytes 393224 | tf_op jit(solution)/shard_map/ppermute | solution.py:500
  54.6 18.3 %collective-permute-start.7 = (bf16[2,64,512]{2,1,0:T(8,128)(2,1)S(1)}, bf16[2,64,512]{2,1,0:T(8,128)(2,1)S(1)}, u32[]{:S(2)}, u32[]{:S(2)}) collective-permute-start(bf16[2,64,512]{2,1,0:T(8,128)(2,1)S(1)} %select_select_fusion.rest_0_), channel_id=1, source_target_pairs={{0,8},{4,12},{8,0},{12,4},{1,9},{5,13},{9,1},{13,5},{2,10},{6,14},... | collective-permute-start | bytes 393224 | tf_op jit(solution)/shard_map/ppermute | solution.py:500
  57.8 1.1 %copy-start.1 = (bf16[2,128,640]{2,1,0:T(8,128)(2,1)}, bf16[2,128,640]{2,1,0:T(8,128)(2,1)S(1)}, u32[]{:S(2)}) copy-start(bf16[2,128,640]{2,1,0:T(8,128)(2,1)S(1)} %collective-permute-done.10.rest_2_) | copy-start | bytes 983044
  57.8 15.1 %collective-permute-start.8 = (bf16[2,64,512]{2,1,0:T(8,128)(2,1)S(1)}, bf16[2,64,512]{2,1,0:T(8,128)(2,1)S(1)}, u32[]{:S(2)}, u32[]{:S(2)}) collective-permute-start(bf16[2,64,512]{2,1,0:T(8,128)(2,1)S(1)} %select_select_fusion.rest_0_), channel_id=1, source_target_pairs={{0,12},{4,8},{8,4},{12,0},{1,13},{5,9},{9,5},{13,1},{2,14},{6,10},... | collective-permute-start | bytes 393224 | tf_op jit(solution)/shard_map/ppermute | solution.py:500
  58.9 0.7 copy-start.2
  58.9 0.8 %copy-start.3 = (bf16[2,128,640]{2,1,0:T(8,128)(2,1)}, bf16[2,128,640]{2,1,0:T(8,128)(2,1)S(1)}, u32[]{:S(2)}) copy-start(bf16[2,128,640]{2,1,0:T(8,128)(2,1)S(1)} %collective-permute-done.9.rest_1_) | copy-start | bytes 983044
  72.9 0.6 copy-start.7
  72.9 0.7 copy-start.8
  72.9 0.7 copy-start.9
where the time goes:
time: 80.1 us; the launch traced here: 79.3 us
  Pallas kernels  37.5 us (47%)
  starting transfers between devices  19.3 us (24%)
  waiting for transfers between devices  15.2 us (19%)
  local copies, waits for them, and re-layouts  4.41 us (6%)
  between operations  1.47 us (2%)
  other arithmetic  1.34 us (2%)
    ppermute x12, starting transfers between devices, trade(): lax.ppermute(blocks[k], axis, [(i, i ^ k) for i in range(devices)])  16 us
    ppermute x12, waiting for transfers between devices, trade(): lax.ppermute(blocks[k], axis, [(i, i ^ k) for i in range(devices)])  15.2 us
    pallas_call x1, Pallas kernels, focus_outer(): pl.pallas_call(functools.partial(outer_kernel, devices=devices), in_specs...  13.2 us
    pallas_call x1, Pallas kernels, compress(): pl.pallas_call(functools.partial(range_kernel, devices=devices, sub=sub),...  11.5 us
    pallas_call x1, Pallas kernels, focus_inner(): pl.pallas_call(functools.partial(inner_kernel, devices=devices, parts=par...  7.17 us
    pallas_call x1, Pallas kernels, correlate(): pl.pallas_call(functools.partial(correlate_kernel, parts=parts), in_specs...  5.65 us
    unnamed x30, local copies, waits for them, and re-layouts  2.27 us
    ppermute x1, starting transfers between devices, with_edges(): before = lax.ppermute(array[:, -LANES:], axis, up)  2.04 us
  transfers between devices with their start and end apart: 14, of which 3 were waited for; matrix products, arithmetic and copies ran while one was open for 2% of the time, Pallas kernels for 26%

commit v1 on v0

v1 whole, which is shorter than its diff:
```python
import functools
import math

import jax
import jax.numpy as jnp
import ml_dtypes
import numpy as np
from jax import lax
from jax.experimental import pallas as pl
from jax.experimental.pallas import tpu as pltpu
from jax.sharding import PartitionSpec as P

PATCH = 64
LANES = 128
HALF = PATCH // 2
EPS = 1e-06
F32 = jnp.float32
BF16 = jnp.bfloat16
VMEM_BYTES = 32 * 1024 * 1024
RANGE_BYTES = 60 * 1024 * 1024

ROW_PARTS = 1
COLUMN_PARTS = 2

SIN_POLY = (3.141582022139052, -5.167142795074894, 2.541899011376644, -0.5546361478584824)
COS_POLY = (0.9999933027022169, -4.9339382503784215, 4.041285686469419, -1.2221312612719153)


def split_np(matrix):
    high = matrix.astype(ml_dtypes.bfloat16)
    low = (matrix - high.astype(np.float64)).astype(ml_dtypes.bfloat16)
    return high, low


def angle_np(rows, cols, period):
    return 2.0 * np.pi * ((np.asarray(rows)[:, None] * np.asarray(cols)[None, :]) % period) / period


def right_matrix(theta, sign, scale=1.0):
    cos, sin = np.cos(theta) * scale, sign * np.sin(theta) * scale
    return split_np(np.block([[cos, sin], [-sin, cos]]))


def left_matrix(theta, sign, scale=1.0):
    cos, sin = np.cos(theta) * scale, sign * np.sin(theta) * scale
    return split_np(np.block([[cos, -sin], [sin, cos]]))


def cost(microseconds):
    return pl.CostEstimate(
        flops=int(microseconds * 1e9), bytes_accessed=int(microseconds * 3.5e6), transcendentals=0
    )


def split(value):
    high = value.astype(BF16)
    low = (value - high.astype(F32)).astype(BF16)
    return high, low


def dot(lhs, rhs):
    return jnp.dot(lhs, rhs, preferred_element_type=F32)


def fft_list(re, im, sign):
    size = len(re)
    if size == 1:
        return re, im
    if size == 2:
        return [re[0] + re[1], re[0] - re[1]], [im[0] + im[1], im[0] - im[1]]
    even_re, even_im = fft_list(re[0::2], im[0::2], sign)
    odd_re, odd_im = fft_list(re[1::2], im[1::2], sign)
    half = size // 2
    out_re, out_im = [None] * size, [None] * size
    root = math.sqrt(0.5)
    for k in range(half):
        a, b = odd_re[k], odd_im[k]
        if k == 0:
            t_re, t_im = a, b
        elif 4 * k == size:
            t_re, t_im = (b, -a) if sign < 0 else (-b, a)
        elif 8 * k == size:
            t_re, t_im = ((a + b) * root, (b - a) * root) if sign < 0 else ((a - b) * root, (a + b) * root)
        elif 8 * k == 3 * size:
            t_re, t_im = ((b - a) * root, (a + b) * -root) if sign < 0 else ((a + b) * -root, (a - b) * root)
        else:
            cos = math.cos(2.0 * math.pi * k / size)
            sin = sign * math.sin(2.0 * math.pi * k / size)
            t_re, t_im = a * cos - b * sin, a * sin + b * cos
        if 4 * k == size:
            if sign < 0:
                out_re[k], out_re[k + half] = even_re[k] + b, even_re[k] - b
                out_im[k], out_im[k + half] = even_im[k] - a, even_im[k] + a
            else:
                out_re[k], out_re[k + half] = even_re[k] - b, even_re[k] + b
                out_im[k], out_im[k + half] = even_im[k] + a, even_im[k] - a
            continue
        out_re[k], out_re[k + half] = even_re[k] + t_re, even_re[k] - t_re
        out_im[k], out_im[k + half] = even_im[k] + t_im, even_im[k] - t_im
    return out_re, out_im


def three_pass(lhs, high, low):
    lhs_high, lhs_low = lhs
    return dot(lhs_high, high) + dot(lhs_low, high) + dot(lhs_high, low)


def spread_filter(filt_ref, out):
    count = out.shape[1]
    for part in range(2):
        rows = [filt_ref[part : part + 1, a * LANES : (a + 1) * LANES] for a in range(count)]
        rows.append(jnp.zeros((LANES - count, LANES), F32))
        turned = jnp.concatenate(rows, axis=0).T
        out[part] = jnp.concatenate(
            [turned[e * count : (e + 1) * count, :count] for e in range(LANES // count)], axis=1
        )


def edge_rows(slope_ref, centre_ref):
    lane = lax.broadcasted_iota(jnp.int32, (1, LANES), 1)
    rows = []
    for ref in (slope_ref, centre_ref):
        value = jnp.where(lane < 96, pltpu.roll(ref[:, :LANES], 64, 1), ref[:, -LANES:])
        for _ in range(3):
            part = value.astype(BF16).astype(F32)
            rows.append(part)
            value = value - part
    return jnp.concatenate(rows + [jnp.zeros((16 - len(rows), LANES), F32)], axis=0)


def range_kernel(valid, x_ref, filter_ref, slope_ref, centre_ref, tw_ref, mat_ref, *rest, devices, first, chunks, held):
    rest = rest[held:]
    outs, (in_scr, out_scr, filt_ref) = rest[:-3], rest[-3:]
    inner_refs = [outs[k * len(chunks) : (k + 1) * len(chunks)] for k in range(devices)]
    outer_refs = outs[devices * len(chunks) :]
    rows, length = x_ref.shape[1], x_ref.shape[2]
    count = length // LANES
    half = count // devices // 2
    me = lax.axis_index("lines")
    sub = 8

    @pl.when(pl.program_id(0) == 0)
    def _():
        spread_filter(filter_ref, filt_ref)

    base = me * first[1] + first[0] + pl.program_id(0) * rows
    lane = lax.broadcasted_iota(jnp.int32, (sub, LANES), 1)
    for block in range(rows // sub):
        span = slice(block * sub, (block + 1) * sub)
        keep = base + block * sub + lax.broadcasted_iota(jnp.int32, (sub, LANES), 0) < valid[0]
        re, im = [], []
        for a in range(count):
            at = slice(a * LANES, (a + 1) * LANES)
            re.append(jnp.where(keep, x_ref[0, span, at].astype(F32), 0.0))
            im.append(jnp.where(keep, x_ref[1, span, at].astype(F32), 0.0))
        re, im = fft_list(re, im, -1)
        mixed = []
        for c in range(count):
            cos, sin = tw_ref[0, c : c + 1, :], tw_ref[1, c : c + 1, :]
            mixed.append(jnp.concatenate([re[c] * cos - im[c] * sin, re[c] * sin + im[c] * cos], axis=1))
        spectrum = three_pass(split(jnp.concatenate(mixed, 0)), mat_ref[0], mat_ref[1])
        mixed = []
        for c in range(count):
            at = slice(c * sub, (c + 1) * sub)
            a, b = spectrum[at, :LANES], spectrum[at, LANES:]
            cos, sin = filt_ref[0, c : c + 1, :], filt_ref[1, c : c + 1, :]
            mixed.append(jnp.concatenate([a * cos - b * sin, a * sin + b * cos], axis=1))
        pulse = three_pass(split(jnp.concatenate(mixed, 0)), mat_ref[2], mat_ref[3])
        re, im = [], []
        for c in range(count):
            at = slice(c * sub, (c + 1) * sub)
            a, b = pulse[at, :LANES], pulse[at, LANES:]
            cos, sin = tw_ref[2, c : c + 1, :], tw_ref[3, c : c + 1, :]
            re.append(a * cos - b * sin)
            im.append(a * sin + b * cos)
        parts = fft_list(re, im, 1)
        zero = jnp.zeros((sub, LANES), F32)
        for part in range(2):
            y = parts[part]
            group = [jnp.where(lane < 96, y[a - 1] if a else zero, y[a] if a < count else zero) for a in range(count + 1)]
            group.append(zero)
            for u in range(count // 2):
                in_scr[u, part, span, :] = jnp.where(
                    lane < 64, y[2 * u], pltpu.roll(y[2 * u + 1], 64, 1)
                )
            for u in range(count // 2 + 1):
                out_scr[u, part, span, :] = jnp.where(
                    lane < 64, pltpu.roll(group[2 * u], 64, 1), group[2 * u + 1]
                )
    for k in range(devices):
        start = (me ^ k) * half
        at = 0
        for refs, tiles in zip(inner_refs[k], chunks):
            for t in range(tiles):
                refs[:, :, t * LANES : (t + 1) * LANES] = in_scr[start + at + t].astype(BF16)
            at += tiles
        for t in range(half + 1):
            outer_refs[k][:, :, t * LANES : (t + 1) * LANES] = out_scr[start + t].astype(BF16)
    if first[0] == 0:

        @pl.when(pl.program_id(0) == 0)
        def _():
            edge = edge_rows(slope_ref, centre_ref)
            wide = lax.broadcasted_iota(jnp.int32, (16, LANES), 1)
            for k in range(devices):
                at = slice(half * LANES, (half + 1) * LANES)
                known = outer_refs[k][0, :16, at].astype(F32)
                outer_refs[k][0, :16, at] = jnp.where(wide < 64, known, edge).astype(BF16)


def compress(echo, filt, slope, centre, valid, devices, part, parts, chunks, outer):
    _, rows, length = echo.shape
    count = length // LANES
    half = count // devices // 2
    mine = rows // parts
    step = min(64, mine)
    steps = mine // step
    natural = np.arange(LANES)
    turned = (natural + HALF) % LANES
    q = LANES // count
    freq = q * (natural % count) + natural // count
    twf = -angle_np(np.arange(count), natural, length)
    twi = angle_np(np.arange(count), turned, length)
    twiddles = np.stack([np.cos(twf), np.sin(twf), np.cos(twi), np.sin(twi)])
    mats = right_matrix(angle_np(natural, freq, LANES), -1) + right_matrix(
        angle_np(freq, turned, LANES), 1, 1.0 / length
    )
    inner_widths = [c * LANES for c in chunks] * devices
    width = (half + 1) * LANES
    outs = pl.pallas_call(
        functools.partial(
            range_kernel, devices=devices, first=(part * mine, rows), chunks=chunks, held=len(outer)
        ),
        grid=(steps,),
        in_specs=[
            pl.BlockSpec(memory_space=pltpu.SMEM),
            pl.BlockSpec((2, step, length), lambda i: (0, part * steps + i, 0)),
            pl.BlockSpec((2, length), lambda i: (0, 0)),
            pl.BlockSpec(slope.shape, lambda i: (0, 0)),
            pl.BlockSpec(slope.shape, lambda i: (0, 0)),
            pl.BlockSpec((4, count, LANES), lambda i: (0, 0, 0)),
            pl.BlockSpec((4, 2 * LANES, 2 * LANES), lambda i: (0, 0, 0)),
        ]
        + [pl.BlockSpec(memory_space=pl.ANY)] * len(outer),
        out_specs=[pl.BlockSpec((2, step, w), lambda i: (0, i, 0)) for w in inner_widths]
        + [pl.BlockSpec((2, step, width), lambda i: (0, part * steps + i, 0))] * devices,
        scratch_shapes=[
            pltpu.VMEM((count // 2, 2, step, LANES), F32),
            pltpu.VMEM((count // 2 + 1, 2, step, LANES), F32),
            pltpu.VMEM((2, count, LANES), F32),
        ],
        out_shape=[jax.ShapeDtypeStruct((2, mine, w), BF16) for w in inner_widths]
        + [jax.ShapeDtypeStruct((2, rows, width), BF16)] * devices,
        input_output_aliases={7 + k: len(inner_widths) + k for k in range(len(outer))},
        compiler_params=pltpu.CompilerParams(vmem_limit_bytes=RANGE_BYTES),
        cost_estimate=cost(9.0 / parts),
        name="range_compress",
    )(valid, echo, filt, slope, centre, jnp.asarray(twiddles, F32), jnp.asarray(np.stack(mats)), *outer)
    inner = [outs[k * len(chunks) : (k + 1) * len(chunks)] for k in range(devices)]
    return inner, outs[len(inner_widths) :]


def turn(turns):
    x = turns - jnp.round(turns)
    z = x * x
    a, b = [v * math.sqrt(2.0) for v in SIN_POLY], [v * math.sqrt(2.0) for v in COS_POLY]
    sin = x * (a[0] + z * (a[1] + z * (a[2] + z * a[3])))
    cos = b[0] + z * (b[1] + z * (b[2] + z * b[3]))
    return 1.0 - sin * sin, sin * cos


def focus_tile(scr, col, width, slope, centre, af_ref, ai_ref):
    lines = scr.shape[1]
    radix = lines // LANES
    at = slice(col, col + width)
    re = [scr[0, s * LANES : (s + 1) * LANES, at].astype(F32) for s in range(radix)]
    im = [scr[1, s * LANES : (s + 1) * LANES, at].astype(F32) for s in range(radix)]
    re, im = fft_list(re, im, -1)
    k = radix * lax.broadcasted_iota(jnp.int32, (LANES, width), 0)
    u = jnp.where(k >= lines // 2, k - lines, k).astype(F32) * (1.0 / lines)
    back_re, back_im = [], []
    rate = slope * (lines / 8.0)
    for c in range(radix):
        high, low = split(jnp.concatenate([re[c], im[c]], axis=0))
        freq = dot(af_ref[0, c], high) + dot(af_ref[0, c], low) + dot(af_ref[1, c], high)
        w = u - (centre - c / lines)
        cos, sin = turn(rate * w * w)
        a, b = freq[:LANES], freq[LANES:]
        high, low = split(jnp.concatenate([a * cos - b * sin, a * sin + b * cos], axis=0))
        back = dot(ai_ref[0, c], high) + dot(ai_ref[0, c], low) + dot(ai_ref[1, c], high)
        back_re.append(back[:LANES])
        back_im.append(back[LANES:])
    return fft_list(back_re, back_im, 1)


def azimuth_matrices(lines):
    radix = lines // LANES
    t = np.arange(LANES)
    forward, inverse = [], []
    for c in range(radix):
        k = c + radix * t
        forward.append(np.stack(left_matrix(angle_np(k, t, lines), -1)))
        inverse.append(np.stack(left_matrix(angle_np(t, k, lines), 1, 1.0 / lines)))
    return jnp.asarray(np.stack(forward, axis=1)), jnp.asarray(np.stack(inverse, axis=1))


def gather_lines(blocks, scr):
    me = lax.axis_index("lines")
    devices = len(blocks)
    rows = scr.shape[1] // devices
    for k, parts in enumerate(blocks):
        share = rows // len(parts)
        for h, part in enumerate(parts):
            start = pl.multiple_of((me ^ k) * rows + h * share, share)
            scr[:, pl.ds(start, share), :] = part[...]


def nested(refs, devices):
    per = len(refs) // devices
    return [refs[k * per : (k + 1) * per] for k in range(devices)]


def inner_kernel(*rest, devices, row_parts, parts):
    blocks, rest = nested(rest[: devices * row_parts], devices), rest[devices * row_parts :]
    slope_ref, centre_ref, af_ref, ai_ref, out_ref = rest[:5]
    p_refs, (scr, p_scr) = rest[5 : 5 + parts], rest[5 + parts :]
    gather_lines(blocks, scr)
    width = out_ref.shape[2]
    lane = lax.broadcasted_iota(jnp.int32, (1, LANES), 1)

    def packed(ref):
        tiles = []
        for t in range(width // LANES):
            a = pltpu.roll(ref[:, 2 * t * LANES : (2 * t + 1) * LANES], 96, 1)
            b = pltpu.roll(ref[:, (2 * t + 1) * LANES : (2 * t + 2) * LANES], 32, 1)
            tiles.append(jnp.where(lane < 64, a, b))
        return jnp.concatenate(tiles, axis=1)

    re, im = focus_tile(scr, 0, width, packed(slope_ref), packed(centre_ref), af_ref, ai_ref)
    for part, value in enumerate((re, im)):
        for s in range(len(value)):
            image = value[s].astype(BF16)
            out_ref[part, s * LANES : (s + 1) * LANES, :] = image
            p_scr[part, s * PATCH : (s + 1) * PATCH, :] = image[HALF : HALF + PATCH]
    share = p_scr.shape[1] // parts
    me = lax.axis_index("acq") if parts > 1 else 0
    for k in range(parts):
        start = pl.multiple_of((me ^ k) * share, share)
        p_refs[k][...] = p_scr[:, pl.ds(start, share), :]


def focus_inner(blocks, slope, centre, matrices, first, parts):
    devices, row_parts = len(blocks), len(blocks[0])
    _, rows, cols = blocks[0][0].shape
    lines = rows * devices * row_parts
    tile = 2 * LANES if cols % (2 * LANES) == 0 else LANES
    skip = first * LANES // (2 * tile)
    prows = lines // 2
    shape = (2, lines // LANES, 2 * LANES, 2 * LANES)
    return pl.pallas_call(
        functools.partial(inner_kernel, devices=devices, row_parts=row_parts, parts=parts),
        grid=(cols // tile,),
        in_specs=[pl.BlockSpec((2, rows, tile), lambda i: (0, 0, i))] * (devices * row_parts)
        + [pl.BlockSpec((1, 2 * tile), lambda i: (0, skip + i))] * 2
        + [pl.BlockSpec(shape, lambda i: (0, 0, 0, 0))] * 2,
        out_specs=[pl.BlockSpec((2, lines, tile), lambda i: (0, 0, i))]
        + [pl.BlockSpec((2, prows // parts, tile), lambda i: (0, 0, i))] * parts,
        scratch_shapes=[pltpu.VMEM((2, lines, tile), BF16), pltpu.VMEM((2, prows, tile), BF16)],
        out_shape=[jax.ShapeDtypeStruct((2, lines, cols), BF16)]
        + [jax.ShapeDtypeStruct((2, prows // parts, cols), BF16)] * parts,
        compiler_params=pltpu.CompilerParams(vmem_limit_bytes=VMEM_BYTES),
        cost_estimate=cost(0.8 * cols / LANES),
        name="focus_inner",
    )(*[part for parts_of in blocks for part in parts_of], slope, centre, *matrices)


def outer_kernel(*rest, devices):
    blocks, rest = rest[:devices], rest[devices:]
    slope_ref, centre_ref, af_ref, ai_ref, out_ref, scr = rest
    gather_lines([[b] for b in blocks], scr)
    width = scr.shape[2]
    lane = lax.broadcasted_iota(jnp.int32, (1, LANES), 1)
    pairs = width // LANES - 1

    me = lax.axis_index("lines")

    def extended(ref, row):
        before = after = jnp.zeros((1, LANES), F32)
        for k in range(1, devices):
            told = blocks[k][0, :16, pairs * LANES :].astype(F32)
            told = told[row : row + 1] + told[row + 1 : row + 2] + told[row + 2 : row + 3]
            before = jnp.where((me ^ k) == me - 1, told, before)
            after = jnp.where((me ^ k) == me + 1, pltpu.roll(told, 64, 1), after)
        return [before] + [ref[:, t * LANES : (t + 1) * LANES] for t in range(ref.shape[1] // LANES)] + [after]

    def group(values, a):
        return jnp.where(lane < 96, pltpu.roll(values[a], 96, 1), pltpu.roll(values[a + 1], 96, 1))

    def packed(values, u):
        left = pltpu.roll(group(values, 2 * u), 64, 1)
        if u == pairs:
            return jnp.where(lane < 64, left, 0.0)
        return jnp.where(lane < 64, left, group(values, 2 * u + 1))

    slopes, centres = extended(slope_ref, 0), extended(centre_ref, 3)
    u = 0
    while u <= pairs:
        tiles = min(2, pairs + 1 - u)
        slope = jnp.concatenate([packed(slopes, u + t) for t in range(tiles)], axis=1)
        centre = jnp.concatenate([packed(centres, u + t) for t in range(tiles)], axis=1)
        at = slice(u * LANES, (u + tiles) * LANES)
        for part, value in enumerate(focus_tile(scr, u * LANES, tiles * LANES, slope, centre, af_ref, ai_ref)):
            for s in range(len(value)):
                out_ref[part, s * LANES : (s + 1) * LANES, at] = value[s].astype(BF16)
        u += tiles


def focus_outer(blocks, slope, centre, matrices):
    devices = len(blocks)
    _, rows, cols = blocks[0].shape
    lines = rows * devices
    vmem = pl.BlockSpec(memory_space=pltpu.VMEM)
    return pl.pallas_call(
        functools.partial(outer_kernel, devices=devices),
        in_specs=[vmem] * (devices + 4),
        out_specs=vmem,
        out_shape=jax.ShapeDtypeStruct((2, lines, cols), BF16),
        scratch_shapes=[pltpu.VMEM((2, lines, cols), BF16)],
        compiler_params=pltpu.CompilerParams(vmem_limit_bytes=VMEM_BYTES),
        cost_estimate=cost(4.0),
        name="focus_outer",
    )(*blocks, slope, centre, *matrices)


def patch_matrices():
    n = np.arange(PATCH)
    theta = angle_np(n, n, PATCH)

    def lanes(sign):
        cos = np.kron(np.eye(2), np.cos(theta))
        sin = sign * np.kron(np.eye(2), np.sin(theta))
        return np.stack(split_np(np.block([[cos, sin], [-sin, cos]])))

    high, low = split_np(np.concatenate([np.cos(theta), np.sin(theta)], axis=0))
    column = np.concatenate([high, high, low], axis=1)
    return jnp.asarray(lanes(-1)), jnp.asarray(lanes(1)), jnp.asarray(column)


def columns(value, column_ref, sign):
    high, low = split(value)
    both = dot(column_ref[...], jnp.concatenate([high, low, high], axis=0))
    c_re, c_im = both[:PATCH, :LANES], both[:PATCH, LANES:]
    s_re, s_im = both[PATCH:, :LANES], both[PATCH:, LANES:]
    if sign < 0:
        return c_re + s_im, c_im - s_re
    return c_re - s_im, c_im + s_re


def power(re, im):
    lane = lax.broadcasted_iota(jnp.int32, (1, LANES), 1)
    total = jnp.sum(re * re + im * im, axis=0, keepdims=True)
    left = jnp.sum(jnp.where(lane < PATCH, total, 0.0), axis=1, keepdims=True)
    right = jnp.sum(jnp.where(lane < PATCH, 0.0, total), axis=1, keepdims=True)
    return jnp.where(lane < PATCH, left, right) * (1.0 / (PATCH * PATCH))


def window_kernel(offsets, *rest, chunks):
    inner_refs, rest = rest[: len(chunks)], rest[len(chunks) :]
    outer_ref, lane_ref, column_ref = rest[:3]
    spec_ref, image, windows = rest[3:]
    lines, pairs = outer_ref.shape[1], outer_ref.shape[2] // LANES - 1
    lane = lax.broadcasted_iota(jnp.int32, (1, LANES), 1)
    edge = jnp.zeros((HALF, image.shape[2]), F32)
    for part in range(2):
        image[part, :HALF, :] = edge
        image[part, HALF + lines : 2 * HALF + lines, :] = edge
    where = [(c, t) for c, tiles in enumerate(chunks) for t in range(tiles)]
    for u in range(pairs + 1):
        for part in range(2):
            fresh = outer_ref[part, :, u * LANES : (u + 1) * LANES].astype(F32)
            at = slice(HALF, HALF + lines)
            if u == pairs:
                image[part, at, 2 * u * LANES : (2 * u + 1) * LANES] = fresh
                continue
            c, t = where[u]
            known = inner_refs[c][part, :, t * LANES : (t + 1) * LANES].astype(F32)
            image[part, at, 2 * u * LANES : (2 * u + 1) * LANES] = jnp.where(
                lane < 64, fresh, pltpu.roll(known, 64, 1)
            )
            image[part, at, (2 * u + 1) * LANES : (2 * u + 2) * LANES] = jnp.where(
                lane < 64, pltpu.roll(fresh, 64, 1), known
            )
    row_blocks = lines // (2 * PATCH)
    wide = lax.broadcasted_iota(jnp.int32, (PATCH + 8, LANES), 1)

    def block(i, carry):
        gains = []
        for u in range(pairs):
            found = [[], []]
            for side in range(2):
                j = 2 * u + side
                start = 2 * PATCH * i + PATCH + offsets[0, i, j]
                shift = PATCH + offsets[1, i, j]
                back = jnp.bitwise_and(2 * LANES - shift + side * PATCH, LANES - 1)
                base = pl.multiple_of(lax.shift_left(lax.shift_right_logical(start, 3), 3), 8)
                up = PATCH + 8 - jnp.bitwise_and(start, 7)
                for part in range(2):
                    left = image[part, pl.ds(base, PATCH + 8), j * LANES : (j + 1) * LANES]
                    right = image[part, pl.ds(base, PATCH + 8), (j + 1) * LANES : (j + 2) * LANES]
                    turned = pltpu.roll(jnp.where(wide >= shift, left, right), back, 1)
                    found[part].append(pltpu.roll(turned, up, 0)[:PATCH])
            re = jnp.where(lane < PATCH, found[0][0], found[0][1])
            im = jnp.where(lane < PATCH, found[1][0], found[1][1])
            gains.append(lax.rsqrt(power(re, im) + EPS) * (1.0 / PATCH**3))
            windows[u * PATCH : (u + 1) * PATCH, :] = jnp.concatenate([re, im], axis=1).astype(BF16)
        mixed = dot(windows[...], lane_ref[0]) + dot(windows[...], lane_ref[1])
        for u in range(pairs):
            re, im = columns(mixed[u * PATCH : (u + 1) * PATCH], column_ref, -1)
            spec_ref[0, i * pairs + u] = re * gains[u]
            spec_ref[1, i * pairs + u] = im * gains[u]
        return carry

    lax.fori_loop(0, row_blocks, block, 0)


def window_spectra(inner, outer, patch, offsets, chunks):
    lines, pairs = outer.shape[1], outer.shape[2] // LANES - 1
    vmem = pl.BlockSpec(memory_space=pltpu.VMEM)
    return pl.pallas_call(
        functools.partial(window_kernel, chunks=chunks),
        in_specs=[pl.BlockSpec(memory_space=pltpu.SMEM)] + [vmem] * (len(chunks) + 3),
        out_specs=vmem,
        out_shape=jax.ShapeDtypeStruct((2, lines // (2 * PATCH) * pairs, PATCH, LANES), F32),
        scratch_shapes=[
            pltpu.VMEM((2, lines + 2 * HALF + 8, (2 * pairs + 1) * LANES), F32),
            pltpu.VMEM((pairs * PATCH, 2 * LANES), BF16),
        ],
        compiler_params=pltpu.CompilerParams(vmem_limit_bytes=VMEM_BYTES),
        cost_estimate=cost(4.0),
        name="window_spectra",
    )(offsets, *inner, outer, patch[0], patch[2])


def primary_kernel(reference, *rest, parts):
    shares, (lane_ref, column_ref, out_ref, scr) = rest[:-4], rest[-4:]
    source = lax.axis_index("acq") ^ reference[0] if parts > 1 else 0
    for k in range(parts):

        @pl.when(source == k)
        def _(k=k):
            col = 0
            for ref in shares[k::parts]:
                scr[:, :, col : col + ref.shape[2]] = ref[...]
                col += ref.shape[2]

    rows, cols = scr.shape[1], scr.shape[2]
    for u in range(cols // LANES):
        lanes = slice(u * LANES, (u + 1) * LANES)
        both = jnp.concatenate([scr[0, :, lanes], scr[1, :, lanes]], axis=1)
        mixed = dot(both, lane_ref[0]) + dot(both, lane_ref[1])
        for i in range(rows // PATCH):
            at = slice(i * PATCH, (i + 1) * PATCH)
            value = both[at].astype(F32)
            gain = lax.rsqrt(power(value[:, :LANES], value[:, LANES:]) + EPS)
            re, im = columns(mixed[at], column_ref, -1)
            out_ref[0, at, lanes] = (re * gain).astype(BF16)
            out_ref[1, at, lanes] = (im * gain).astype(BF16)


def primary_spectra(reference, shares, patch):
    vmem = pl.BlockSpec(memory_space=pltpu.VMEM)
    flat = [share for chunk in shares for share in chunk]
    shape = flat[0].shape[:2] + (sum(chunk[0].shape[2] for chunk in shares),)
    return pl.pallas_call(
        functools.partial(primary_kernel, parts=len(shares[0])),
        in_specs=[pl.BlockSpec(memory_space=pltpu.SMEM)] + [vmem] * (len(flat) + 2),
        out_specs=vmem,
        out_shape=jax.ShapeDtypeStruct(shape, BF16),
        scratch_shapes=[pltpu.VMEM(shape, BF16)],
        compiler_params=pltpu.CompilerParams(vmem_limit_bytes=VMEM_BYTES),
        cost_estimate=cost(1.0),
        name="primary_spectra",
    )(reference, *flat, patch[0], patch[2])


def correlate_kernel(*rest, parts):
    shares, (spec_ref, inverse_ref, column_ref, out_ref) = rest[:parts], rest[parts:]
    _, rows, cols = shares[0].shape
    pairs = cols // LANES
    per = rows // PATCH
    me = lax.axis_index("acq") if parts > 1 else 0
    for k in range(parts):
        for r in range(per):
            i = (me ^ k) * per + r
            middle = []
            for u in range(pairs):
                at, lanes = slice(r * PATCH, (r + 1) * PATCH), slice(u * LANES, (u + 1) * LANES)
                p_re, p_im = shares[k][0, at, lanes].astype(F32), shares[k][1, at, lanes].astype(F32)
                s_re, s_im = spec_ref[0, i * pairs + u], spec_ref[1, i * pairs + u]
                cross = jnp.concatenate([p_re * s_re + p_im * s_im, p_im * s_re - p_re * s_im], axis=1)
                middle.append(jnp.concatenate(columns(cross, column_ref, 1), axis=1))
            surface = three_pass(split(jnp.concatenate(middle, axis=0)), inverse_ref[0], inverse_ref[1])
            line = pl.ds(pl.multiple_of(i * PATCH, PATCH), PATCH)
            for u in range(pairs):
                lanes = slice(u * LANES, (u + 1) * LANES)
                block = surface[u * PATCH : (u + 1) * PATCH]
                out_ref[0, 0, line, lanes] = block[:, :LANES]
                out_ref[0, 1, line, lanes] = block[:, LANES:]


def correlate(shares, spectrum, patch):
    parts = len(shares)
    _, rows, cols = shares[0].shape
    vmem = pl.BlockSpec(memory_space=pltpu.VMEM)
    return pl.pallas_call(
        functools.partial(correlate_kernel, parts=parts),
        in_specs=[vmem] * (parts + 3),
        out_specs=vmem,
        out_shape=jax.ShapeDtypeStruct((1, 2, rows * parts, cols), F32),
        compiler_params=pltpu.CompilerParams(vmem_limit_bytes=VMEM_BYTES),
        cost_estimate=cost(2.0),
        name="correlate",
    )(*shares, spectrum, patch[1], patch[2])


def far_first(devices):
    return list(range(2, devices)) + list(range(min(2, devices)))[::-1]


def trade(block, k, axis):
    if k == 0:
        return block
    return lax.ppermute(block, axis, [(i, i ^ k) for i in range(lax.axis_size(axis))])


def on_device(echo, filt, slope, centre, valid, reference, offsets):
    devices, parts = lax.axis_size("lines"), lax.axis_size("acq")
    rows, length = echo.shape[2], echo.shape[3]
    lines = rows * devices
    tiles = length // devices // (2 * LANES)
    chunks = (tiles // COLUMN_PARTS,) * COLUMN_PARTS if tiles % COLUMN_PARTS == 0 else (tiles,)
    row_parts = ROW_PARTS if rows % (32 * ROW_PARTS) == 0 else 1
    spread = lines // (2 * PATCH) % parts == 0
    matrices = azimuth_matrices(lines)
    patch = patch_matrices()
    inner = [[[] for _ in range(devices)] for _ in chunks]
    outer = []
    for h in range(row_parts):
        mine, outer = compress(echo[0], filt[0], slope, centre, valid, devices, h, row_parts, chunks, outer)
        for c in range(len(chunks)):
            for k in far_first(devices):
                inner[c][k].append(trade(mine[k][c], k, "lines"))
    outer = {k: trade(outer[k], k, "lines") for k in far_first(devices)}
    outer = [outer[k] for k in range(devices)]
    if len(inner) > 1:
        inner[-1], outer[1] = lax.optimization_barrier((inner[-1], outer[1]))
    images, primaries = [], []
    for c in range(len(chunks)):
        image, *shares = focus_inner(
            inner[c], slope, centre, matrices, 2 * sum(chunks[:c]), parts if spread else 1
        )
        images.append(image)
        if spread:
            shares = {k: trade(shares[k], k, "acq") for k in far_first(parts)}
            shares = [shares[k] for k in range(parts)]
        else:
            mine = lax.axis_index("acq") == reference[0]
            shares = [lax.psum(jnp.where(mine, shares[0], 0).astype(BF16), "acq")]
        primaries.append(shares)
    outer = focus_outer(outer, slope, centre, matrices)
    spectrum = window_spectra(images, outer, patch, offsets[0], chunks)
    shares = [primary_spectra(reference, primaries, patch)]
    for k in range(1, parts if spread else 1):
        low = k & -k
        shares.append(trade(shares[k - low], low, "acq"))
    return correlate(shares, spectrum, patch)


def solution(mesh):
    return jax.shard_map(
        on_device,
        mesh=mesh,
        in_specs=(
            P(("stack", "acq"), None, "lines", None),
            P(("stack", "acq"), None, None),
            P(("stack", "acq"), "lines"),
            P(("stack", "acq"), "lines"),
            P(("stack", "acq")),
            P("stack"),
            P(("stack", "acq"), None, None, "lines"),
        ),
        out_specs=P(("stack", "acq"), None, None, "lines"),
        check_vma=False,
    )
```

time: 80.1 us -> 60.3 us (0.75)
  Pallas kernels: 37.5 us -> 24 us
  waiting for transfers between devices: 15.2 us -> 9.61 us
  starting transfers between devices: 19.3 us -> 24.2 us
  local copies, waits for them, and re-layouts: 4.41 us -> 0.95 us
  other arithmetic: 1.34 us -> 0 us
    pallas_call x1, Pallas kernels: 13.2 us -> 4.24 us  [focus_outer(): pl.pallas_call(functools.partial(outer_kernel, devices=devices), in_specs...]
    ppermute x14 -> x18, waiting for transfers between devices: 15.2 us -> 9.61 us  [trade(): lax.ppermute(block, axis, [(i, i ^ k) for i in range(lax.axis_size(axis))])]
    ppermute x14 -> x18, starting transfers between devices: 19.3 us -> 24.2 us  [trade(): lax.ppermute(block, axis, [(i, i ^ k) for i in range(lax.axis_size(axis))])]
    pallas_call x1, Pallas kernels: 5.65 us -> 2.03 us  [correlate(): pl.pallas_call(functools.partial(correlate_kernel, parts=parts), in_specs...]
    another operation x2 -> x0, local copies, waits for them, and re-layouts: 1.55 us -> none  [compress(): filt.reshape(2, LANES, count).transpose(0, 2, 1)]
    unnamed x30 -> x22, local copies, waits for them, and re-layouts: 2.27 us -> 0.95 us
    another operation x2 -> x0, other arithmetic: 1.28 us -> none  [the longest x1 0.66 us: focus_inner(): jnp.stack([me, me_acq]).astype(jnp.int32)]
    pallas_call x2 -> x5, Pallas kernels: 18.7 us -> 17.7 us  [the longest x1 9.29 us: compress(): pl.pallas_call(functools.partial(range_kernel, devices=devices, first=(pa...]
  transfers between devices with their start and end apart: 14 -> 18, of which waited for: 3 -> 7; matrix products, arithmetic and copies ran while one was open for 2% -> 0% of each run, Pallas kernels for 26% -> 21%
where the time goes in v1:
time: 60.3 us; the launch traced here: 60.2 us
  starting transfers between devices  24.2 us (40%)
  Pallas kernels  24 us (40%)
  waiting for transfers between devices  9.61 us (16%)
  between operations  1.47 us (2%)
  local copies, waits for them, and re-layouts  0.95 us (2%)
    ppermute x18, starting transfers between devices, trade(): lax.ppermute(block, axis, [(i, i ^ k) for i in range(lax.axis_size(axis))])  24.2 us
    ppermute x18, waiting for transfers between devices, trade(): lax.ppermute(block, axis, [(i, i ^ k) for i in range(lax.axis_size(axis))])  9.61 us
    pallas_call x1, Pallas kernels, compress(): pl.pallas_call(functools.partial(range_kernel, devices=devices, first=(pa...  9.29 us
    pallas_call x1, Pallas kernels, focus_outer(): pl.pallas_call(functools.partial(outer_kernel, devices=devices), in_specs...  4.24 us
    pallas_call x1, Pallas kernels, window_spectra(): pl.pallas_call(functools.partial(window_kernel, chunks=chunks), in_specs=...  4.02 us
    pallas_call x2, Pallas kernels, focus_inner(): pl.pallas_call(functools.partial(inner_kernel, devices=devices, row_parts...  3.17 us
    pallas_call x1, Pallas kernels, correlate(): pl.pallas_call(functools.partial(correlate_kernel, parts=parts), in_specs...  2.03 us
    pallas_call x1, Pallas kernels, primary_spectra(): pl.pallas_call(functools.partial(primary_kernel, parts=len(shares[0])), i...  1.22 us
  transfers between devices with their start and end apart: 18, of which 7 were waited for; matrix products, arithmetic and copies ran while one was open for 0% of the time, Pallas kernels for 21%

profile of v1, /device:TPU:0, one launch (start us, length us, event | category | flops | bytes accessed | tf_op | source)
XLA Modules:
  0.0 60.2 jit_solution(2234411072216464718)
XLA Ops:
  0.7 0.0 copy-start.3
  0.7 0.0 copy-start.4
  0.7 9.3 %range_compress.1 = (bf16[2,128,256]{2,1,0:T(8,128)(2,1)}, bf16[2,128,256]{2,1,0:T(8,128)(2,1)}, bf16[2,128,256]{2,1,0:T(8,128)(2,1)}, bf16[2,128,256]{2,1,0:T(8...) custom-call(s32[1]{0:T(128)S(6)} %copy.15.valid, ...), custom_call_target="tpu_custom_call" | custom-call | flops 8999999488 | bytes 31500000 | tf_op jit(solution)/shard_map/range_compress/pallas_call | solution.py:230
  10.0 0.5 collective-permute-start.9
  10.5 0.1 collective-permute-start.6
  10.6 0.4 collective-permute-start
  11.0 2.6 %collective-permute-start.1 = (bf16[2,128,256]{2,1,0:T(8,128)(2,1)}, bf16[2,128,256]{2,1,0:T(8,128)(2,1)S(1)}, u32[]{:S(2)}, u32[]{:S(2)}) collective-permute-start(bf16[2,128,256]{2,1,0:T(8,128)(2,1)} %get-tuple-element.34), channel_id=1, source_target_pairs={{0,2},{1,3},{2,0},{3,1},{4,6},{5,7},{6,4},{7,5},{8,10},{9,11},{10,... | collective-permute-start | bytes 393224 | tf_op jit(solution)/shard_map/ppermute | solution.py:633
  13.6 0.1 collective-permute-start.2
  13.7 0.0 collective-permute-done.6.rest_1_
  13.7 1.7 %collective-permute-start.7 = (bf16[2,128,256]{2,1,0:T(8,128)(2,1)}, bf16[2,128,256]{2,1,0:T(8,128)(2,1)S(1)}, u32[]{:S(2)}, u32[]{:S(2)}) collective-permute-start(bf16[2,128,256]{2,1,0:T(8,128)(2,1)} %get-tuple-element.42), channel_id=1, source_target_pairs={{0,2},{1,3},{2,0},{3,1},{4,6},{5,7},{6,4},{7,5},{8,10},{9,11},{10,... | collective-permute-start | bytes 393224 | tf_op jit(solution)/shard_map/ppermute | solution.py:633
  15.4 0.0 collective-permute-done.rest_1_
  15.4 0.0 collective-permute-start.8
  15.4 2.7 %collective-permute-done.1.rest_2_ = bf16[2,128,256]{2,1,0:T(8,128)(2,1)S(1)} collective-permute-done((bf16[2,128,256]{2,1,0:T(8,128)(2,1)}, bf16[2,128,256]{2,1,0:T(8,128)(2,1)S(1)}, u32[]{:S(2)}, u32[]{:S(2)}) %collective-permute-start.1) | collective-permute-done | bytes 131104 | tf_op jit(solution)/shard_map/ppermute | solution.py:633
  18.1 2.0 %collective-permute-start.16 = (bf16[2,128,640]{2,1,0:T(8,128)(2,1)}, bf16[2,128,640]{2,1,0:T(8,128)(2,1)S(1)}, u32[]{:S(2)}, u32[]{:S(2)}) collective-permute-start(bf16[2,128,640]{2,1,0:T(8,128)(2,1)} %get-tuple-element.57), channel_id=1, source_target_pairs={{0,2},{1,3},{2,0},{3,1},{4,6},{5,7},{6,4},{7,5},{8,10},{9,11},{10,... | collective-permute-start | bytes 983048 | tf_op jit(solution)/shard_map/ppermute | solution.py:633
  20.1 0.4 collective-permute-done.2.rest_3_
  20.5 1.8 %collective-permute-start.17 = (bf16[2,128,640]{2,1,0:T(8,128)(2,1)}, bf16[2,128,640]{2,1,0:T(8,128)(2,1)S(1)}, u32[]{:S(2)}, u32[]{:S(2)}) collective-permute-start(bf16[2,128,640]{2,1,0:T(8,128)(2,1)} %get-tuple-element.58), channel_id=1, source_target_pairs={{0,3},{1,2},{2,1},{3,0},{4,7},{5,6},{6,5},{7,4},{8,11},{9,10},{10,... | collective-permute-start | bytes 983048 | tf_op jit(solution)/shard_map/ppermute | solution.py:633
  22.4 0.9 %copy-done.9 = bf16[2,128,256]{2,1,0:T(8,128)(2,1)S(1)} copy-done((bf16[2,128,256]{2,1,0:T(8,128)(2,1)S(1)}, bf16[2,128,256]{2,1,0:T(8,128)(2,1)}, u32[]{:S(2)}) %copy-start.9) | copy-done | bytes 131096
  23.3 1.6 %focus_inner.2 = (bf16[2,512,256]{2,1,0:T(8,128)(2,1)S(1)}, bf16[2,64,256]{2,1,0:T(8,128)(2,1)S(1)}, bf16[2,64,256]{2,1,0:T(8,128)(2,1)S(1)}, bf16[2,64,256]{2,1,0:T(8,128)(2,1)S(1)}, bf16[2,64,256]{2,1,0:T(8,128)(2,1)S(1)}) custom-call(bf16[2,128,256]{2,1,0:T(8,128)(2,1)S(1)} %copy-done.9, bf16[2,128,256]{2,1,0:T(8,128)(2,1)S(1)} %collective-permute-done.rest_1_, ...), custom_call_target="tpu_custom_call" | custom-call | flops 1600000000 | bytes 5600000 | tf_op jit(solution)/shard_map/focus_inner/pallas_call | solution.py:360
  24.8 0.0 collective-permute-done.7.rest_2_
  24.9 1.6 %collective-permute-start.3 = (bf16[2,64,256]{2,1,0:T(8,128)(2,1)S(1)}, bf16[2,64,256]{2,1,0:T(8,128)(2,1)S(1)}, u32[]{:S(2)}, u32[]{:S(2)}) collective-permute-start(bf16[2,64,256]{2,1,0:T(8,128)(2,1)S(1)} %get-tuple-element.37), channel_id=1, source_target_pairs={{0,4},{4,0},{8,12},{12,8},{1,5},{5,1},{9,13},{13,9},{2,6},{6,2},{1... | collective-permute-start | bytes 196616 | tf_op jit(solution)/shard_map/ppermute | solution.py:633
  26.5 0.0 collective-permute-done.8.rest_3_
  26.5 2.6 %collective-permute-start.4 = (bf16[2,64,256]{2,1,0:T(8,128)(2,1)S(1)}, bf16[2,64,256]{2,1,0:T(8,128)(2,1)S(1)}, u32[]{:S(2)}, u32[]{:S(2)}) collective-permute-start(bf16[2,64,256]{2,1,0:T(8,128)(2,1)S(1)} %get-tuple-element.38), channel_id=1, source_target_pairs={{0,8},{4,12},{8,0},{12,4},{1,9},{5,13},{9,1},{13,5},{2,10},{6,14},... | collective-permute-start | bytes 196616 | tf_op jit(solution)/shard_map/ppermute | solution.py:633
  29.1 0.0 collective-permute-done.9.rest_1_
  29.1 1.0 %collective-permute-start.5 = (bf16[2,64,256]{2,1,0:T(8,128)(2,1)S(1)}, bf16[2,64,256]{2,1,0:T(8,128)(2,1)S(1)}, u32[]{:S(2)}, u32[]{:S(2)}) collective-permute-start(bf16[2,64,256]{2,1,0:T(8,128)(2,1)S(1)} %get-tuple-element.39), channel_id=1, source_target_pairs={{0,12},{4,8},{8,4},{12,0},{1,13},{5,9},{9,5},{13,1},{2,14},{6,10},... | collective-permute-start | bytes 196616 | tf_op jit(solution)/shard_map/ppermute | solution.py:633
  30.1 1.6 %focus_inner.3 = (bf16[2,512,256]{2,1,0:T(8,128)(2,1)S(1)}, bf16[2,64,256]{2,1,0:T(8,128)(2,1)S(1)}, bf16[2,64,256]{2,1,0:T(8,128)(2,1)S(1)}, bf16[2,64,256]{2,1,0:T(8,128)(2,1)S(1)}, bf16[2,64,256]{2,1,0:T(8,128)(2,1)S(1)}) custom-call(bf16[2,128,256]{2,1,0:T(8,128)(2,1)S(1)} %copy-done.8, bf16[2,128,256]{2,1,0:T(8,128)(2,1)S(1)} %collective-permute-done.6.rest_1_, ...), custom_call_target="tpu_custom_call" | custom-call | flops 1600000000 | bytes 5600000 | tf_op jit(solution)/shard_map/focus_inner/pallas_call | solution.py:360
  31.7 0.0 copy-start.10
  31.7 0.0 collective-permute-done.3.rest_1_
  31.7 0.3 collective-permute-start.10
  32.0 1.2 %collective-permute-done.4.rest_2_ = bf16[2,64,256]{2,1,0:T(8,128)(2,1)S(1)} collective-permute-done((bf16[2,64,256]{2,1,0:T(8,128)(2,1)S(1)}, bf16[2,64,256]{2,1,0:T(8,128)(2,1)S(1)}, u32[]{:S(2)}, u32[]{:S(2)}) %collective-permute-start.4) | collective-permute-done | bytes 65568 | tf_op jit(solution)/shard_map/ppermute | solution.py:633
  33.3 1.9 %collective-permute-start.11 = (bf16[2,64,256]{2,1,0:T(8,128)(2,1)S(1)}, bf16[2,64,256]{2,1,0:T(8,128)(2,1)S(1)}, u32[]{:S(2)}, u32[]{:S(2)}) collective-permute-start(bf16[2,64,256]{2,1,0:T(8,128)(2,1)S(1)} %get-tuple-element.51), channel_id=1, source_target_pairs={{0,8},{4,12},{8,0},{12,4},{1,9},{5,13},{9,1},{13,5},{2,10},{6,14},... | collective-permute-start | bytes 196616 | tf_op jit(solution)/shard_map/ppermute | solution.py:633
  35.2 0.1 collective-permute-done.5.rest_3_
  35.2 2.9 %collective-permute-start.12 = (bf16[2,64,256]{2,1,0:T(8,128)(2,1)S(1)}, bf16[2,64,256]{2,1,0:T(8,128)(2,1)S(1)}, u32[]{:S(2)}, u32[]{:S(2)}) collective-permute-start(bf16[2,64,256]{2,1,0:T(8,128)(2,1)S(1)} %get-tuple-element.52), channel_id=1, source_target_pairs={{0,12},{4,8},{8,4},{12,0},{1,13},{5,9},{9,5},{13,1},{2,14},{6,10},... | collective-permute-start | bytes 196616 | tf_op jit(solution)/shard_map/ppermute | solution.py:633
  38.8 0.0 collective-permute-done.10.rest_5_
  38.8 0.0 collective-permute-done.11.rest_6_
  38.8 3.1 %collective-permute-done.12.rest_7_ = bf16[2,64,256]{2,1,0:T(8,128)(2,1)S(1)} collective-permute-done((bf16[2,64,256]{2,1,0:T(8,128)(2,1)S(1)}, bf16[2,64,256]{2,1,0:T(8,128)(2,1)S(1)}, u32[]{:S(2)}, u32[]{:S(2)}) %collective-permute-start.12) | collective-permute-done | bytes 65568 | tf_op jit(solution)/shard_map/ppermute | solution.py:633
  41.9 1.2 %primary_spectra.1.rest_0_ = bf16[2,64,512]{2,1,0:T(8,128)(2,1)S(1)} custom-call(s32[1]{0:T(128)S(6)} %copy.16.reference, bf16[2,64,256]{2,1,0:T(8,128)(2,1)S(1)} %get-tuple-element.36.rest_0_, bf16[2,64,256]{2,1,0:T(8,128)(2,1)S(1)} %collective-permute-done.3.rest_1_, bf16[2,64,256]{2,1,0:T(8,128)(2,1)S(1)} %collective-permute-done.4.rest_2_, ...), custom_call_target="tpu_custom_call" | custom-call | flops 1000000000 | bytes 3500000 | tf_op jit(solution)/shard_map/primary_spectra/pallas_call | solution.py:574
  43.1 3.3 %collective-permute-start.14 = (bf16[2,64,512]{2,1,0:T(8,128)(2,1)S(1)}, bf16[2,64,512]{2,1,0:T(8,128)(2,1)S(1)}, u32[]{:S(2)}, u32[]{:S(2)}) collective-permute-start(bf16[2,64,512]{2,1,0:T(8,128)(2,1)S(1)} %primary_spectra.1.rest_0_), channel_id=1, source_target_pairs={{0,8},{4,12},{8,0},{12,4},{1,9},{5,13},{9,1},{13,5},{2,10},{6,14},... | collective-permute-start | bytes 393224 | tf_op jit(solution)/shard_map/ppermute | solution.py:633
  46.4 0.0 collective-permute-done.16.rest_2_
  46.4 0.0 collective-permute-done.17.rest_3_
  46.5 0.0 copy-start.2
  46.5 4.2 %focus_outer.1.rest_2_ = bf16[2,512,640]{2,1,0:T(8,128)(2,1)S(1)} custom-call(bf16[2,128,640]{2,1,0:T(8,128)(2,1)S(1)} %copy-done.10, bf16[2,128,640]{2,1,0:T(8,128)(2,1)S(1)} %collective-permute-done.9.rest_1_, bf16[2,128,640]{2,1,0:T(8,128)(2,1)S(1)} %collective-permute-done.16.rest_2_, bf16[2,128,640]{2,1,0:T(8,128)(2,1)S(1)} %collective-permute-done.17.rest_3_, ...), custom_call_target="tpu_custom_call" | custom-call | flops 4000000000 | bytes 14000000 | tf_op jit(solution)/shard_map/focus_outer/pallas_call | solution.py:423
  50.7 0.8 %collective-permute-start.13 = (bf16[2,64,512]{2,1,0:T(8,128)(2,1)S(1)}, bf16[2,64,512]{2,1,0:T(8,128)(2,1)S(1)}, u32[]{:S(2)}, u32[]{:S(2)}) collective-permute-start(bf16[2,64,512]{2,1,0:T(8,128)(2,1)S(1)} %primary_spectra.1.rest_0_), channel_id=1, source_target_pairs={{0,4},{4,0},{8,12},{12,8},{1,5},{5,1},{9,13},{13,9},{2,6},{6,2},{1... | collective-permute-start | bytes 393224 | tf_op jit(solution)/shard_map/ppermute | solution.py:633
  51.6 0.8 %collective-permute-done.14.rest_2_ = bf16[2,64,512]{2,1,0:T(8,128)(2,1)S(1)} collective-permute-done((bf16[2,64,512]{2,1,0:T(8,128)(2,1)S(1)}, bf16[2,64,512]{2,1,0:T(8,128)(2,1)S(1)}, u32[]{:S(2)}, u32[]{:S(2)}) %collective-permute-start.14) | collective-permute-done | bytes 131104 | tf_op jit(solution)/shard_map/ppermute | solution.py:633
  52.3 0.5 collective-permute-start.15
  52.8 4.0 %window_spectra.1.rest_4_ = f32[2,16,64,128]{3,2,1,0:T(8,128)S(1)} custom-call(s32[2,4,8]{2,1,0:T(4,128)S(1)} %bitcast.3, bf16[2,512,256]{2,1,0:T(8,128)(2,1)S(1)} %get-tuple-element.53.rest_0_, bf16[2,512,256]{2,1,0:T(8,128)(2,1)S(1)} %get-tuple-element.54.rest_1_, bf16[2,512,640]{2,1,0:T(8,128)(2,1)S(1)} %focus_outer.1.rest_2_, ...), custom_call_target="tpu_custom_call" | custom-call | flops 4000000000 | bytes 14000000 | tf_op jit(solution)/shard_map/window_spectra/pallas_call | solution.py:529
  56.9 0.0 collective-permute-done.13.rest_1_
  56.9 1.3 %collective-permute-done.15.rest_3_ = bf16[2,64,512]{2,1,0:T(8,128)(2,1)S(1)} collective-permute-done((bf16[2,64,512]{2,1,0:T(8,128)(2,1)S(1)}, bf16[2,64,512]{2,1,0:T(8,128)(2,1)S(1)}, u32[]{:S(2)}, u32[]{:S(2)}) %collective-permute-start.15) | collective-permute-done | bytes 131104 | tf_op jit(solution)/shard_map/ppermute | solution.py:633
  58.1 2.0 %correlate.1 = f32[1,2,256,512]{3,2,1,0:T(8,128)} custom-call(bf16[2,64,512]{2,1,0:T(8,128)(2,1)S(1)} %primary_spectra.1.rest_0_, bf16[2,64,512]{2,1,0:T(8,128)(2,1)S(1)} %collective-permute-done.13.rest_1_, bf16[2,64,512]{2,1,0:T(8,128)(2,1)S(1)} %collective-permute-done.14.rest_2_, bf16[2,64,512]{2,1,0:T(8,128)(2,1)S(1)} %collective-permute-done.15.rest_3_, ...), custom_call_target="tpu_custom_call" | custom-call | flops 2000000000 | bytes 7000000 | tf_op jit(solution)/shard_map/correlate/pallas_call | solution.py:615
  (17 shorter events, 0.0 us)
Async XLA Ops:
  0.7 21.7 %copy-start = (f32[1,1024]{1,0:T(1,128)S(1)}, f32[1,1024]{1,0:T(1,128)}, u32[]{:S(2)}) copy-start(f32[1,1024]{1,0:T(1,128)} %rest_4_.6) | copy-start | bytes 12292
  0.7 21.7 %copy-start.1 = (f32[1,1024]{1,0:T(1,128)S(1)}, f32[1,1024]{1,0:T(1,128)}, u32[]{:S(2)}) copy-start(f32[1,1024]{1,0:T(1,128)} %rest_5_.6) | copy-start | bytes 12292
  0.7 21.7 %copy-start.3 = (bf16[2,4,256,256]{3,2,1,0:T(8,128)(2,1)S(1)}, bf16[2,4,256,256]{3,2,1,0:T(8,128)(2,1)}, u32[]{:S(2)}) copy-start(bf16[2,4,256,256]{3,2,1,0:T(8,128)(2,1)} %constant.14.clone.rest_6_) | copy-start | bytes 3145732
  0.7 21.7 %copy-start.4 = (bf16[2,4,256,256]{3,2,1,0:T(8,128)(2,1)S(1)}, bf16[2,4,256,256]{3,2,1,0:T(8,128)(2,1)}, u32[]{:S(2)}) copy-start(bf16[2,4,256,256]{3,2,1,0:T(8,128)(2,1)} %constant.15.clone.rest_7_) | copy-start | bytes 3145732
  10.0 19.1 %collective-permute-start.9 = (bf16[2,128,640]{2,1,0:T(8,128)(2,1)}, bf16[2,128,640]{2,1,0:T(8,128)(2,1)S(1)}, u32[]{:S(2)}, u32[]{:S(2)}) collective-permute-start(bf16[2,128,640]{2,1,0:T(8,128)(2,1)} %get-tuple-element.44), channel_id=1, source_target_pairs={{0,1},{1,0},{2,3},{3,2},{4,5},{5,4},{6,7},{7,6},{8,9},{9,8},{10,11... | collective-permute-start | bytes 983048 | tf_op jit(solution)/shard_map/ppermute | solution.py:633
  10.5 3.1 %collective-permute-start.6 = (bf16[2,128,256]{2,1,0:T(8,128)(2,1)}, bf16[2,128,256]{2,1,0:T(8,128)(2,1)S(1)}, u32[]{:S(2)}, u32[]{:S(2)}) collective-permute-start(bf16[2,128,256]{2,1,0:T(8,128)(2,1)} %get-tuple-element.41), channel_id=1, source_target_pairs={{0,1},{1,0},{2,3},{3,2},{4,5},{5,4},{6,7},{7,6},{8,9},{9,8},{10,11... | collective-permute-start | bytes 393224 | tf_op jit(solution)/shard_map/ppermute | solution.py:633
  10.6 4.8 %collective-permute-start = (bf16[2,128,256]{2,1,0:T(8,128)(2,1)}, bf16[2,128,256]{2,1,0:T(8,128)(2,1)S(1)}, u32[]{:S(2)}, u32[]{:S(2)}) collective-permute-start(bf16[2,128,256]{2,1,0:T(8,128)(2,1)} %get-tuple-element.33), channel_id=1, source_target_pairs={{0,1},{1,0},{2,3},{3,2},{4,5},{5,4},{6,7},{7,6},{8,9},{9,8},{10,11... | collective-permute-start | bytes 393224 | tf_op jit(solution)/shard_map/ppermute | solution.py:633
  11.0 7.1 %collective-permute-start.1 = (bf16[2,128,256]{2,1,0:T(8,128)(2,1)}, bf16[2,128,256]{2,1,0:T(8,128)(2,1)S(1)}, u32[]{:S(2)}, u32[]{:S(2)}) collective-permute-start(bf16[2,128,256]{2,1,0:T(8,128)(2,1)} %get-tuple-element.34), channel_id=1, source_target_pairs={{0,2},{1,3},{2,0},{3,1},{4,6},{5,7},{6,4},{7,5},{8,10},{9,11},{10,... | collective-permute-start | bytes 393224 | tf_op jit(solution)/shard_map/ppermute | solution.py:633
  13.6 6.9 %collective-permute-start.2 = (bf16[2,128,256]{2,1,0:T(8,128)(2,1)}, bf16[2,128,256]{2,1,0:T(8,128)(2,1)S(1)}, u32[]{:S(2)}, u32[]{:S(2)}) collective-permute-start(bf16[2,128,256]{2,1,0:T(8,128)(2,1)} %get-tuple-element.35), channel_id=1, source_target_pairs={{0,3},{1,2},{2,1},{3,0},{4,7},{5,6},{6,5},{7,4},{8,11},{9,10},{10,... | collective-permute-start | bytes 393224 | tf_op jit(solution)/shard_map/ppermute | solution.py:633
  13.7 11.2 %collective-permute-start.7 = (bf16[2,128,256]{2,1,0:T(8,128)(2,1)}, bf16[2,128,256]{2,1,0:T(8,128)(2,1)S(1)}, u32[]{:S(2)}, u32[]{:S(2)}) collective-permute-start(bf16[2,128,256]{2,1,0:T(8,128)(2,1)} %get-tuple-element.42), channel_id=1, source_target_pairs={{0,2},{1,3},{2,0},{3,1},{4,6},{5,7},{6,4},{7,5},{8,10},{9,11},{10,... | collective-permute-start | bytes 393224 | tf_op jit(solution)/shard_map/ppermute | solution.py:633
  15.4 11.1 %collective-permute-start.8 = (bf16[2,128,256]{2,1,0:T(8,128)(2,1)}, bf16[2,128,256]{2,1,0:T(8,128)(2,1)S(1)}, u32[]{:S(2)}, u32[]{:S(2)}) collective-permute-start(bf16[2,128,256]{2,1,0:T(8,128)(2,1)} %get-tuple-element.43), channel_id=1, source_target_pairs={{0,3},{1,2},{2,1},{3,0},{4,7},{5,6},{6,5},{7,4},{8,11},{9,10},{10,... | collective-permute-start | bytes 393224 | tf_op jit(solution)/shard_map/ppermute | solution.py:633
  18.1 28.3 %collective-permute-start.16 = (bf16[2,128,640]{2,1,0:T(8,128)(2,1)}, bf16[2,128,640]{2,1,0:T(8,128)(2,1)S(1)}, u32[]{:S(2)}, u32[]{:S(2)}) collective-permute-start(bf16[2,128,640]{2,1,0:T(8,128)(2,1)} %get-tuple-element.57), channel_id=1, source_target_pairs={{0,2},{1,3},{2,0},{3,1},{4,6},{5,7},{6,4},{7,5},{8,10},{9,11},{10,... | collective-permute-start | bytes 983048 | tf_op jit(solution)/shard_map/ppermute | solution.py:633
  20.5 25.9 %collective-permute-start.17 = (bf16[2,128,640]{2,1,0:T(8,128)(2,1)}, bf16[2,128,640]{2,1,0:T(8,128)(2,1)S(1)}, u32[]{:S(2)}, u32[]{:S(2)}) collective-permute-start(bf16[2,128,640]{2,1,0:T(8,128)(2,1)} %get-tuple-element.58), channel_id=1, source_target_pairs={{0,3},{1,2},{2,1},{3,0},{4,7},{5,6},{6,5},{7,4},{8,11},{9,10},{10,... | collective-permute-start | bytes 983048 | tf_op jit(solution)/shard_map/ppermute | solution.py:633
  22.3 0.9 %copy-start.9 = (bf16[2,128,256]{2,1,0:T(8,128)(2,1)S(1)}, bf16[2,128,256]{2,1,0:T(8,128)(2,1)}, u32[]{:S(2)}) copy-start(bf16[2,128,256]{2,1,0:T(8,128)(2,1)} %get-tuple-element.32.rest_0_) | copy-start | bytes 393220
  23.2 6.8 %copy-start.8 = (bf16[2,128,256]{2,1,0:T(8,128)(2,1)S(1)}, bf16[2,128,256]{2,1,0:T(8,128)(2,1)}, u32[]{:S(2)}) copy-start(bf16[2,128,256]{2,1,0:T(8,128)(2,1)} %get-tuple-element.45.rest_0_) | copy-start | bytes 393220
  24.9 6.8 %collective-permute-start.3 = (bf16[2,64,256]{2,1,0:T(8,128)(2,1)S(1)}, bf16[2,64,256]{2,1,0:T(8,128)(2,1)S(1)}, u32[]{:S(2)}, u32[]{:S(2)}) collective-permute-start(bf16[2,64,256]{2,1,0:T(8,128)(2,1)S(1)} %get-tuple-element.37), channel_id=1, source_target_pairs={{0,4},{4,0},{8,12},{12,8},{1,5},{5,1},{9,13},{13,9},{2,6},{6,2},{1... | collective-permute-start | bytes 196616 | tf_op jit(solution)/shard_map/ppermute | solution.py:633
  26.5 6.8 %collective-permute-start.4 = (bf16[2,64,256]{2,1,0:T(8,128)(2,1)S(1)}, bf16[2,64,256]{2,1,0:T(8,128)(2,1)S(1)}, u32[]{:S(2)}, u32[]{:S(2)}) collective-permute-start(bf16[2,64,256]{2,1,0:T(8,128)(2,1)S(1)} %get-tuple-element.38), channel_id=1, source_target_pairs={{0,8},{4,12},{8,0},{12,4},{1,9},{5,13},{9,1},{13,5},{2,10},{6,14},... | collective-permute-start | bytes 196616 | tf_op jit(solution)/shard_map/ppermute | solution.py:633
  29.1 6.1 %collective-permute-start.5 = (bf16[2,64,256]{2,1,0:T(8,128)(2,1)S(1)}, bf16[2,64,256]{2,1,0:T(8,128)(2,1)S(1)}, u32[]{:S(2)}, u32[]{:S(2)}) collective-permute-start(bf16[2,64,256]{2,1,0:T(8,128)(2,1)S(1)} %get-tuple-element.39), channel_id=1, source_target_pairs={{0,12},{4,8},{8,4},{12,0},{1,13},{5,9},{9,5},{13,1},{2,14},{6,10},... | collective-permute-start | bytes 196616 | tf_op jit(solution)/shard_map/ppermute | solution.py:633
  30.1 11.8 %copy-start.6 = (bf16[2,256,256]{2,1,0:T(8,128)(2,1)S(1)}, bf16[2,256,256]{2,1,0:T(8,128)(2,1)}, u32[]{:S(2)}) copy-start(bf16[2,256,256]{2,1,0:T(8,128)(2,1)} %constant.16.clone.rest_8_.rest_3_) | copy-start | bytes 786436
  30.1 11.8 %copy-start.7 = (bf16[128,192]{1,0:T(8,128)(2,1)S(1)}, bf16[128,192]{1,0:T(8,128)(2,1)}, u32[]{:S(2)}) copy-start(bf16[128,192]{1,0:T(8,128)(2,1)} %constant.18.clone.rest_9_.rest_4_.rest_6_) | copy-start | bytes 147460
  31.7 14.8 %copy-start.10 = (bf16[2,128,640]{2,1,0:T(8,128)(2,1)S(1)}, bf16[2,128,640]{2,1,0:T(8,128)(2,1)}, u32[]{:S(2)}) copy-start(bf16[2,128,640]{2,1,0:T(8,128)(2,1)} %get-tuple-element.55.rest_0_) | copy-start | bytes 983044
  31.7 7.1 %collective-permute-start.10 = (bf16[2,64,256]{2,1,0:T(8,128)(2,1)S(1)}, bf16[2,64,256]{2,1,0:T(8,128)(2,1)S(1)}, u32[]{:S(2)}, u32[]{:S(2)}) collective-permute-start(bf16[2,64,256]{2,1,0:T(8,128)(2,1)S(1)} %get-tuple-element.50), channel_id=1, source_target_pairs={{0,4},{4,0},{8,12},{12,8},{1,5},{5,1},{9,13},{13,9},{2,6},{6,2},{1... | collective-permute-start | bytes 196616 | tf_op jit(solution)/shard_map/ppermute | solution.py:633
  33.3 5.5 %collective-permute-start.11 = (bf16[2,64,256]{2,1,0:T(8,128)(2,1)S(1)}, bf16[2,64,256]{2,1,0:T(8,128)(2,1)S(1)}, u32[]{:S(2)}, u32[]{:S(2)}) collective-permute-start(bf16[2,64,256]{2,1,0:T(8,128)(2,1)S(1)} %get-tuple-element.51), channel_id=1, source_target_pairs={{0,8},{4,12},{8,0},{12,4},{1,9},{5,13},{9,1},{13,5},{2,10},{6,14},... | collective-permute-start | bytes 196616 | tf_op jit(solution)/shard_map/ppermute | solution.py:633
  35.2 6.7 %collective-permute-start.12 = (bf16[2,64,256]{2,1,0:T(8,128)(2,1)S(1)}, bf16[2,64,256]{2,1,0:T(8,128)(2,1)S(1)}, u32[]{:S(2)}, u32[]{:S(2)}) collective-permute-start(bf16[2,64,256]{2,1,0:T(8,128)(2,1)S(1)} %get-tuple-element.52), channel_id=1, source_target_pairs={{0,12},{4,8},{8,4},{12,0},{1,13},{5,9},{9,5},{13,1},{2,14},{6,10},... | collective-permute-start | bytes 196616 | tf_op jit(solution)/shard_map/ppermute | solution.py:633
  43.1 9.2 %collective-permute-start.14 = (bf16[2,64,512]{2,1,0:T(8,128)(2,1)S(1)}, bf16[2,64,512]{2,1,0:T(8,128)(2,1)S(1)}, u32[]{:S(2)}, u32[]{:S(2)}) collective-permute-start(bf16[2,64,512]{2,1,0:T(8,128)(2,1)S(1)} %primary_spectra.1.rest_0_), channel_id=1, source_target_pairs={{0,8},{4,12},{8,0},{12,4},{1,9},{5,13},{9,1},{13,5},{2,10},{6,14},... | collective-permute-start | bytes 393224 | tf_op jit(solution)/shard_map/ppermute | solution.py:633
  46.5 6.4 %copy-start.2 = (s32[1,2,4,8]{3,2,1,0:T(4,128)S(1)}, s32[1,2,4,8]{3,2,1,0:T(4,128)}, u32[]{:S(2)}) copy-start(s32[1,2,4,8]{3,2,1,0:T(4,128)} %param.20) | copy-start | bytes 772
  50.7 6.2 %collective-permute-start.13 = (bf16[2,64,512]{2,1,0:T(8,128)(2,1)S(1)}, bf16[2,64,512]{2,1,0:T(8,128)(2,1)S(1)}, u32[]{:S(2)}, u32[]{:S(2)}) collective-permute-start(bf16[2,64,512]{2,1,0:T(8,128)(2,1)S(1)} %primary_spectra.1.rest_0_), channel_id=1, source_target_pairs={{0,4},{4,0},{8,12},{12,8},{1,5},{5,1},{9,13},{13,9},{2,6},{6,2},{1... | collective-permute-start | bytes 393224 | tf_op jit(solution)/shard_map/ppermute | solution.py:633
  52.3 5.8 %collective-permute-start.15 = (bf16[2,64,512]{2,1,0:T(8,128)(2,1)S(1)}, bf16[2,64,512]{2,1,0:T(8,128)(2,1)S(1)}, u32[]{:S(2)}, u32[]{:S(2)}) collective-permute-start(bf16[2,64,512]{2,1,0:T(8,128)(2,1)S(1)} %collective-permute-done.14.rest_2_), channel_id=1, source_target_pairs={{0,4},{4,0},{8,12},{12,8},{1,5},{5,1},{9,13},{13,9},{2,6},{6,2},{1... | collective-permute-start | bytes 393224 | tf_op jit(solution)/shard_map/ppermute | solution.py:633
  52.8 5.3 %copy-start.5 = (bf16[2,256,256]{2,1,0:T(8,128)(2,1)S(1)}, bf16[2,256,256]{2,1,0:T(8,128)(2,1)}, u32[]{:S(2)}) copy-start(bf16[2,256,256]{2,1,0:T(8,128)(2,1)} %constant.17.clone.rest_5_) | copy-start | bytes 786436

commit v2 on v1

--- a/solution.py
+++ b/solution.py
@@ -147,12 +147,14 @@
     lane = lax.broadcasted_iota(jnp.int32, (sub, LANES), 1)
     for block in range(rows // sub):
         span = slice(block * sub, (block + 1) * sub)
+        odd = block * sub % 16
+        whole = slice(block * sub - odd, block * sub - odd + 16)
         keep = base + block * sub + lax.broadcasted_iota(jnp.int32, (sub, LANES), 0) < valid[0]
         re, im = [], []
         for a in range(count):
             at = slice(a * LANES, (a + 1) * LANES)
-            re.append(jnp.where(keep, x_ref[0, span, at].astype(F32), 0.0))
-            im.append(jnp.where(keep, x_ref[1, span, at].astype(F32), 0.0))
+            re.append(jnp.where(keep, x_ref[0, whole, at].astype(F32)[odd : odd + sub], 0.0))
+            im.append(jnp.where(keep, x_ref[1, whole, at].astype(F32)[odd : odd + sub], 0.0))
         re, im = fft_list(re, im, -1)
         mixed = []
         for c in range(count):
@@ -650,10 +652,9 @@
         for c in range(len(chunks)):
             for k in far_first(devices):
                 inner[c][k].append(trade(mine[k][c], k, "lines"))
-    outer = {k: trade(outer[k], k, "lines") for k in far_first(devices)}
-    outer = [outer[k] for k in range(devices)]
+    near = trade(outer[1], 1, "lines")
     if len(inner) > 1:
-        inner[-1], outer[1] = lax.optimization_barrier((inner[-1], outer[1]))
+        inner[-1], near = lax.optimization_barrier((inner[-1], near))
     images, primaries = [], []
     for c in range(len(chunks)):
         image, *shares = focus_inner(
@@ -667,6 +668,9 @@
             mine = lax.axis_index("acq") == reference[0]
             shares = [lax.psum(jnp.where(mine, shares[0], 0).astype(BF16), "acq")]
         primaries.append(shares)
+    far, _ = lax.optimization_barrier((list(outer[2:]), images[0]))
+    far = [trade(block, k + 2, "lines") for k, block in enumerate(far)]
+    outer = [outer[0], near, *far]
     outer = focus_outer(outer, slope, centre, matrices)
     spectrum = window_spectra(images, outer, patch, offsets[0], chunks)
     shares = [primary_spectra(reference, primaries, patch)]

time: 60.3 us -> 58.8 us (0.975)
  starting transfers between devices: 24.2 us -> 20.4 us
  waiting for transfers between devices: 9.61 us -> 11.8 us
    ppermute x18, starting transfers between devices: 24.2 us -> 20.4 us  [trade(): lax.ppermute(block, axis, [(i, i ^ k) for i in range(lax.axis_size(axis))])]
    ppermute x18, waiting for transfers between devices: 9.61 us -> 11.8 us  [trade(): lax.ppermute(block, axis, [(i, i ^ k) for i in range(lax.axis_size(axis))])]
  transfers between devices with their start and end apart: 18 -> 18, of which waited for: 7 -> 8; matrix products, arithmetic and copies ran while one was open for 0% -> 0% of each run, Pallas kernels for 21% -> 22%
where the time goes in v2:
time: 58.8 us; the launch traced here: 58.6 us
  Pallas kernels  24 us (41%)
  starting transfers between devices  20.4 us (35%)
  waiting for transfers between devices  11.8 us (20%)
  between operations  1.47 us (2%)
  local copies, waits for them, and re-layouts  0.95 us (2%)
    ppermute x18, starting transfers between devices, trade(): lax.ppermute(block, axis, [(i, i ^ k) for i in range(lax.axis_size(axis))])  20.4 us
    ppermute x18, waiting for transfers between devices, trade(): lax.ppermute(block, axis, [(i, i ^ k) for i in range(lax.axis_size(axis))])  11.8 us
    pallas_call x1, Pallas kernels, compress(): pl.pallas_call(functools.partial(range_kernel, devices=devices, first=(pa...  9.3 us
    pallas_call x1, Pallas kernels, focus_outer(): pl.pallas_call(functools.partial(outer_kernel, devices=devices), in_specs...  4.25 us
    pallas_call x1, Pallas kernels, window_spectra(): pl.pallas_call(functools.partial(window_kernel, chunks=chunks), in_specs=...  4.02 us
    pallas_call x2, Pallas kernels, focus_inner(): pl.pallas_call(functools.partial(inner_kernel, devices=devices, row_parts...  3.16 us
    pallas_call x1, Pallas kernels, correlate(): pl.pallas_call(functools.partial(correlate_kernel, parts=parts), in_specs...  2.03 us
    pallas_call x1, Pallas kernels, primary_spectra(): pl.pallas_call(functools.partial(primary_kernel, parts=len(shares[0])), i...  1.22 us
  transfers between devices with their start and end apart: 18, of which 8 were waited for; matrix products, arithmetic and copies ran while one was open for 0% of the time, Pallas kernels for 22%

profile of v2, /device:TPU:0, one launch (start us, length us, event | category | flops | bytes accessed | tf_op | source)
XLA Modules:
  0.0 58.6 jit_solution(13173984437145991498)
XLA Ops:
  0.7 0.0 copy-start.3
  0.7 0.0 copy-start.4
  0.7 9.3 %range_compress.1 = (bf16[2,128,256]{2,1,0:T(8,128)(2,1)}, bf16[2,128,256]{2,1,0:T(8,128)(2,1)}, bf16[2,128,256]{2,1,0:T(8,128)(2,1)}, bf16[2,128,256]{2,1,0:T(8...) custom-call(s32[1]{0:T(128)S(6)} %copy.15.valid, ...), custom_call_target="tpu_custom_call" | custom-call | flops 8999999488 | bytes 31500000 | tf_op jit(solution)/shard_map/range_compress/pallas_call | solution.py:232
  10.0 0.5 collective-permute-start.9
  10.5 0.1 collective-permute-start
  10.6 2.9 %collective-permute-start.1 = (bf16[2,128,256]{2,1,0:T(8,128)(2,1)}, bf16[2,128,256]{2,1,0:T(8,128)(2,1)S(1)}, u32[]{:S(2)}, u32[]{:S(2)}) collective-permute-start(bf16[2,128,256]{2,1,0:T(8,128)(2,1)} %get-tuple-element.36), channel_id=1, source_target_pairs={{0,2},{1,3},{2,0},{3,1},{4,6},{5,7},{6,4},{7,5},{8,10},{9,11},{10,... | collective-permute-start | bytes 393224 | tf_op jit(solution)/shard_map/ppermute | solution.py:635
  13.5 0.0 collective-permute-start.2
  13.5 0.1 collective-permute-start.6
  13.7 0.0 collective-permute-done.rest_1_
  13.7 2.0 %collective-permute-start.7 = (bf16[2,128,256]{2,1,0:T(8,128)(2,1)}, bf16[2,128,256]{2,1,0:T(8,128)(2,1)S(1)}, u32[]{:S(2)}, u32[]{:S(2)}) collective-permute-start(bf16[2,128,256]{2,1,0:T(8,128)(2,1)} %get-tuple-element.44), channel_id=1, source_target_pairs={{0,2},{1,3},{2,0},{3,1},{4,6},{5,7},{6,4},{7,5},{8,10},{9,11},{10,... | collective-permute-start | bytes 393224 | tf_op jit(solution)/shard_map/ppermute | solution.py:635
  15.7 2.4 %collective-permute-done.1.rest_2_ = bf16[2,128,256]{2,1,0:T(8,128)(2,1)S(1)} collective-permute-done((bf16[2,128,256]{2,1,0:T(8,128)(2,1)}, bf16[2,128,256]{2,1,0:T(8,128)(2,1)S(1)}, u32[]{:S(2)}, u32[]{:S(2)}) %collective-permute-start.1) | collective-permute-done | bytes 131104 | tf_op jit(solution)/shard_map/ppermute | solution.py:635
  18.0 0.0 collective-permute-start.8
  18.1 2.5 %collective-permute-done.2.rest_3_ = bf16[2,128,256]{2,1,0:T(8,128)(2,1)S(1)} collective-permute-done((bf16[2,128,256]{2,1,0:T(8,128)(2,1)}, bf16[2,128,256]{2,1,0:T(8,128)(2,1)S(1)}, u32[]{:S(2)}, u32[]{:S(2)}) %collective-permute-start.2) | collective-permute-done | bytes 131104 | tf_op jit(solution)/shard_map/ppermute | solution.py:635
  20.5 0.9 %copy-done.9 = bf16[2,128,256]{2,1,0:T(8,128)(2,1)S(1)} copy-done((bf16[2,128,256]{2,1,0:T(8,128)(2,1)S(1)}, bf16[2,128,256]{2,1,0:T(8,128)(2,1)}, u32[]{:S(2)}) %copy-start.9) | copy-done | bytes 131096
  21.4 1.6 %focus_inner.2 = (bf16[2,512,256]{2,1,0:T(8,128)(2,1)S(1)}, bf16[2,64,256]{2,1,0:T(8,128)(2,1)S(1)}, bf16[2,64,256]{2,1,0:T(8,128)(2,1)S(1)}, bf16[2,64,256]{2,1,0:T(8,128)(2,1)S(1)}, bf16[2,64,256]{2,1,0:T(8,128)(2,1)S(1)}) custom-call(bf16[2,128,256]{2,1,0:T(8,128)(2,1)S(1)} %copy-done.9, bf16[2,128,256]{2,1,0:T(8,128)(2,1)S(1)} %collective-permute-done.rest_1_, ...), custom_call_target="tpu_custom_call" | custom-call | flops 1600000000 | bytes 5600000 | tf_op jit(solution)/shard_map/focus_inner/pallas_call | solution.py:362
  23.0 0.7 %collective-permute-start.16 = (bf16[2,128,640]{2,1,0:T(8,128)(2,1)S(1)}, bf16[2,128,640]{2,1,0:T(8,128)(2,1)S(1)}, u32[]{:S(2)}, u32[]{:S(2)}) collective-permute-start(bf16[2,128,640]{2,1,0:T(8,128)(2,1)S(1)} %copy-done.12), channel_id=1, source_target_pairs={{0,2},{1,3},{2,0},{3,1},{4,6},{5,7},{6,4},{7,5},{8,10},{9,11},{10,... | collective-permute-start | bytes 983048 | tf_op jit(solution)/shard_map/ppermute | solution.py:635
  23.7 0.0 collective-permute-done.6.rest_1_
  23.7 1.3 %collective-permute-start.17 = (bf16[2,128,640]{2,1,0:T(8,128)(2,1)S(1)}, bf16[2,128,640]{2,1,0:T(8,128)(2,1)S(1)}, u32[]{:S(2)}, u32[]{:S(2)}) collective-permute-start(bf16[2,128,640]{2,1,0:T(8,128)(2,1)S(1)} %copy-done.11), channel_id=1, source_target_pairs={{0,3},{1,2},{2,1},{3,0},{4,7},{5,6},{6,5},{7,4},{8,11},{9,10},{10,... | collective-permute-start | bytes 983048 | tf_op jit(solution)/shard_map/ppermute | solution.py:635
  25.0 0.0 collective-permute-done.7.rest_2_
  25.0 1.8 %collective-permute-start.3 = (bf16[2,64,256]{2,1,0:T(8,128)(2,1)S(1)}, bf16[2,64,256]{2,1,0:T(8,128)(2,1)S(1)}, u32[]{:S(2)}, u32[]{:S(2)}) collective-permute-start(bf16[2,64,256]{2,1,0:T(8,128)(2,1)S(1)} %get-tuple-element.39), channel_id=1, source_target_pairs={{0,4},{4,0},{8,12},{12,8},{1,5},{5,1},{9,13},{13,9},{2,6},{6,2},{1... | collective-permute-start | bytes 196616 | tf_op jit(solution)/shard_map/ppermute | solution.py:635
  26.8 0.0 collective-permute-done.8.rest_3_
  26.8 2.6 %collective-permute-start.4 = (bf16[2,64,256]{2,1,0:T(8,128)(2,1)S(1)}, bf16[2,64,256]{2,1,0:T(8,128)(2,1)S(1)}, u32[]{:S(2)}, u32[]{:S(2)}) collective-permute-start(bf16[2,64,256]{2,1,0:T(8,128)(2,1)S(1)} %get-tuple-element.40), channel_id=1, source_target_pairs={{0,8},{4,12},{8,0},{12,4},{1,9},{5,13},{9,1},{13,5},{2,10},{6,14},... | collective-permute-start | bytes 196616 | tf_op jit(solution)/shard_map/ppermute | solution.py:635
  29.4 0.0 collective-permute-done.9.rest_1_
  29.4 0.1 collective-permute-start.5
  29.4 1.6 %focus_inner.3 = (bf16[2,512,256]{2,1,0:T(8,128)(2,1)S(1)}, bf16[2,64,256]{2,1,0:T(8,128)(2,1)S(1)}, bf16[2,64,256]{2,1,0:T(8,128)(2,1)S(1)}, bf16[2,64,256]{2,1,0:T(8,128)(2,1)S(1)}, bf16[2,64,256]{2,1,0:T(8,128)(2,1)S(1)}) custom-call(bf16[2,128,256]{2,1,0:T(8,128)(2,1)S(1)} %copy-done.8, bf16[2,128,256]{2,1,0:T(8,128)(2,1)S(1)} %collective-permute-done.6.rest_1_, ...), custom_call_target="tpu_custom_call" | custom-call | flops 1600000000 | bytes 5600000 | tf_op jit(solution)/shard_map/focus_inner/pallas_call | solution.py:362
  31.0 0.0 copy-start.10
  31.0 0.0 collective-permute-done.3.rest_1_
  31.0 0.9 %collective-permute-start.10 = (bf16[2,64,256]{2,1,0:T(8,128)(2,1)S(1)}, bf16[2,64,256]{2,1,0:T(8,128)(2,1)S(1)}, u32[]{:S(2)}, u32[]{:S(2)}) collective-permute-start(bf16[2,64,256]{2,1,0:T(8,128)(2,1)S(1)} %get-tuple-element.52), channel_id=1, source_target_pairs={{0,4},{4,0},{8,12},{12,8},{1,5},{5,1},{9,13},{13,9},{2,6},{6,2},{1... | collective-permute-start | bytes 196616 | tf_op jit(solution)/shard_map/ppermute | solution.py:635
  32.0 1.4 %collective-permute-done.4.rest_2_ = bf16[2,64,256]{2,1,0:T(8,128)(2,1)S(1)} collective-permute-done((bf16[2,64,256]{2,1,0:T(8,128)(2,1)S(1)}, bf16[2,64,256]{2,1,0:T(8,128)(2,1)S(1)}, u32[]{:S(2)}, u32[]{:S(2)}) %collective-permute-start.4) | collective-permute-done | bytes 65568 | tf_op jit(solution)/shard_map/ppermute | solution.py:635
  33.3 2.1 %collective-permute-start.11 = (bf16[2,64,256]{2,1,0:T(8,128)(2,1)S(1)}, bf16[2,64,256]{2,1,0:T(8,128)(2,1)S(1)}, u32[]{:S(2)}, u32[]{:S(2)}) collective-permute-start(bf16[2,64,256]{2,1,0:T(8,128)(2,1)S(1)} %get-tuple-element.53), channel_id=1, source_target_pairs={{0,8},{4,12},{8,0},{12,4},{1,9},{5,13},{9,1},{13,5},{2,10},{6,14},... | collective-permute-start | bytes 196616 | tf_op jit(solution)/shard_map/ppermute | solution.py:635
  35.4 0.5 collective-permute-done.5.rest_3_
  35.9 1.9 %collective-permute-start.12 = (bf16[2,64,256]{2,1,0:T(8,128)(2,1)S(1)}, bf16[2,64,256]{2,1,0:T(8,128)(2,1)S(1)}, u32[]{:S(2)}, u32[]{:S(2)}) collective-permute-start(bf16[2,64,256]{2,1,0:T(8,128)(2,1)S(1)} %get-tuple-element.54), channel_id=1, source_target_pairs={{0,12},{4,8},{8,4},{12,0},{1,13},{5,9},{9,5},{13,1},{2,14},{6,10},... | collective-permute-start | bytes 196616 | tf_op jit(solution)/shard_map/ppermute | solution.py:635
  38.5 0.0 collective-permute-done.10.rest_5_
  38.5 2.5 %collective-permute-done.11.rest_6_ = bf16[2,64,256]{2,1,0:T(8,128)(2,1)S(1)} collective-permute-done((bf16[2,64,256]{2,1,0:T(8,128)(2,1)S(1)}, bf16[2,64,256]{2,1,0:T(8,128)(2,1)S(1)}, u32[]{:S(2)}, u32[]{:S(2)}) %collective-permute-start.11) | collective-permute-done | bytes 65568 | tf_op jit(solution)/shard_map/ppermute | solution.py:635
  41.0 1.0 %collective-permute-done.12.rest_7_ = bf16[2,64,256]{2,1,0:T(8,128)(2,1)S(1)} collective-permute-done((bf16[2,64,256]{2,1,0:T(8,128)(2,1)S(1)}, bf16[2,64,256]{2,1,0:T(8,128)(2,1)S(1)}, u32[]{:S(2)}, u32[]{:S(2)}) %collective-permute-start.12) | collective-permute-done | bytes 65568 | tf_op jit(solution)/shard_map/ppermute | solution.py:635
  42.0 1.2 %primary_spectra.1.rest_0_ = bf16[2,64,512]{2,1,0:T(8,128)(2,1)S(1)} custom-call(s32[1]{0:T(128)S(6)} %copy.16.reference, bf16[2,64,256]{2,1,0:T(8,128)(2,1)S(1)} %get-tuple-element.38.rest_0_, bf16[2,64,256]{2,1,0:T(8,128)(2,1)S(1)} %collective-permute-done.3.rest_1_, bf16[2,64,256]{2,1,0:T(8,128)(2,1)S(1)} %collective-permute-done.4.rest_2_, ...), custom_call_target="tpu_custom_call" | custom-call | flops 1000000000 | bytes 3500000 | tf_op jit(solution)/shard_map/primary_spectra/pallas_call | solution.py:576
  43.3 2.3 %collective-permute-start.14 = (bf16[2,64,512]{2,1,0:T(8,128)(2,1)S(1)}, bf16[2,64,512]{2,1,0:T(8,128)(2,1)S(1)}, u32[]{:S(2)}, u32[]{:S(2)}) collective-permute-start(bf16[2,64,512]{2,1,0:T(8,128)(2,1)S(1)} %primary_spectra.1.rest_0_), channel_id=1, source_target_pairs={{0,8},{4,12},{8,0},{12,4},{1,9},{5,13},{9,1},{13,5},{2,10},{6,14},... | collective-permute-start | bytes 393224 | tf_op jit(solution)/shard_map/ppermute | solution.py:635
  45.6 0.8 %collective-permute-start.13 = (bf16[2,64,512]{2,1,0:T(8,128)(2,1)S(1)}, bf16[2,64,512]{2,1,0:T(8,128)(2,1)S(1)}, u32[]{:S(2)}, u32[]{:S(2)}) collective-permute-start(bf16[2,64,512]{2,1,0:T(8,128)(2,1)S(1)} %primary_spectra.1.rest_0_), channel_id=1, source_target_pairs={{0,4},{4,0},{8,12},{12,8},{1,5},{5,1},{9,13},{13,9},{2,6},{6,2},{1... | collective-permute-start | bytes 393224 | tf_op jit(solution)/shard_map/ppermute | solution.py:635
  46.4 0.0 collective-permute-done.16.rest_2_
  46.4 0.0 collective-permute-done.17.rest_3_
  46.4 0.0 copy-start.2
  46.4 4.2 %focus_outer.1.rest_2_ = bf16[2,512,640]{2,1,0:T(8,128)(2,1)S(1)} custom-call(bf16[2,128,640]{2,1,0:T(8,128)(2,1)S(1)} %copy-done.10, bf16[2,128,640]{2,1,0:T(8,128)(2,1)S(1)} %collective-permute-done.9.rest_1_, bf16[2,128,640]{2,1,0:T(8,128)(2,1)S(1)} %collective-permute-done.16.rest_2_, bf16[2,128,640]{2,1,0:T(8,128)(2,1)S(1)} %collective-permute-done.17.rest_3_, ...), custom_call_target="tpu_custom_call" | custom-call | flops 4000000000 | bytes 14000000 | tf_op jit(solution)/shard_map/focus_outer/pallas_call | solution.py:425
  50.6 1.0 %collective-permute-done.14.rest_2_ = bf16[2,64,512]{2,1,0:T(8,128)(2,1)S(1)} collective-permute-done((bf16[2,64,512]{2,1,0:T(8,128)(2,1)S(1)}, bf16[2,64,512]{2,1,0:T(8,128)(2,1)S(1)}, u32[]{:S(2)}, u32[]{:S(2)}) %collective-permute-start.14) | collective-permute-done | bytes 131104 | tf_op jit(solution)/shard_map/ppermute | solution.py:635
  51.6 0.3 collective-permute-start.15
  52.0 4.0 %window_spectra.1.rest_4_ = f32[2,16,64,128]{3,2,1,0:T(8,128)S(1)} custom-call(s32[2,4,8]{2,1,0:T(4,128)S(1)} %bitcast.3, bf16[2,512,256]{2,1,0:T(8,128)(2,1)S(1)} %get-tuple-element.55.rest_0_, bf16[2,512,256]{2,1,0:T(8,128)(2,1)S(1)} %get-tuple-element.56.rest_1_, bf16[2,512,640]{2,1,0:T(8,128)(2,1)S(1)} %focus_outer.1.rest_2_, ...), custom_call_target="tpu_custom_call" | custom-call | flops 4000000000 | bytes 14000000 | tf_op jit(solution)/shard_map/window_spectra/pallas_call | solution.py:531
  56.0 0.0 collective-permute-done.13.rest_1_
  56.0 0.6 collective-permute-done.15.rest_3_
  56.6 2.0 %correlate.1 = f32[1,2,256,512]{3,2,1,0:T(8,128)} custom-call(bf16[2,64,512]{2,1,0:T(8,128)(2,1)S(1)} %primary_spectra.1.rest_0_, bf16[2,64,512]{2,1,0:T(8,128)(2,1)S(1)} %collective-permute-done.13.rest_1_, bf16[2,64,512]{2,1,0:T(8,128)(2,1)S(1)} %collective-permute-done.14.rest_2_, bf16[2,64,512]{2,1,0:T(8,128)(2,1)S(1)} %collective-permute-done.15.rest_3_, ...), custom_call_target="tpu_custom_call" | custom-call | flops 2000000000 | bytes 7000000 | tf_op jit(solution)/shard_map/correlate/pallas_call | solution.py:617
  (21 shorter events, 0.0 us)
Async XLA Ops:
  0.7 19.9 %copy-start = (f32[1,1024]{1,0:T(1,128)S(1)}, f32[1,1024]{1,0:T(1,128)}, u32[]{:S(2)}) copy-start(f32[1,1024]{1,0:T(1,128)} %rest_4_.6) | copy-start | bytes 12292
  0.7 19.9 %copy-start.1 = (f32[1,1024]{1,0:T(1,128)S(1)}, f32[1,1024]{1,0:T(1,128)}, u32[]{:S(2)}) copy-start(f32[1,1024]{1,0:T(1,128)} %rest_5_.6) | copy-start | bytes 12292
  0.7 19.9 %copy-start.3 = (bf16[2,4,256,256]{3,2,1,0:T(8,128)(2,1)S(1)}, bf16[2,4,256,256]{3,2,1,0:T(8,128)(2,1)}, u32[]{:S(2)}) copy-start(bf16[2,4,256,256]{3,2,1,0:T(8,128)(2,1)} %constant.14.clone.rest_6_) | copy-start | bytes 3145732
  0.7 19.8 %copy-start.4 = (bf16[2,4,256,256]{3,2,1,0:T(8,128)(2,1)S(1)}, bf16[2,4,256,256]{3,2,1,0:T(8,128)(2,1)}, u32[]{:S(2)}) copy-start(bf16[2,4,256,256]{3,2,1,0:T(8,128)(2,1)} %constant.15.clone.rest_7_) | copy-start | bytes 3145732
  10.0 19.4 %collective-permute-start.9 = (bf16[2,128,640]{2,1,0:T(8,128)(2,1)}, bf16[2,128,640]{2,1,0:T(8,128)(2,1)S(1)}, u32[]{:S(2)}, u32[]{:S(2)}) collective-permute-start(bf16[2,128,640]{2,1,0:T(8,128)(2,1)} %get-tuple-element.46), channel_id=1, source_target_pairs={{0,1},{1,0},{2,3},{3,2},{4,5},{5,4},{6,7},{7,6},{8,9},{9,8},{10,11... | collective-permute-start | bytes 983048 | tf_op jit(solution)/shard_map/ppermute | solution.py:635
  10.5 3.1 %collective-permute-start = (bf16[2,128,256]{2,1,0:T(8,128)(2,1)}, bf16[2,128,256]{2,1,0:T(8,128)(2,1)S(1)}, u32[]{:S(2)}, u32[]{:S(2)}) collective-permute-start(bf16[2,128,256]{2,1,0:T(8,128)(2,1)} %get-tuple-element.35), channel_id=1, source_target_pairs={{0,1},{1,0},{2,3},{3,2},{4,5},{5,4},{6,7},{7,6},{8,9},{9,8},{10,11... | collective-permute-start | bytes 393224 | tf_op jit(solution)/shard_map/ppermute | solution.py:635
  10.6 7.4 %collective-permute-start.1 = (bf16[2,128,256]{2,1,0:T(8,128)(2,1)}, bf16[2,128,256]{2,1,0:T(8,128)(2,1)S(1)}, u32[]{:S(2)}, u32[]{:S(2)}) collective-permute-start(bf16[2,128,256]{2,1,0:T(8,128)(2,1)} %get-tuple-element.36), channel_id=1, source_target_pairs={{0,2},{1,3},{2,0},{3,1},{4,6},{5,7},{6,4},{7,5},{8,10},{9,11},{10,... | collective-permute-start | bytes 393224 | tf_op jit(solution)/shard_map/ppermute | solution.py:635
  13.5 7.0 %collective-permute-start.2 = (bf16[2,128,256]{2,1,0:T(8,128)(2,1)}, bf16[2,128,256]{2,1,0:T(8,128)(2,1)S(1)}, u32[]{:S(2)}, u32[]{:S(2)}) collective-permute-start(bf16[2,128,256]{2,1,0:T(8,128)(2,1)} %get-tuple-element.37), channel_id=1, source_target_pairs={{0,3},{1,2},{2,1},{3,0},{4,7},{5,6},{6,5},{7,4},{8,11},{9,10},{10,... | collective-permute-start | bytes 393224 | tf_op jit(solution)/shard_map/ppermute | solution.py:635
  13.5 10.2 %collective-permute-start.6 = (bf16[2,128,256]{2,1,0:T(8,128)(2,1)}, bf16[2,128,256]{2,1,0:T(8,128)(2,1)S(1)}, u32[]{:S(2)}, u32[]{:S(2)}) collective-permute-start(bf16[2,128,256]{2,1,0:T(8,128)(2,1)} %get-tuple-element.43), channel_id=1, source_target_pairs={{0,1},{1,0},{2,3},{3,2},{4,5},{5,4},{6,7},{7,6},{8,9},{9,8},{10,11... | collective-permute-start | bytes 393224 | tf_op jit(solution)/shard_map/ppermute | solution.py:635
  13.7 11.3 %collective-permute-start.7 = (bf16[2,128,256]{2,1,0:T(8,128)(2,1)}, bf16[2,128,256]{2,1,0:T(8,128)(2,1)S(1)}, u32[]{:S(2)}, u32[]{:S(2)}) collective-permute-start(bf16[2,128,256]{2,1,0:T(8,128)(2,1)} %get-tuple-element.44), channel_id=1, source_target_pairs={{0,2},{1,3},{2,0},{3,1},{4,6},{5,7},{6,4},{7,5},{8,10},{9,11},{10,... | collective-permute-start | bytes 393224 | tf_op jit(solution)/shard_map/ppermute | solution.py:635
  18.0 8.8 %collective-permute-start.8 = (bf16[2,128,256]{2,1,0:T(8,128)(2,1)}, bf16[2,128,256]{2,1,0:T(8,128)(2,1)S(1)}, u32[]{:S(2)}, u32[]{:S(2)}) collective-permute-start(bf16[2,128,256]{2,1,0:T(8,128)(2,1)} %get-tuple-element.45), channel_id=1, source_target_pairs={{0,3},{1,2},{2,1},{3,0},{4,7},{5,6},{6,5},{7,4},{8,11},{9,10},{10,... | collective-permute-start | bytes 393224 | tf_op jit(solution)/shard_map/ppermute | solution.py:635
  20.5 0.9 %copy-start.9 = (bf16[2,128,256]{2,1,0:T(8,128)(2,1)S(1)}, bf16[2,128,256]{2,1,0:T(8,128)(2,1)}, u32[]{:S(2)}) copy-start(bf16[2,128,256]{2,1,0:T(8,128)(2,1)} %get-tuple-element.34.rest_0_) | copy-start | bytes 393220
  21.4 1.6 %copy-start.12 = (bf16[2,128,640]{2,1,0:T(8,128)(2,1)S(1)}, bf16[2,128,640]{2,1,0:T(8,128)(2,1)}, u32[]{:S(2)}) copy-start(bf16[2,128,640]{2,1,0:T(8,128)(2,1)} %get-tuple-element.61) | copy-start | bytes 983044
  21.4 2.3 %copy-start.11 = (bf16[2,128,640]{2,1,0:T(8,128)(2,1)S(1)}, bf16[2,128,640]{2,1,0:T(8,128)(2,1)}, u32[]{:S(2)}) copy-start(bf16[2,128,640]{2,1,0:T(8,128)(2,1)} %get-tuple-element.62) | copy-start | bytes 983044
  21.4 8.0 %copy-start.8 = (bf16[2,128,256]{2,1,0:T(8,128)(2,1)S(1)}, bf16[2,128,256]{2,1,0:T(8,128)(2,1)}, u32[]{:S(2)}) copy-start(bf16[2,128,256]{2,1,0:T(8,128)(2,1)} %get-tuple-element.47.rest_0_) | copy-start | bytes 393220
  23.0 23.3 %collective-permute-start.16 = (bf16[2,128,640]{2,1,0:T(8,128)(2,1)S(1)}, bf16[2,128,640]{2,1,0:T(8,128)(2,1)S(1)}, u32[]{:S(2)}, u32[]{:S(2)}) collective-permute-start(bf16[2,128,640]{2,1,0:T(8,128)(2,1)S(1)} %copy-done.12), channel_id=1, source_target_pairs={{0,2},{1,3},{2,0},{3,1},{4,6},{5,7},{6,4},{7,5},{8,10},{9,11},{10,... | collective-permute-start | bytes 983048 | tf_op jit(solution)/shard_map/ppermute | solution.py:635
  23.7 22.6 %collective-permute-start.17 = (bf16[2,128,640]{2,1,0:T(8,128)(2,1)S(1)}, bf16[2,128,640]{2,1,0:T(8,128)(2,1)S(1)}, u32[]{:S(2)}, u32[]{:S(2)}) collective-permute-start(bf16[2,128,640]{2,1,0:T(8,128)(2,1)S(1)} %copy-done.11), channel_id=1, source_target_pairs={{0,3},{1,2},{2,1},{3,0},{4,7},{5,6},{6,5},{7,4},{8,11},{9,10},{10,... | collective-permute-start | bytes 983048 | tf_op jit(solution)/shard_map/ppermute | solution.py:635
  25.0 6.0 %collective-permute-start.3 = (bf16[2,64,256]{2,1,0:T(8,128)(2,1)S(1)}, bf16[2,64,256]{2,1,0:T(8,128)(2,1)S(1)}, u32[]{:S(2)}, u32[]{:S(2)}) collective-permute-start(bf16[2,64,256]{2,1,0:T(8,128)(2,1)S(1)} %get-tuple-element.39), channel_id=1, source_target_pairs={{0,4},{4,0},{8,12},{12,8},{1,5},{5,1},{9,13},{13,9},{2,6},{6,2},{1... | collective-permute-start | bytes 196616 | tf_op jit(solution)/shard_map/ppermute | solution.py:635
  26.8 6.5 %collective-permute-start.4 = (bf16[2,64,256]{2,1,0:T(8,128)(2,1)S(1)}, bf16[2,64,256]{2,1,0:T(8,128)(2,1)S(1)}, u32[]{:S(2)}, u32[]{:S(2)}) collective-permute-start(bf16[2,64,256]{2,1,0:T(8,128)(2,1)S(1)} %get-tuple-element.40), channel_id=1, source_target_pairs={{0,8},{4,12},{8,0},{12,4},{1,9},{5,13},{9,1},{13,5},{2,10},{6,14},... | collective-permute-start | bytes 196616 | tf_op jit(solution)/shard_map/ppermute | solution.py:635
  29.4 6.5 %collective-permute-start.5 = (bf16[2,64,256]{2,1,0:T(8,128)(2,1)S(1)}, bf16[2,64,256]{2,1,0:T(8,128)(2,1)S(1)}, u32[]{:S(2)}, u32[]{:S(2)}) collective-permute-start(bf16[2,64,256]{2,1,0:T(8,128)(2,1)S(1)} %get-tuple-element.41), channel_id=1, source_target_pairs={{0,12},{4,8},{8,4},{12,0},{1,13},{5,9},{9,5},{13,1},{2,14},{6,10},... | collective-permute-start | bytes 196616 | tf_op jit(solution)/shard_map/ppermute | solution.py:635
  29.4 12.6 %copy-start.6 = (bf16[2,256,256]{2,1,0:T(8,128)(2,1)S(1)}, bf16[2,256,256]{2,1,0:T(8,128)(2,1)}, u32[]{:S(2)}) copy-start(bf16[2,256,256]{2,1,0:T(8,128)(2,1)} %constant.16.clone.rest_8_.rest_3_) | copy-start | bytes 786436
  29.4 12.6 %copy-start.7 = (bf16[128,192]{1,0:T(8,128)(2,1)S(1)}, bf16[128,192]{1,0:T(8,128)(2,1)}, u32[]{:S(2)}) copy-start(bf16[128,192]{1,0:T(8,128)(2,1)} %constant.18.clone.rest_9_.rest_4_.rest_6_) | copy-start | bytes 147460
  31.0 15.4 %copy-start.10 = (bf16[2,128,640]{2,1,0:T(8,128)(2,1)S(1)}, bf16[2,128,640]{2,1,0:T(8,128)(2,1)}, u32[]{:S(2)}) copy-start(bf16[2,128,640]{2,1,0:T(8,128)(2,1)} %get-tuple-element.57.rest_0_) | copy-start | bytes 983044
  31.0 7.4 %collective-permute-start.10 = (bf16[2,64,256]{2,1,0:T(8,128)(2,1)S(1)}, bf16[2,64,256]{2,1,0:T(8,128)(2,1)S(1)}, u32[]{:S(2)}, u32[]{:S(2)}) collective-permute-start(bf16[2,64,256]{2,1,0:T(8,128)(2,1)S(1)} %get-tuple-element.52), channel_id=1, source_target_pairs={{0,4},{4,0},{8,12},{12,8},{1,5},{5,1},{9,13},{13,9},{2,6},{6,2},{1... | collective-permute-start | bytes 196616 | tf_op jit(solution)/shard_map/ppermute | solution.py:635
  33.3 7.7 %collective-permute-start.11 = (bf16[2,64,256]{2,1,0:T(8,128)(2,1)S(1)}, bf16[2,64,256]{2,1,0:T(8,128)(2,1)S(1)}, u32[]{:S(2)}, u32[]{:S(2)}) collective-permute-start(bf16[2,64,256]{2,1,0:T(8,128)(2,1)S(1)} %get-tuple-element.53), channel_id=1, source_target_pairs={{0,8},{4,12},{8,0},{12,4},{1,9},{5,13},{9,1},{13,5},{2,10},{6,14},... | collective-permute-start | bytes 196616 | tf_op jit(solution)/shard_map/ppermute | solution.py:635
  35.9 6.1 %collective-permute-start.12 = (bf16[2,64,256]{2,1,0:T(8,128)(2,1)S(1)}, bf16[2,64,256]{2,1,0:T(8,128)(2,1)S(1)}, u32[]{:S(2)}, u32[]{:S(2)}) collective-permute-start(bf16[2,64,256]{2,1,0:T(8,128)(2,1)S(1)} %get-tuple-element.54), channel_id=1, source_target_pairs={{0,12},{4,8},{8,4},{12,0},{1,13},{5,9},{9,5},{13,1},{2,14},{6,10},... | collective-permute-start | bytes 196616 | tf_op jit(solution)/shard_map/ppermute | solution.py:635
  43.3 8.4 %collective-permute-start.14 = (bf16[2,64,512]{2,1,0:T(8,128)(2,1)S(1)}, bf16[2,64,512]{2,1,0:T(8,128)(2,1)S(1)}, u32[]{:S(2)}, u32[]{:S(2)}) collective-permute-start(bf16[2,64,512]{2,1,0:T(8,128)(2,1)S(1)} %primary_spectra.1.rest_0_), channel_id=1, source_target_pairs={{0,8},{4,12},{8,0},{12,4},{1,9},{5,13},{9,1},{13,5},{2,10},{6,14},... | collective-permute-start | bytes 393224 | tf_op jit(solution)/shard_map/ppermute | solution.py:635
  45.6 10.4 %collective-permute-start.13 = (bf16[2,64,512]{2,1,0:T(8,128)(2,1)S(1)}, bf16[2,64,512]{2,1,0:T(8,128)(2,1)S(1)}, u32[]{:S(2)}, u32[]{:S(2)}) collective-permute-start(bf16[2,64,512]{2,1,0:T(8,128)(2,1)S(1)} %primary_spectra.1.rest_0_), channel_id=1, source_target_pairs={{0,4},{4,0},{8,12},{12,8},{1,5},{5,1},{9,13},{13,9},{2,6},{6,2},{1... | collective-permute-start | bytes 393224 | tf_op jit(solution)/shard_map/ppermute | solution.py:635
  46.4 5.6 %copy-start.2 = (s32[1,2,4,8]{3,2,1,0:T(4,128)S(1)}, s32[1,2,4,8]{3,2,1,0:T(4,128)}, u32[]{:S(2)}) copy-start(s32[1,2,4,8]{3,2,1,0:T(4,128)} %param.20) | copy-start | bytes 772
  51.6 5.0 %collective-permute-start.15 = (bf16[2,64,512]{2,1,0:T(8,128)(2,1)S(1)}, bf16[2,64,512]{2,1,0:T(8,128)(2,1)S(1)}, u32[]{:S(2)}, u32[]{:S(2)}) collective-permute-start(bf16[2,64,512]{2,1,0:T(8,128)(2,1)S(1)} %collective-permute-done.14.rest_2_), channel_id=1, source_target_pairs={{0,4},{4,0},{8,12},{12,8},{1,5},{5,1},{9,13},{13,9},{2,6},{6,2},{1... | collective-permute-start | bytes 393224 | tf_op jit(solution)/shard_map/ppermute | solution.py:635
  52.0 4.6 %copy-start.5 = (bf16[2,256,256]{2,1,0:T(8,128)(2,1)S(1)}, bf16[2,256,256]{2,1,0:T(8,128)(2,1)}, u32[]{:S(2)}) copy-start(bf16[2,256,256]{2,1,0:T(8,128)(2,1)} %constant.17.clone.rest_5_) | copy-start | bytes 786436

commit v3 on v2

--- a/solution.py
+++ b/solution.py
@@ -469,7 +469,7 @@
 def window_kernel(offsets, *rest, chunks):
     inner_refs, rest = rest[: len(chunks)], rest[len(chunks) :]
     outer_ref, lane_ref, column_ref = rest[:3]
-    spec_ref, image, windows = rest[3:]
+    spec_ref, image = rest[3:]
     lines, pairs = outer_ref.shape[1], outer_ref.shape[2] // LANES - 1
     lane = lax.broadcasted_iota(jnp.int32, (1, LANES), 1)
     edge = jnp.zeros((HALF, image.shape[2]), F32)
@@ -496,7 +496,7 @@
     wide = lax.broadcasted_iota(jnp.int32, (PATCH + 8, LANES), 1)
 
     def block(i, carry):
-        gains = []
+        gains, windows = [], []
         for u in range(pairs):
             found = [[], []]
             for side in range(2):
@@ -514,15 +514,16 @@
             re = jnp.where(lane < PATCH, found[0][0], found[0][1])
             im = jnp.where(lane < PATCH, found[1][0], found[1][1])
             gains.append(lax.rsqrt(power(re, im) + EPS) * (1.0 / PATCH**3))
-            windows[u * PATCH : (u + 1) * PATCH, :] = jnp.concatenate([re, im], axis=1).astype(BF16)
-        mixed = dot(windows[...], lane_ref[0]) + dot(windows[...], lane_ref[1])
+            windows.append(jnp.concatenate([re, im], axis=1))
+        stack = jnp.concatenate(windows, axis=0).astype(BF16)
+        mixed = dot(stack, lane_ref[0]) + dot(stack, lane_ref[1])
         for u in range(pairs):
             re, im = columns(mixed[u * PATCH : (u + 1) * PATCH], column_ref, -1)
             spec_ref[0, i * pairs + u] = re * gains[u]
             spec_ref[1, i * pairs + u] = im * gains[u]
         return carry
 
-    lax.fori_loop(0, row_blocks, block, 0)
+    lax.fori_loop(0, row_blocks, block, 0, unroll=True)
 
 
 def window_spectra(inner, outer, patch, offsets, chunks):
@@ -535,7 +536,6 @@
         out_shape=jax.ShapeDtypeStruct((2, lines // (2 * PATCH) * pairs, PATCH, LANES), F32),
         scratch_shapes=[
             pltpu.VMEM((2, lines + 2 * HALF + 8, (2 * pairs + 1) * LANES), F32),
-            pltpu.VMEM((pairs * PATCH, 2 * LANES), BF16),
         ],
         compiler_params=pltpu.CompilerParams(vmem_limit_bytes=VMEM_BYTES),
         cost_estimate=cost(4.0),

time: 58.8 us -> 58.8 us (level)
  Pallas kernels: 24 us -> 22.9 us
  waiting for transfers between devices: 11.8 us -> 12.9 us
    pallas_call x1, Pallas kernels: 4.02 us -> 2.91 us  [window_spectra(): pl.pallas_call(functools.partial(window_kernel, chunks=chunks), in_specs=...]
    ppermute x18, waiting for transfers between devices: 11.8 us -> 12.9 us  [trade(): lax.ppermute(block, axis, [(i, i ^ k) for i in range(lax.axis_size(axis))])]
  transfers between devices with their start and end apart: 18 -> 18, of which waited for: 8 -> 8; matrix products, arithmetic and copies ran while one was open for 0% -> 0% of each run, Pallas kernels for 22% -> 20%
where the time goes in v3:
time: 58.8 us; the launch traced here: 58.6 us
  Pallas kernels  22.9 us (39%)
  starting transfers between devices  20.4 us (35%)
  waiting for transfers between devices  12.9 us (22%)
  between operations  1.47 us (2%)
  local copies, waits for them, and re-layouts  0.95 us (2%)
    ppermute x18, starting transfers between devices, trade(): lax.ppermute(block, axis, [(i, i ^ k) for i in range(lax.axis_size(axis))])  20.4 us
    ppermute x18, waiting for transfers between devices, trade(): lax.ppermute(block, axis, [(i, i ^ k) for i in range(lax.axis_size(axis))])  12.9 us
    pallas_call x1, Pallas kernels, compress(): pl.pallas_call(functools.partial(range_kernel, devices=devices, first=(pa...  9.3 us
    pallas_call x1, Pallas kernels, focus_outer(): pl.pallas_call(functools.partial(outer_kernel, devices=devices), in_specs...  4.25 us
    pallas_call x2, Pallas kernels, focus_inner(): pl.pallas_call(functools.partial(inner_kernel, devices=devices, row_parts...  3.16 us
    pallas_call x1, Pallas kernels, window_spectra(): pl.pallas_call(functools.partial(window_kernel, chunks=chunks), in_specs=...  2.91 us
    pallas_call x1, Pallas kernels, correlate(): pl.pallas_call(functools.partial(correlate_kernel, parts=parts), in_specs...  2.03 us
    pallas_call x1, Pallas kernels, primary_spectra(): pl.pallas_call(functools.partial(primary_kernel, parts=len(shares[0])), i...  1.22 us
  transfers between devices with their start and end apart: 18, of which 8 were waited for; matrix products, arithmetic and copies ran while one was open for 0% of the time, Pallas kernels for 20%

profile of v3, /device:TPU:0, one launch (start us, length us, event | category | flops | bytes accessed | tf_op | source)
XLA Modules:
  0.0 58.6 jit_solution(14159223970988395439)
XLA Ops:
  0.7 0.0 copy-start.3
  0.7 0.0 copy-start.4
  0.7 9.3 %range_compress.1 = (bf16[2,128,256]{2,1,0:T(8,128)(2,1)}, bf16[2,128,256]{2,1,0:T(8,128)(2,1)}, bf16[2,128,256]{2,1,0:T(8,128)(2,1)}, bf16[2,128,256]{2,1,0:T(8...) custom-call(s32[1]{0:T(128)S(6)} %copy.15.valid, ...), custom_call_target="tpu_custom_call" | custom-call | flops 8999999488 | bytes 31500000 | tf_op jit(solution)/shard_map/range_compress/pallas_call | solution.py:232
  10.0 0.5 collective-permute-start.9
  10.5 0.1 collective-permute-start
  10.6 2.9 %collective-permute-start.1 = (bf16[2,128,256]{2,1,0:T(8,128)(2,1)}, bf16[2,128,256]{2,1,0:T(8,128)(2,1)S(1)}, u32[]{:S(2)}, u32[]{:S(2)}) collective-permute-start(bf16[2,128,256]{2,1,0:T(8,128)(2,1)} %get-tuple-element.36), channel_id=1, source_target_pairs={{0,2},{1,3},{2,0},{3,1},{4,6},{5,7},{6,4},{7,5},{8,10},{9,11},{10,... | collective-permute-start | bytes 393224 | tf_op jit(solution)/shard_map/ppermute | solution.py:635
  13.5 0.0 collective-permute-start.2
  13.5 0.1 collective-permute-start.6
  13.7 0.0 collective-permute-done.rest_1_
  13.7 2.0 %collective-permute-start.7 = (bf16[2,128,256]{2,1,0:T(8,128)(2,1)}, bf16[2,128,256]{2,1,0:T(8,128)(2,1)S(1)}, u32[]{:S(2)}, u32[]{:S(2)}) collective-permute-start(bf16[2,128,256]{2,1,0:T(8,128)(2,1)} %get-tuple-element.44), channel_id=1, source_target_pairs={{0,2},{1,3},{2,0},{3,1},{4,6},{5,7},{6,4},{7,5},{8,10},{9,11},{10,... | collective-permute-start | bytes 393224 | tf_op jit(solution)/shard_map/ppermute | solution.py:635
  15.7 2.4 %collective-permute-done.1.rest_2_ = bf16[2,128,256]{2,1,0:T(8,128)(2,1)S(1)} collective-permute-done((bf16[2,128,256]{2,1,0:T(8,128)(2,1)}, bf16[2,128,256]{2,1,0:T(8,128)(2,1)S(1)}, u32[]{:S(2)}, u32[]{:S(2)}) %collective-permute-start.1) | collective-permute-done | bytes 131104 | tf_op jit(solution)/shard_map/ppermute | solution.py:635
  18.0 0.0 collective-permute-start.8
  18.1 2.5 %collective-permute-done.2.rest_3_ = bf16[2,128,256]{2,1,0:T(8,128)(2,1)S(1)} collective-permute-done((bf16[2,128,256]{2,1,0:T(8,128)(2,1)}, bf16[2,128,256]{2,1,0:T(8,128)(2,1)S(1)}, u32[]{:S(2)}, u32[]{:S(2)}) %collective-permute-start.2) | collective-permute-done | bytes 131104 | tf_op jit(solution)/shard_map/ppermute | solution.py:635
  20.5 0.9 %copy-done.9 = bf16[2,128,256]{2,1,0:T(8,128)(2,1)S(1)} copy-done((bf16[2,128,256]{2,1,0:T(8,128)(2,1)S(1)}, bf16[2,128,256]{2,1,0:T(8,128)(2,1)}, u32[]{:S(2)}) %copy-start.9) | copy-done | bytes 131096
  21.4 1.6 %focus_inner.2 = (bf16[2,512,256]{2,1,0:T(8,128)(2,1)S(1)}, bf16[2,64,256]{2,1,0:T(8,128)(2,1)S(1)}, bf16[2,64,256]{2,1,0:T(8,128)(2,1)S(1)}, bf16[2,64,256]{2,1,0:T(8,128)(2,1)S(1)}, bf16[2,64,256]{2,1,0:T(8,128)(2,1)S(1)}) custom-call(bf16[2,128,256]{2,1,0:T(8,128)(2,1)S(1)} %copy-done.9, bf16[2,128,256]{2,1,0:T(8,128)(2,1)S(1)} %collective-permute-done.rest_1_, ...), custom_call_target="tpu_custom_call" | custom-call | flops 1600000000 | bytes 5600000 | tf_op jit(solution)/shard_map/focus_inner/pallas_call | solution.py:362
  23.0 0.7 %collective-permute-start.16 = (bf16[2,128,640]{2,1,0:T(8,128)(2,1)S(1)}, bf16[2,128,640]{2,1,0:T(8,128)(2,1)S(1)}, u32[]{:S(2)}, u32[]{:S(2)}) collective-permute-start(bf16[2,128,640]{2,1,0:T(8,128)(2,1)S(1)} %copy-done.12), channel_id=1, source_target_pairs={{0,2},{1,3},{2,0},{3,1},{4,6},{5,7},{6,4},{7,5},{8,10},{9,11},{10,... | collective-permute-start | bytes 983048 | tf_op jit(solution)/shard_map/ppermute | solution.py:635
  23.7 0.0 collective-permute-done.6.rest_1_
  23.7 1.3 %collective-permute-start.17 = (bf16[2,128,640]{2,1,0:T(8,128)(2,1)S(1)}, bf16[2,128,640]{2,1,0:T(8,128)(2,1)S(1)}, u32[]{:S(2)}, u32[]{:S(2)}) collective-permute-start(bf16[2,128,640]{2,1,0:T(8,128)(2,1)S(1)} %copy-done.11), channel_id=1, source_target_pairs={{0,3},{1,2},{2,1},{3,0},{4,7},{5,6},{6,5},{7,4},{8,11},{9,10},{10,... | collective-permute-start | bytes 983048 | tf_op jit(solution)/shard_map/ppermute | solution.py:635
  25.0 0.0 collective-permute-done.7.rest_2_
  25.0 1.8 %collective-permute-start.3 = (bf16[2,64,256]{2,1,0:T(8,128)(2,1)S(1)}, bf16[2,64,256]{2,1,0:T(8,128)(2,1)S(1)}, u32[]{:S(2)}, u32[]{:S(2)}) collective-permute-start(bf16[2,64,256]{2,1,0:T(8,128)(2,1)S(1)} %get-tuple-element.39), channel_id=1, source_target_pairs={{0,4},{4,0},{8,12},{12,8},{1,5},{5,1},{9,13},{13,9},{2,6},{6,2},{1... | collective-permute-start | bytes 196616 | tf_op jit(solution)/shard_map/ppermute | solution.py:635
  26.8 0.0 collective-permute-done.8.rest_3_
  26.8 2.6 %collective-permute-start.4 = (bf16[2,64,256]{2,1,0:T(8,128)(2,1)S(1)}, bf16[2,64,256]{2,1,0:T(8,128)(2,1)S(1)}, u32[]{:S(2)}, u32[]{:S(2)}) collective-permute-start(bf16[2,64,256]{2,1,0:T(8,128)(2,1)S(1)} %get-tuple-element.40), channel_id=1, source_target_pairs={{0,8},{4,12},{8,0},{12,4},{1,9},{5,13},{9,1},{13,5},{2,10},{6,14},... | collective-permute-start | bytes 196616 | tf_op jit(solution)/shard_map/ppermute | solution.py:635
  29.4 0.0 collective-permute-done.9.rest_1_
  29.4 0.1 collective-permute-start.5
  29.4 1.6 %focus_inner.3 = (bf16[2,512,256]{2,1,0:T(8,128)(2,1)S(1)}, bf16[2,64,256]{2,1,0:T(8,128)(2,1)S(1)}, bf16[2,64,256]{2,1,0:T(8,128)(2,1)S(1)}, bf16[2,64,256]{2,1,0:T(8,128)(2,1)S(1)}, bf16[2,64,256]{2,1,0:T(8,128)(2,1)S(1)}) custom-call(bf16[2,128,256]{2,1,0:T(8,128)(2,1)S(1)} %copy-done.8, bf16[2,128,256]{2,1,0:T(8,128)(2,1)S(1)} %collective-permute-done.6.rest_1_, ...), custom_call_target="tpu_custom_call" | custom-call | flops 1600000000 | bytes 5600000 | tf_op jit(solution)/shard_map/focus_inner/pallas_call | solution.py:362
  31.0 0.0 copy-start.10
  31.0 0.0 collective-permute-done.3.rest_1_
  31.0 0.9 %collective-permute-start.10 = (bf16[2,64,256]{2,1,0:T(8,128)(2,1)S(1)}, bf16[2,64,256]{2,1,0:T(8,128)(2,1)S(1)}, u32[]{:S(2)}, u32[]{:S(2)}) collective-permute-start(bf16[2,64,256]{2,1,0:T(8,128)(2,1)S(1)} %get-tuple-element.52), channel_id=1, source_target_pairs={{0,4},{4,0},{8,12},{12,8},{1,5},{5,1},{9,13},{13,9},{2,6},{6,2},{1... | collective-permute-start | bytes 196616 | tf_op jit(solution)/shard_map/ppermute | solution.py:635
  32.0 1.4 %collective-permute-done.4.rest_2_ = bf16[2,64,256]{2,1,0:T(8,128)(2,1)S(1)} collective-permute-done((bf16[2,64,256]{2,1,0:T(8,128)(2,1)S(1)}, bf16[2,64,256]{2,1,0:T(8,128)(2,1)S(1)}, u32[]{:S(2)}, u32[]{:S(2)}) %collective-permute-start.4) | collective-permute-done | bytes 65568 | tf_op jit(solution)/shard_map/ppermute | solution.py:635
  33.3 2.1 %collective-permute-start.11 = (bf16[2,64,256]{2,1,0:T(8,128)(2,1)S(1)}, bf16[2,64,256]{2,1,0:T(8,128)(2,1)S(1)}, u32[]{:S(2)}, u32[]{:S(2)}) collective-permute-start(bf16[2,64,256]{2,1,0:T(8,128)(2,1)S(1)} %get-tuple-element.53), channel_id=1, source_target_pairs={{0,8},{4,12},{8,0},{12,4},{1,9},{5,13},{9,1},{13,5},{2,10},{6,14},... | collective-permute-start | bytes 196616 | tf_op jit(solution)/shard_map/ppermute | solution.py:635
  35.4 0.5 collective-permute-done.5.rest_3_
  35.9 1.9 %collective-permute-start.12 = (bf16[2,64,256]{2,1,0:T(8,128)(2,1)S(1)}, bf16[2,64,256]{2,1,0:T(8,128)(2,1)S(1)}, u32[]{:S(2)}, u32[]{:S(2)}) collective-permute-start(bf16[2,64,256]{2,1,0:T(8,128)(2,1)S(1)} %get-tuple-element.54), channel_id=1, source_target_pairs={{0,12},{4,8},{8,4},{12,0},{1,13},{5,9},{9,5},{13,1},{2,14},{6,10},... | collective-permute-start | bytes 196616 | tf_op jit(solution)/shard_map/ppermute | solution.py:635
  38.5 0.0 collective-permute-done.10.rest_5_
  38.5 2.5 %collective-permute-done.11.rest_6_ = bf16[2,64,256]{2,1,0:T(8,128)(2,1)S(1)} collective-permute-done((bf16[2,64,256]{2,1,0:T(8,128)(2,1)S(1)}, bf16[2,64,256]{2,1,0:T(8,128)(2,1)S(1)}, u32[]{:S(2)}, u32[]{:S(2)}) %collective-permute-start.11) | collective-permute-done | bytes 65568 | tf_op jit(solution)/shard_map/ppermute | solution.py:635
  41.0 1.0 %collective-permute-done.12.rest_7_ = bf16[2,64,256]{2,1,0:T(8,128)(2,1)S(1)} collective-permute-done((bf16[2,64,256]{2,1,0:T(8,128)(2,1)S(1)}, bf16[2,64,256]{2,1,0:T(8,128)(2,1)S(1)}, u32[]{:S(2)}, u32[]{:S(2)}) %collective-permute-start.12) | collective-permute-done | bytes 65568 | tf_op jit(solution)/shard_map/ppermute | solution.py:635
  42.0 1.2 %primary_spectra.1.rest_0_ = bf16[2,64,512]{2,1,0:T(8,128)(2,1)S(1)} custom-call(s32[1]{0:T(128)S(6)} %copy.16.reference, bf16[2,64,256]{2,1,0:T(8,128)(2,1)S(1)} %get-tuple-element.38.rest_0_, bf16[2,64,256]{2,1,0:T(8,128)(2,1)S(1)} %collective-permute-done.3.rest_1_, bf16[2,64,256]{2,1,0:T(8,128)(2,1)S(1)} %collective-permute-done.4.rest_2_, ...), custom_call_target="tpu_custom_call" | custom-call | flops 1000000000 | bytes 3500000 | tf_op jit(solution)/shard_map/primary_spectra/pallas_call | solution.py:576
  43.3 2.3 %collective-permute-start.14 = (bf16[2,64,512]{2,1,0:T(8,128)(2,1)S(1)}, bf16[2,64,512]{2,1,0:T(8,128)(2,1)S(1)}, u32[]{:S(2)}, u32[]{:S(2)}) collective-permute-start(bf16[2,64,512]{2,1,0:T(8,128)(2,1)S(1)} %primary_spectra.1.rest_0_), channel_id=1, source_target_pairs={{0,8},{4,12},{8,0},{12,4},{1,9},{5,13},{9,1},{13,5},{2,10},{6,14},... | collective-permute-start | bytes 393224 | tf_op jit(solution)/shard_map/ppermute | solution.py:635
  45.6 0.8 %collective-permute-start.13 = (bf16[2,64,512]{2,1,0:T(8,128)(2,1)S(1)}, bf16[2,64,512]{2,1,0:T(8,128)(2,1)S(1)}, u32[]{:S(2)}, u32[]{:S(2)}) collective-permute-start(bf16[2,64,512]{2,1,0:T(8,128)(2,1)S(1)} %primary_spectra.1.rest_0_), channel_id=1, source_target_pairs={{0,4},{4,0},{8,12},{12,8},{1,5},{5,1},{9,13},{13,9},{2,6},{6,2},{1... | collective-permute-start | bytes 393224 | tf_op jit(solution)/shard_map/ppermute | solution.py:635
  46.4 0.0 collective-permute-done.16.rest_2_
  46.4 0.0 collective-permute-done.17.rest_3_
  46.4 0.0 copy-start.2
  46.4 4.2 %focus_outer.1.rest_2_ = bf16[2,512,640]{2,1,0:T(8,128)(2,1)S(1)} custom-call(bf16[2,128,640]{2,1,0:T(8,128)(2,1)S(1)} %copy-done.10, bf16[2,128,640]{2,1,0:T(8,128)(2,1)S(1)} %collective-permute-done.9.rest_1_, bf16[2,128,640]{2,1,0:T(8,128)(2,1)S(1)} %collective-permute-done.16.rest_2_, bf16[2,128,640]{2,1,0:T(8,128)(2,1)S(1)} %collective-permute-done.17.rest_3_, ...), custom_call_target="tpu_custom_call" | custom-call | flops 4000000000 | bytes 14000000 | tf_op jit(solution)/shard_map/focus_outer/pallas_call | solution.py:425
  50.6 1.0 %collective-permute-done.14.rest_2_ = bf16[2,64,512]{2,1,0:T(8,128)(2,1)S(1)} collective-permute-done((bf16[2,64,512]{2,1,0:T(8,128)(2,1)S(1)}, bf16[2,64,512]{2,1,0:T(8,128)(2,1)S(1)}, u32[]{:S(2)}, u32[]{:S(2)}) %collective-permute-start.14) | collective-permute-done | bytes 131104 | tf_op jit(solution)/shard_map/ppermute | solution.py:635
  51.6 0.3 collective-permute-start.15
  52.0 2.9 %window_spectra.1.rest_4_ = f32[2,16,64,128]{3,2,1,0:T(8,128)S(1)} custom-call(s32[2,4,8]{2,1,0:T(4,128)S(1)} %bitcast.3, bf16[2,512,256]{2,1,0:T(8,128)(2,1)S(1)} %get-tuple-element.55.rest_0_, bf16[2,512,256]{2,1,0:T(8,128)(2,1)S(1)} %get-tuple-element.56.rest_1_, bf16[2,512,640]{2,1,0:T(8,128)(2,1)S(1)} %focus_outer.1.rest_2_, ...), custom_call_target="tpu_custom_call" | custom-call | flops 4000000000 | bytes 14000000 | tf_op jit(solution)/shard_map/window_spectra/pallas_call | solution.py:532
  54.9 0.0 collective-permute-done.13.rest_1_
  54.9 1.7 %collective-permute-done.15.rest_3_ = bf16[2,64,512]{2,1,0:T(8,128)(2,1)S(1)} collective-permute-done((bf16[2,64,512]{2,1,0:T(8,128)(2,1)S(1)}, bf16[2,64,512]{2,1,0:T(8,128)(2,1)S(1)}, u32[]{:S(2)}, u32[]{:S(2)}) %collective-permute-start.15) | collective-permute-done | bytes 131104 | tf_op jit(solution)/shard_map/ppermute | solution.py:635
  56.6 2.0 %correlate.1 = f32[1,2,256,512]{3,2,1,0:T(8,128)} custom-call(bf16[2,64,512]{2,1,0:T(8,128)(2,1)S(1)} %primary_spectra.1.rest_0_, bf16[2,64,512]{2,1,0:T(8,128)(2,1)S(1)} %collective-permute-done.13.rest_1_, bf16[2,64,512]{2,1,0:T(8,128)(2,1)S(1)} %collective-permute-done.14.rest_2_, bf16[2,64,512]{2,1,0:T(8,128)(2,1)S(1)} %collective-permute-done.15.rest_3_, ...), custom_call_target="tpu_custom_call" | custom-call | flops 2000000000 | bytes 7000000 | tf_op jit(solution)/shard_map/correlate/pallas_call | solution.py:617
  (21 shorter events, 0.0 us)
Async XLA Ops:
  0.7 19.9 %copy-start = (f32[1,1024]{1,0:T(1,128)S(1)}, f32[1,1024]{1,0:T(1,128)}, u32[]{:S(2)}) copy-start(f32[1,1024]{1,0:T(1,128)} %rest_4_.6) | copy-start | bytes 12292
  0.7 19.9 %copy-start.1 = (f32[1,1024]{1,0:T(1,128)S(1)}, f32[1,1024]{1,0:T(1,128)}, u32[]{:S(2)}) copy-start(f32[1,1024]{1,0:T(1,128)} %rest_5_.6) | copy-start | bytes 12292
  0.7 19.9 %copy-start.3 = (bf16[2,4,256,256]{3,2,1,0:T(8,128)(2,1)S(1)}, bf16[2,4,256,256]{3,2,1,0:T(8,128)(2,1)}, u32[]{:S(2)}) copy-start(bf16[2,4,256,256]{3,2,1,0:T(8,128)(2,1)} %constant.14.clone.rest_6_) | copy-start | bytes 3145732
  0.7 19.8 %copy-start.4 = (bf16[2,4,256,256]{3,2,1,0:T(8,128)(2,1)S(1)}, bf16[2,4,256,256]{3,2,1,0:T(8,128)(2,1)}, u32[]{:S(2)}) copy-start(bf16[2,4,256,256]{3,2,1,0:T(8,128)(2,1)} %constant.15.clone.rest_7_) | copy-start | bytes 3145732
  10.0 19.4 %collective-permute-start.9 = (bf16[2,128,640]{2,1,0:T(8,128)(2,1)}, bf16[2,128,640]{2,1,0:T(8,128)(2,1)S(1)}, u32[]{:S(2)}, u32[]{:S(2)}) collective-permute-start(bf16[2,128,640]{2,1,0:T(8,128)(2,1)} %get-tuple-element.46), channel_id=1, source_target_pairs={{0,1},{1,0},{2,3},{3,2},{4,5},{5,4},{6,7},{7,6},{8,9},{9,8},{10,11... | collective-permute-start | bytes 983048 | tf_op jit(solution)/shard_map/ppermute | solution.py:635
  10.5 3.1 %collective-permute-start = (bf16[2,128,256]{2,1,0:T(8,128)(2,1)}, bf16[2,128,256]{2,1,0:T(8,128)(2,1)S(1)}, u32[]{:S(2)}, u32[]{:S(2)}) collective-permute-start(bf16[2,128,256]{2,1,0:T(8,128)(2,1)} %get-tuple-element.35), channel_id=1, source_target_pairs={{0,1},{1,0},{2,3},{3,2},{4,5},{5,4},{6,7},{7,6},{8,9},{9,8},{10,11... | collective-permute-start | bytes 393224 | tf_op jit(solution)/shard_map/ppermute | solution.py:635
  10.6 7.4 %collective-permute-start.1 = (bf16[2,128,256]{2,1,0:T(8,128)(2,1)}, bf16[2,128,256]{2,1,0:T(8,128)(2,1)S(1)}, u32[]{:S(2)}, u32[]{:S(2)}) collective-permute-start(bf16[2,128,256]{2,1,0:T(8,128)(2,1)} %get-tuple-element.36), channel_id=1, source_target_pairs={{0,2},{1,3},{2,0},{3,1},{4,6},{5,7},{6,4},{7,5},{8,10},{9,11},{10,... | collective-permute-start | bytes 393224 | tf_op jit(solution)/shard_map/ppermute | solution.py:635
  13.5 7.0 %collective-permute-start.2 = (bf16[2,128,256]{2,1,0:T(8,128)(2,1)}, bf16[2,128,256]{2,1,0:T(8,128)(2,1)S(1)}, u32[]{:S(2)}, u32[]{:S(2)}) collective-permute-start(bf16[2,128,256]{2,1,0:T(8,128)(2,1)} %get-tuple-element.37), channel_id=1, source_target_pairs={{0,3},{1,2},{2,1},{3,0},{4,7},{5,6},{6,5},{7,4},{8,11},{9,10},{10,... | collective-permute-start | bytes 393224 | tf_op jit(solution)/shard_map/ppermute | solution.py:635
  13.5 10.2 %collective-permute-start.6 = (bf16[2,128,256]{2,1,0:T(8,128)(2,1)}, bf16[2,128,256]{2,1,0:T(8,128)(2,1)S(1)}, u32[]{:S(2)}, u32[]{:S(2)}) collective-permute-start(bf16[2,128,256]{2,1,0:T(8,128)(2,1)} %get-tuple-element.43), channel_id=1, source_target_pairs={{0,1},{1,0},{2,3},{3,2},{4,5},{5,4},{6,7},{7,6},{8,9},{9,8},{10,11... | collective-permute-start | bytes 393224 | tf_op jit(solution)/shard_map/ppermute | solution.py:635
  13.7 11.3 %collective-permute-start.7 = (bf16[2,128,256]{2,1,0:T(8,128)(2,1)}, bf16[2,128,256]{2,1,0:T(8,128)(2,1)S(1)}, u32[]{:S(2)}, u32[]{:S(2)}) collective-permute-start(bf16[2,128,256]{2,1,0:T(8,128)(2,1)} %get-tuple-element.44), channel_id=1, source_target_pairs={{0,2},{1,3},{2,0},{3,1},{4,6},{5,7},{6,4},{7,5},{8,10},{9,11},{10,... | collective-permute-start | bytes 393224 | tf_op jit(solution)/shard_map/ppermute | solution.py:635
  18.0 8.8 %collective-permute-start.8 = (bf16[2,128,256]{2,1,0:T(8,128)(2,1)}, bf16[2,128,256]{2,1,0:T(8,128)(2,1)S(1)}, u32[]{:S(2)}, u32[]{:S(2)}) collective-permute-start(bf16[2,128,256]{2,1,0:T(8,128)(2,1)} %get-tuple-element.45), channel_id=1, source_target_pairs={{0,3},{1,2},{2,1},{3,0},{4,7},{5,6},{6,5},{7,4},{8,11},{9,10},{10,... | collective-permute-start | bytes 393224 | tf_op jit(solution)/shard_map/ppermute | solution.py:635
  20.5 0.9 %copy-start.9 = (bf16[2,128,256]{2,1,0:T(8,128)(2,1)S(1)}, bf16[2,128,256]{2,1,0:T(8,128)(2,1)}, u32[]{:S(2)}) copy-start(bf16[2,128,256]{2,1,0:T(8,128)(2,1)} %get-tuple-element.34.rest_0_) | copy-start | bytes 393220
  21.4 1.6 %copy-start.12 = (bf16[2,128,640]{2,1,0:T(8,128)(2,1)S(1)}, bf16[2,128,640]{2,1,0:T(8,128)(2,1)}, u32[]{:S(2)}) copy-start(bf16[2,128,640]{2,1,0:T(8,128)(2,1)} %get-tuple-element.61) | copy-start | bytes 983044
  21.4 2.3 %copy-start.11 = (bf16[2,128,640]{2,1,0:T(8,128)(2,1)S(1)}, bf16[2,128,640]{2,1,0:T(8,128)(2,1)}, u32[]{:S(2)}) copy-start(bf16[2,128,640]{2,1,0:T(8,128)(2,1)} %get-tuple-element.62) | copy-start | bytes 983044
  21.4 8.0 %copy-start.8 = (bf16[2,128,256]{2,1,0:T(8,128)(2,1)S(1)}, bf16[2,128,256]{2,1,0:T(8,128)(2,1)}, u32[]{:S(2)}) copy-start(bf16[2,128,256]{2,1,0:T(8,128)(2,1)} %get-tuple-element.47.rest_0_) | copy-start | bytes 393220
  23.0 23.3 %collective-permute-start.16 = (bf16[2,128,640]{2,1,0:T(8,128)(2,1)S(1)}, bf16[2,128,640]{2,1,0:T(8,128)(2,1)S(1)}, u32[]{:S(2)}, u32[]{:S(2)}) collective-permute-start(bf16[2,128,640]{2,1,0:T(8,128)(2,1)S(1)} %copy-done.12), channel_id=1, source_target_pairs={{0,2},{1,3},{2,0},{3,1},{4,6},{5,7},{6,4},{7,5},{8,10},{9,11},{10,... | collective-permute-start | bytes 983048 | tf_op jit(solution)/shard_map/ppermute | solution.py:635
  23.7 22.6 %collective-permute-start.17 = (bf16[2,128,640]{2,1,0:T(8,128)(2,1)S(1)}, bf16[2,128,640]{2,1,0:T(8,128)(2,1)S(1)}, u32[]{:S(2)}, u32[]{:S(2)}) collective-permute-start(bf16[2,128,640]{2,1,0:T(8,128)(2,1)S(1)} %copy-done.11), channel_id=1, source_target_pairs={{0,3},{1,2},{2,1},{3,0},{4,7},{5,6},{6,5},{7,4},{8,11},{9,10},{10,... | collective-permute-start | bytes 983048 | tf_op jit(solution)/shard_map/ppermute | solution.py:635
  25.0 6.0 %collective-permute-start.3 = (bf16[2,64,256]{2,1,0:T(8,128)(2,1)S(1)}, bf16[2,64,256]{2,1,0:T(8,128)(2,1)S(1)}, u32[]{:S(2)}, u32[]{:S(2)}) collective-permute-start(bf16[2,64,256]{2,1,0:T(8,128)(2,1)S(1)} %get-tuple-element.39), channel_id=1, source_target_pairs={{0,4},{4,0},{8,12},{12,8},{1,5},{5,1},{9,13},{13,9},{2,6},{6,2},{1... | collective-permute-start | bytes 196616 | tf_op jit(solution)/shard_map/ppermute | solution.py:635
  26.8 6.5 %collective-permute-start.4 = (bf16[2,64,256]{2,1,0:T(8,128)(2,1)S(1)}, bf16[2,64,256]{2,1,0:T(8,128)(2,1)S(1)}, u32[]{:S(2)}, u32[]{:S(2)}) collective-permute-start(bf16[2,64,256]{2,1,0:T(8,128)(2,1)S(1)} %get-tuple-element.40), channel_id=1, source_target_pairs={{0,8},{4,12},{8,0},{12,4},{1,9},{5,13},{9,1},{13,5},{2,10},{6,14},... | collective-permute-start | bytes 196616 | tf_op jit(solution)/shard_map/ppermute | solution.py:635
  29.4 6.5 %collective-permute-start.5 = (bf16[2,64,256]{2,1,0:T(8,128)(2,1)S(1)}, bf16[2,64,256]{2,1,0:T(8,128)(2,1)S(1)}, u32[]{:S(2)}, u32[]{:S(2)}) collective-permute-start(bf16[2,64,256]{2,1,0:T(8,128)(2,1)S(1)} %get-tuple-element.41), channel_id=1, source_target_pairs={{0,12},{4,8},{8,4},{12,0},{1,13},{5,9},{9,5},{13,1},{2,14},{6,10},... | collective-permute-start | bytes 196616 | tf_op jit(solution)/shard_map/ppermute | solution.py:635
  29.4 12.6 %copy-start.6 = (bf16[2,256,256]{2,1,0:T(8,128)(2,1)S(1)}, bf16[2,256,256]{2,1,0:T(8,128)(2,1)}, u32[]{:S(2)}) copy-start(bf16[2,256,256]{2,1,0:T(8,128)(2,1)} %constant.16.clone.rest_8_.rest_3_) | copy-start | bytes 786436
  29.4 12.6 %copy-start.7 = (bf16[128,192]{1,0:T(8,128)(2,1)S(1)}, bf16[128,192]{1,0:T(8,128)(2,1)}, u32[]{:S(2)}) copy-start(bf16[128,192]{1,0:T(8,128)(2,1)} %constant.18.clone.rest_9_.rest_4_.rest_6_) | copy-start | bytes 147460
  31.0 15.4 %copy-start.10 = (bf16[2,128,640]{2,1,0:T(8,128)(2,1)S(1)}, bf16[2,128,640]{2,1,0:T(8,128)(2,1)}, u32[]{:S(2)}) copy-start(bf16[2,128,640]{2,1,0:T(8,128)(2,1)} %get-tuple-element.57.rest_0_) | copy-start | bytes 983044
  31.0 7.4 %collective-permute-start.10 = (bf16[2,64,256]{2,1,0:T(8,128)(2,1)S(1)}, bf16[2,64,256]{2,1,0:T(8,128)(2,1)S(1)}, u32[]{:S(2)}, u32[]{:S(2)}) collective-permute-start(bf16[2,64,256]{2,1,0:T(8,128)(2,1)S(1)} %get-tuple-element.52), channel_id=1, source_target_pairs={{0,4},{4,0},{8,12},{12,8},{1,5},{5,1},{9,13},{13,9},{2,6},{6,2},{1... | collective-permute-start | bytes 196616 | tf_op jit(solution)/shard_map/ppermute | solution.py:635
  33.3 7.7 %collective-permute-start.11 = (bf16[2,64,256]{2,1,0:T(8,128)(2,1)S(1)}, bf16[2,64,256]{2,1,0:T(8,128)(2,1)S(1)}, u32[]{:S(2)}, u32[]{:S(2)}) collective-permute-start(bf16[2,64,256]{2,1,0:T(8,128)(2,1)S(1)} %get-tuple-element.53), channel_id=1, source_target_pairs={{0,8},{4,12},{8,0},{12,4},{1,9},{5,13},{9,1},{13,5},{2,10},{6,14},... | collective-permute-start | bytes 196616 | tf_op jit(solution)/shard_map/ppermute | solution.py:635
  35.9 6.1 %collective-permute-start.12 = (bf16[2,64,256]{2,1,0:T(8,128)(2,1)S(1)}, bf16[2,64,256]{2,1,0:T(8,128)(2,1)S(1)}, u32[]{:S(2)}, u32[]{:S(2)}) collective-permute-start(bf16[2,64,256]{2,1,0:T(8,128)(2,1)S(1)} %get-tuple-element.54), channel_id=1, source_target_pairs={{0,12},{4,8},{8,4},{12,0},{1,13},{5,9},{9,5},{13,1},{2,14},{6,10},... | collective-permute-start | bytes 196616 | tf_op jit(solution)/shard_map/ppermute | solution.py:635
  43.3 8.4 %collective-permute-start.14 = (bf16[2,64,512]{2,1,0:T(8,128)(2,1)S(1)}, bf16[2,64,512]{2,1,0:T(8,128)(2,1)S(1)}, u32[]{:S(2)}, u32[]{:S(2)}) collective-permute-start(bf16[2,64,512]{2,1,0:T(8,128)(2,1)S(1)} %primary_spectra.1.rest_0_), channel_id=1, source_target_pairs={{0,8},{4,12},{8,0},{12,4},{1,9},{5,13},{9,1},{13,5},{2,10},{6,14},... | collective-permute-start | bytes 393224 | tf_op jit(solution)/shard_map/ppermute | solution.py:635
  45.6 9.3 %collective-permute-start.13 = (bf16[2,64,512]{2,1,0:T(8,128)(2,1)S(1)}, bf16[2,64,512]{2,1,0:T(8,128)(2,1)S(1)}, u32[]{:S(2)}, u32[]{:S(2)}) collective-permute-start(bf16[2,64,512]{2,1,0:T(8,128)(2,1)S(1)} %primary_spectra.1.rest_0_), channel_id=1, source_target_pairs={{0,4},{4,0},{8,12},{12,8},{1,5},{5,1},{9,13},{13,9},{2,6},{6,2},{1... | collective-permute-start | bytes 393224 | tf_op jit(solution)/shard_map/ppermute | solution.py:635
  46.4 5.6 %copy-start.2 = (s32[1,2,4,8]{3,2,1,0:T(4,128)S(1)}, s32[1,2,4,8]{3,2,1,0:T(4,128)}, u32[]{:S(2)}) copy-start(s32[1,2,4,8]{3,2,1,0:T(4,128)} %param.20) | copy-start | bytes 772
  51.6 5.0 %collective-permute-start.15 = (bf16[2,64,512]{2,1,0:T(8,128)(2,1)S(1)}, bf16[2,64,512]{2,1,0:T(8,128)(2,1)S(1)}, u32[]{:S(2)}, u32[]{:S(2)}) collective-permute-start(bf16[2,64,512]{2,1,0:T(8,128)(2,1)S(1)} %collective-permute-done.14.rest_2_), channel_id=1, source_target_pairs={{0,4},{4,0},{8,12},{12,8},{1,5},{5,1},{9,13},{13,9},{2,6},{6,2},{1... | collective-permute-start | bytes 393224 | tf_op jit(solution)/shard_map/ppermute | solution.py:635
  52.0 4.6 %copy-start.5 = (bf16[2,256,256]{2,1,0:T(8,128)(2,1)S(1)}, bf16[2,256,256]{2,1,0:T(8,128)(2,1)}, u32[]{:S(2)}) copy-start(bf16[2,256,256]{2,1,0:T(8,128)(2,1)} %constant.17.clone.rest_5_) | copy-start | bytes 786436
